TPU v7x, 512 devices: a whole 4x4x16 slice. The times are simulated.
512 devices in a mesh: face: 4 (over x_hi, core), row: 16 (over z), col: 8 (over y, x_lo).
Axes of the slice: x: 4 (x_hi: 2, x_lo: 2; x = x_hi * 2 + x_lo), y: 4, z: 16, core: 2. Of those that a mesh axis runs over, the one named last changes fastest.
Arguments:
- fields: bfloat16 [12, 512, 8192], P('face', 'row', 'col'), may hold values from -6 to 6
- neighbours: int32 [12, 4, 3], replicated, may hold values from 0 to 11, as said below
- w_enc: bfloat16 [16, 128], replicated, may hold values from -1.5 to 1.5
- depthwise_kernel_first: float32 [3, 3, 128], replicated, may hold values from -2 to 2
- norm_gain_first: float32 [128], replicated, may hold values from 0.1 to 1.9
- expand_weight_first: bfloat16 [128, 512], replicated, may hold values from -0.5 to 0.5
- expand_bias_first: float32 [512], replicated, may hold values from -3 to 3
- contract_weight_first: bfloat16 [512, 128], replicated, may hold values from -0.25 to 0.25
- layer_scale_first: float32 [128], replicated, may hold values from 0.2 to 1
- w_down: bfloat16 [128, 256], replicated, may hold values from -0.5 to 0.5
- depthwise_kernel_second: float32 [3, 3, 256], replicated, may hold values from -2 to 2
- norm_gain_second: float32 [256], replicated, may hold values from 0.1 to 1.9
- expand_weight_second: bfloat16 [256, 1024], replicated, may hold values from -0.375 to 0.375
- expand_bias_second: float32 [1024], replicated, may hold values from -3 to 3
- contract_weight_second: bfloat16 [1024, 256], replicated, may hold values from -0.1875 to 0.1875
- layer_scale_second: float32 [256], replicated, may hold values from 0.2 to 1
Outputs:
- features: bfloat16 [12, 256, 65536], P('face', 'row', 'col')
Inputs may be any that keep to these rules, and one draw needn't show every extreme that they name: `neighbours`: faces 3 g, 3 g + 1 and 3 g + 2 form group g. For face f and edge e (0 its first cell row, 1 its last cell row, 2 its first cell column, 3 its last cell column), entry 0 is the face across that edge, which lies in the group of f or in one of the two groups next to it modulo 4; entry 1 is the edge of that face; entry 2 is 1 where position p along the edge meets position 511 - p of the other edge, else 0. Every edge's neighbour names it back.
All inputs are finite; a program needn't handle non-finite values.
Results may differ from a plain program's by a relative error of at most 0.008.
Values may be sent and summed in bfloat16 or wider, within the bound.
No kernel may reach another device: no remote copies, remote signals or barrier semaphores. Data moves between devices by JAX's collectives and lax.ppermute only.
A program may use at most 64 MiB of HBM per device.

v0:
```python
import jax
import jax.numpy as jnp
from jax import lax
from jax.sharding import PartitionSpec as P

CIN = 16
C1 = 128
C2 = 256
DILATION_LEVEL1 = 1
DILATION_LEVEL2 = 2


EPSILON = 1e-06


def with_halo(cells, sides, width, closed):
    for axis, dim in sides:
        count = lax.axis_size(axis)
        ends = count if closed else count - 1
        head = lax.slice_in_dim(cells, 0, width, axis=dim)
        tail = lax.slice_in_dim(cells, cells.shape[dim] - width, cells.shape[dim], axis=dim)
        cells = jnp.concatenate(
            [
                lax.ppermute(tail, axis, [(i, (i + 1) % count) for i in range(ends)]),
                cells,
                lax.ppermute(head, axis, [((i + 1) % count, i) for i in range(ends)]),
            ],
            axis=dim,
        )
    return cells


def convnext(padded, field, kernel, gain, w_in, b_in, w_out, scale, dilation):
    height, breadth, channels = field.shape
    mixed = jnp.zeros((height, breadth, channels), jnp.float32)
    for tap_row in range(3):
        for tap_col in range(3):
            window = padded[
                tap_row * dilation : tap_row * dilation + height,
                tap_col * dilation : tap_col * dilation + breadth,
            ]
            mixed = mixed + window.astype(jnp.float32) * kernel[tap_row, tap_col]
    center = jnp.mean(mixed, axis=-1, keepdims=True)
    spread = jnp.mean(jnp.square(mixed - center), axis=-1, keepdims=True)
    normed = ((mixed - center) * lax.rsqrt(spread + EPSILON) * gain).astype(jnp.bfloat16)
    hidden = jnp.dot(normed.reshape(-1, channels), w_in, preferred_element_type=jnp.float32) + b_in
    hidden = jax.nn.gelu(hidden, approximate=False).astype(jnp.bfloat16)
    update = jnp.dot(hidden, w_out, preferred_element_type=jnp.float32)
    result = field.reshape(-1, channels).astype(jnp.float32) + scale * update
    return result.astype(jnp.bfloat16).reshape(height, breadth, channels)


def across_groups(packed):
    return with_halo(packed[None], (("face", 0),), 1, True)


def select_slots(picker, moved):
    return jnp.einsum("jk,kdpc->jdpc", picker, moved, preferred_element_type=jnp.float32)


def convnext_level_block(field, neighbours, kernel, gain, w_in, b_in, w_out, scale, dilation):
    group = lax.axis_index("face")
    row_index = lax.axis_index("row")
    col_index = lax.axis_index("col")
    row_count = lax.axis_size("row")
    col_count = lax.axis_size("col")
    faces, height, breadth, channels = field.shape
    nside = height * row_count
    padded = with_halo(field, (("row", 1), ("col", 2)), dilation, False)
    upper = field[:, :dilation]
    lower = jnp.flip(field[:, height - dilation :], axis=1)
    leftmost = jnp.transpose(field[:, :, :dilation], (0, 2, 1, 3))
    rightmost = jnp.transpose(jnp.flip(field[:, :, breadth - dilation :], axis=2), (0, 2, 1, 3))
    upper = jnp.where(row_index == 0, upper, jnp.zeros_like(upper))
    lower = jnp.where(row_index == row_count - 1, lower, jnp.zeros_like(lower))
    leftmost = jnp.where(col_index == 0, leftmost, jnp.zeros_like(leftmost))
    rightmost = jnp.where(col_index == col_count - 1, rightmost, jnp.zeros_like(rightmost))
    row_pieces = jnp.stack([upper, lower], axis=1).reshape(faces * 2, dilation, breadth, channels)
    col_pieces = jnp.stack([leftmost, rightmost], axis=1).reshape(
        faces * 2, dilation, height, channels
    )
    row_lines = lax.psum(row_pieces.astype(jnp.float32).astype(jnp.bfloat16), "row")
    col_lines = lax.psum(col_pieces.astype(jnp.float32).astype(jnp.bfloat16), "col")
    links = lax.dynamic_slice_in_dim(neighbours, group * 3, 3, 0).reshape(12, 3)
    target = links[:, 0]
    target_edge = links[:, 1]
    flipped = links[:, 2]
    offset = (target // 3 - group + 5) % 4
    source = offset * 6 + target % 3 * 2 + target_edge % 2
    choose = jnp.arange(18)[None, :] == source[:, None]
    along_rows = target_edge < 2
    row_pick = (choose & along_rows[:, None]).astype(jnp.bfloat16)
    col_pick = (choose & jnp.logical_not(along_rows)[:, None]).astype(jnp.bfloat16)
    packed = jnp.concatenate([row_lines, col_lines], axis=2)
    moved = across_groups(packed).reshape(18, dilation, breadth + height, channels)
    row_sel = select_slots(row_pick, moved[:, :, :breadth]).astype(jnp.bfloat16)
    col_sel = select_slots(col_pick, moved[:, :, breadth:]).astype(jnp.bfloat16)
    row_whole = lax.all_gather(row_sel, "col", axis=2, tiled=True)
    col_whole = lax.all_gather(col_sel, "row", axis=2, tiled=True)
    strips = row_whole + col_whole
    strips = jnp.where(flipped[:, None, None, None] == 1, jnp.flip(strips, axis=2), strips)
    widened = jnp.pad(strips, ((0, 0), (0, 0), (dilation, dilation), (0, 0)))
    widened = widened.reshape(faces, 4, dilation, nside + 2 * dilation, channels)
    top_band = jnp.flip(
        lax.dynamic_slice_in_dim(widened[:, 0], col_index * breadth, breadth + 2 * dilation, 2),
        axis=1,
    )
    bottom_band = lax.dynamic_slice_in_dim(
        widened[:, 1], col_index * breadth, breadth + 2 * dilation, 2
    )
    left_band = jnp.flip(
        lax.dynamic_slice_in_dim(widened[:, 2], row_index * height, height + 2 * dilation, 2),
        axis=1,
    )
    left_band = jnp.transpose(left_band, (0, 2, 1, 3))
    right_band = jnp.transpose(
        lax.dynamic_slice_in_dim(widened[:, 3], row_index * height, height + 2 * dilation, 2),
        (0, 2, 1, 3),
    )
    padded = padded.at[:, :dilation].set(jnp.where(row_index == 0, top_band, padded[:, :dilation]))
    padded = padded.at[:, height + dilation :].set(
        jnp.where(row_index == row_count - 1, bottom_band, padded[:, height + dilation :])
    )
    padded = padded.at[:, :, :dilation].set(
        jnp.where(col_index == 0, left_band, padded[:, :, :dilation])
    )
    padded = padded.at[:, :, breadth + dilation :].set(
        jnp.where(col_index == col_count - 1, right_band, padded[:, :, breadth + dilation :])
    )

    def one_face(item):
        return convnext(item[0], item[1], kernel, gain, w_in, b_in, w_out, scale, dilation)

    return lax.map(one_face, (padded, field))


def per_device(
    fields,
    neighbours,
    w_enc,
    depthwise_kernel_first,
    norm_gain_first,
    expand_weight_first,
    expand_bias_first,
    contract_weight_first,
    layer_scale_first,
    w_down,
    depthwise_kernel_second,
    norm_gain_second,
    expand_weight_second,
    expand_bias_second,
    contract_weight_second,
    layer_scale_second,
):
    faces, height, flat_cols = fields.shape
    breadth = flat_cols // CIN
    encoder_level_zeroth = jnp.dot(
        fields.reshape(-1, CIN), w_enc, preferred_element_type=jnp.float32
    )
    encoder_level_zeroth = encoder_level_zeroth.astype(jnp.bfloat16).reshape(
        faces, height, breadth, C1
    )
    encoder_level_first = convnext_level_block(
        encoder_level_zeroth,
        neighbours,
        depthwise_kernel_first,
        norm_gain_first,
        expand_weight_first,
        expand_bias_first,
        contract_weight_first,
        layer_scale_first,
        DILATION_LEVEL1,
    )
    pooled = (
        encoder_level_first.astype(jnp.float32)
        .reshape(faces, height // 2, 2, breadth // 2, 2, C1)
        .mean(axis=(2, 4))
        .astype(jnp.bfloat16)
    )
    coarse_input = jnp.dot(pooled.reshape(-1, C1), w_down, preferred_element_type=jnp.float32)
    coarse_input = coarse_input.astype(jnp.bfloat16).reshape(faces, height // 2, breadth // 2, C2)
    features = convnext_level_block(
        coarse_input,
        neighbours,
        depthwise_kernel_second,
        norm_gain_second,
        expand_weight_second,
        expand_bias_second,
        contract_weight_second,
        layer_scale_second,
        DILATION_LEVEL2,
    )
    return features.reshape(faces, height // 2, breadth // 2 * C2)


def solution(mesh):
    return jax.shard_map(
        per_device,
        mesh=mesh,
        in_specs=(
            P("face", "row", "col"),
            P(),
            P(),
            P(),
            P(),
            P(),
            P(),
            P(),
            P(),
            P(),
            P(),
            P(),
            P(),
            P(),
            P(),
            P(),
        ),
        out_specs=P("face", "row", "col"),
        check_vma=False,
    )
```

profile of v0, /device:TPU:6, one launch (start us, length us, event | category | flops | bytes accessed | tf_op | source)
XLA Modules:
  0.0 840.0 jit_solution(15531137407725908295)
XLA Ops:
  6.5 2.3 reshape.427
  8.8 1.2 convolution_convert_fusion
  11.3 31.4 %psum.29 = bf16[6,1,32,128]{3,2,0,1:T(8,128)(2,1)S(1)} all-reduce(bf16[6,1,32,128]{3,2,0,1:T(8,128)(2,1)S(1)} %bitcast.226), channel_id=1, replica_groups=mesh['face'=4,'row'=16,'col'=8] {'col'}, use_global_device_ids=true, to_apply=%region_1.2 | all-reduce | flops 24576 | bytes 98304 | tf_op jit(solution)/shard_map/psum | solution.py:83
  42.7 106.7 %all-reduce.6.cloned.1.call-done = bf16[6,1,64,128]{3,2,0,1:T(8,128)(2,1)} async-done(((bf16[6,1,64,128]{3,2,0,1:T(8,128)(2,1)}), bf16[6,1,64,128]{3,2,0,1:T(8,128)(2,1)}) %all-reduce.6.cloned.1.call-update) | async-done | bytes 98320 | tf_op jit(solution)/shard_map/psum | solution.py:82
  150.3 1.9 collective-permute-start.4
  152.2 5.1 collective-permute-start.5
  158.3 1.8 collective-permute-done.5
  162.3 3.3 collective-permute-start
  165.6 1.3 collective-permute-start.1
  167.6 4.1 collective-permute-done.1
  171.8 1.2 copy-done.1
  173.0 3.6 collective-permute-start.2
  176.7 2.2 collective-permute-start.3
  178.9 1.5 collective-permute-done.2
  181.0 3.8 collective-permute-done.3
  184.8 2.4 pad_maximum_fusion
  187.2 21.8 %all-gather.11.cloned.1.call-done = bf16[12,512,128]{2,1,0:T(8,128)(2,1)} async-done(((bf16[12,64,128]{2,1,0:T(8,128)(2,1)}), bf16[12,512,128]{2,1,0:T(8,128)(2,1)}) %all-gather.11.cloned.1.call-update) | async-done | bytes 1572880 | tf_op jit(solution)/shard_map/all_gather | solution.py:98
  209.0 74.6 %all-gather.13.cloned.1.call-done = bf16[12,512,128]{2,1,0:T(8,128)(2,1)} async-done(((bf16[12,32,128]{2,1,0:T(8,128)(2,1)}), bf16[12,512,128]{2,1,0:T(8,128)(2,1)}) %all-gather.13.cloned.1.call-update) | async-done | bytes 1572880 | tf_op jit(solution)/shard_map/all_gather | solution.py:99
  283.6 3.5 add.199
  287.1 23.0 %reverse = bf16[12,512,128]{2,1,0:T(8,128)(2,1)} reverse(bf16[12,512,128]{2,1,0:T(8,128)(2,1)} %add.199), dimensions={1} | reverse | bytes 3145728
  310.1 2.1 bitcast_select_fusion
  314.3 2.2 scatter.30
  318.1 2.2 scatter.31
  320.4 54.8 %while.28 = (s32[]{:T(128)}, bf16[3,32,64,128]{3,2,1,0:T(8,128)(2,1)}, bf16[3,32,64,128]{3,2,1,0:T(8,128)(2,1)S(1)}, f32[128]{0:T(128)S(1)}, bf16[3,34,66,128]{3...) while((s32[]{:T(128)}, ...), condition=%wide.region_5.6_spmd, body=%wide.region_2.5_spmd.sunk | while | flops 616040448 | bytes 13560949 | solution.py:134
  320.9 1.2 fusion.184
  322.8 1.4 multiply_convert_fusion.5
  325.0 12.0 %fusion.185 = bf16[2048,128]{1,0:T(8,128)(2,1)} fusion(bf16[512,128]{1,0:T(8,128)(2,1)} %get-tuple-element.524, bf16[2048,128]{1,0:T(8,128)(2,1)} %bitcast.208, bf16[128,512]{1,0:T(8,128)(2,1)} %get-tuple-element.522, f32[512]{0:T(512)S(1)} %get-tuple-element.523, bf16[2048,128]{1,0:T(8,128)(2,1)} %bitcast.210, f32[128]{0:T(128)S(1)} %get-tuple-element.518), kind=kOutput, calls=%fused_computation.21.clone.1 | convolution fusion | flops 607125504 | bytes 1837568 | tf_op jit(solution)/shard_map/while/body/eval_jaxpr/dot_general | solution.py:48
  337.0 1.9 constant_dynamic-update-slice_fusion.7
  339.0 1.2 fusion.184
  340.8 1.4 multiply_convert_fusion.5
  343.1 12.0 %fusion.185 = bf16[2048,128]{1,0:T(8,128)(2,1)} fusion(bf16[512,128]{1,0:T(8,128)(2,1)} %get-tuple-element.524, bf16[2048,128]{1,0:T(8,128)(2,1)} %bitcast.208, bf16[128,512]{1,0:T(8,128)(2,1)} %get-tuple-element.522, f32[512]{0:T(512)S(1)} %get-tuple-element.523, bf16[2048,128]{1,0:T(8,128)(2,1)} %bitcast.210, f32[128]{0:T(128)S(1)} %get-tuple-element.518), kind=kOutput, calls=%fused_computation.21.clone.1 | convolution fusion | flops 607125504 | bytes 1837568 | tf_op jit(solution)/shard_map/while/body/eval_jaxpr/dot_general | solution.py:48
  355.1 1.9 constant_dynamic-update-slice_fusion.7
  357.0 1.2 fusion.184
  358.9 1.4 multiply_convert_fusion.5
  361.2 12.0 %fusion.185 = bf16[2048,128]{1,0:T(8,128)(2,1)} fusion(bf16[512,128]{1,0:T(8,128)(2,1)} %get-tuple-element.524, bf16[2048,128]{1,0:T(8,128)(2,1)} %bitcast.208, bf16[128,512]{1,0:T(8,128)(2,1)} %get-tuple-element.522, f32[512]{0:T(512)S(1)} %get-tuple-element.523, bf16[2048,128]{1,0:T(8,128)(2,1)} %bitcast.210, f32[128]{0:T(128)S(1)} %get-tuple-element.518), kind=kOutput, calls=%fused_computation.21.clone.1 | convolution fusion | flops 607125504 | bytes 1837568 | tf_op jit(solution)/shard_map/while/body/eval_jaxpr/dot_general | solution.py:48
  373.2 1.9 constant_dynamic-update-slice_fusion.7
  375.2 4.1 convert_reduce_fusion
  381.9 80.8 %all-reduce.10.cloned.1.call-done = bf16[6,2,16,256]{3,2,1,0:T(8,128)(2,1)} async-done(((bf16[6,2,16,256]{3,2,1,0:T(8,128)(2,1)}), bf16[6,2,16,256]{3,2,1,0:T(8,128)(2,1)}) %all-reduce.10.cloned.1.call-update) | async-done | bytes 98320 | tf_op jit(solution)/shard_map/psum | solution.py:83
  462.7 138.7 %all-reduce.8.cloned.1.call-done = bf16[6,2,32,256]{3,2,1,0:T(8,128)(2,1)} async-done(((bf16[6,2,32,256]{3,2,1,0:T(8,128)(2,1)}), bf16[6,2,32,256]{3,2,1,0:T(8,128)(2,1)}) %all-reduce.8.cloned.1.call-update) | async-done | bytes 196624 | tf_op jit(solution)/shard_map/psum | solution.py:82
  602.4 1.9 collective-permute-start.10
  604.3 5.1 collective-permute-start.11
  609.5 2.5 collective-permute-done.10
  612.0 1.8 collective-permute-done.11
  613.9 1.4 convolution_convert_fusion.2
  616.5 3.3 collective-permute-start.6
  619.8 1.3 collective-permute-start.7
  621.1 1.1 collective-permute-done.6
  622.3 4.7 collective-permute-done.7
  627.1 4.1 collective-permute-start.8
  631.2 1.9 collective-permute-start.9
  633.1 1.8 collective-permute-done.8
  634.9 4.8 collective-permute-done.9
  640.5 72.1 %all-gather.7.cloned.1.call-done = bf16[12,2,256,256]{3,0,2,1:T(8,128)(2,1)} async-done(((bf16[12,2,32,256]{3,0,2,1:T(8,128)(2,1)}), bf16[12,2,256,256]{3,0,2,1:T(8,128)(2,1)}) %all-gather.7.cloned.1.call-update) | async-done | bytes 3145744 | tf_op jit(solution)/shard_map/all_gather | solution.py:98
  712.7 80.6 %all-gather.9.cloned.1.call-done = bf16[12,2,256,256]{3,0,2,1:T(8,128)(2,1)} async-done(((bf16[12,2,16,256]{3,0,2,1:T(8,128)(2,1)}), bf16[12,2,256,256]{3,0,2,1:T(8,128)(2,1)}) %all-gather.9.cloned.1.call-update) | async-done | bytes 3145744 | tf_op jit(solution)/shard_map/all_gather | solution.py:99
  793.2 4.7 add.196
  797.9 1.8 reverse_select_fusion
  799.7 1.1 copy.104
  800.8 2.0 pad.25.clone
  802.8 1.1 fusion.155
  806.1 24.7 %while.29 = (s32[]{:T(128)}, bf16[3,16,32,256]{3,2,1,0:T(8,128)(2,1)}, bf16[3,16,32,256]{3,2,1,0:T(8,128)(2,1)S(1)}, f32[256]{0:T(256)S(1)}, bf16[3,20,36,256]{3...) while((s32[]{:T(128)}, ...), condition=%wide.region_12.13_spmd, body=%wide.region_9.12_spmd.sunk | while | flops 576455168 | bytes 7868021 | solution.py:134
  807.4 6.3 fusion.191
  815.6 6.3 fusion.191
  823.8 6.3 fusion.191
  830.8 2.2 reshape.443
  (159 shorter events, 28.5 us)
Async XLA Ops:
  6.5 372.9 %copy-start = (bf16[128,256]{1,0:T(8,128)(2,1)S(1)}, bf16[128,256]{1,0:T(8,128)(2,1)}, u32[]{:S(2)}) copy-start(bf16[128,256]{1,0:T(8,128)(2,1)} %param.45) | copy-start | bytes 196612
  6.5 142.9 %all-reduce.6.cloned.1.call-start = ((), (), s32[]{:S(2)}) async-start(), calls=%async_computation | async-start | bytes 196608 | tf_op jit(solution)/shard_map/psum | solution.py:82
  8.8 2.1 copy-start.9
  10.8 198.2 %all-gather.11.cloned.1.call-start = ((), (), s32[]{:S(2)}) async-start(), calls=%async_computation.5 | async-start | bytes 1769472 | tf_op jit(solution)/shard_map/all_gather | solution.py:98
  11.2 151.0 %copy-start.12 = (pred[12]{0:T(512)(128)(4,1)}, pred[12]{0:T(512)(128)(4,1)S(1)}, u32[]{:S(2)}) copy-start(pred[12]{0:T(512)(128)(4,1)S(1)} %get-tuple-element.324) | copy-start | bytes 40
  11.2 151.0 %copy-start.14 = (pred[12]{0:T(512)(128)(4,1)}, pred[12]{0:T(512)(128)(4,1)S(1)}, u32[]{:S(2)}) copy-start(pred[12]{0:T(512)(128)(4,1)S(1)} %get-tuple-element.323) | copy-start | bytes 40
  11.2 298.9 %copy-start.10 = (pred[12]{0:T(512)(128)(4,1)}, pred[12]{0:T(512)(128)(4,1)S(1)}, u32[]{:S(2)}) copy-start(pred[12]{0:T(512)(128)(4,1)S(1)} %get-tuple-element.322) | copy-start | bytes 40
  150.3 8.0 collective-permute-start.4
  152.2 7.8 collective-permute-start.5
  157.4 10.2 %copy-start.7 = (s32[12]{0:T(128)}, s32[12]{0:T(128)S(1)}, u32[]{:S(2)}) copy-start(s32[12]{0:T(128)S(1)} %fusion.151) | copy-start | bytes 148
  161.2 122.4 %all-gather.13.cloned.1.call-start = ((), (), s32[]{:S(2)}) async-start(), calls=%async_computation.6 | async-start | bytes 1671168 | tf_op jit(solution)/shard_map/all_gather | solution.py:99
  162.2 300.5 %all-reduce.10.cloned.1.call-start = ((), (), s32[]{:S(2)}) async-start(), calls=%async_computation.2 | async-start | bytes 196608 | tf_op jit(solution)/shard_map/psum | solution.py:83
  162.3 5.1 collective-permute-start
  165.6 6.1 collective-permute-start.1
  171.7 1.2 copy-start.1
  173.0 7.4 collective-permute-start.2
  176.7 8.2 collective-permute-start.3
  180.4 0.6 copy-start.4
  312.6 7.7 copy-start.3
  312.6 7.7 copy-start.6
  312.7 7.7 copy-start.17
  312.7 7.7 copy-start.19
  381.1 232.8 %copy-start.8 = (s32[12]{0:T(128)S(1)}, s32[12]{0:T(128)}, u32[]{:S(2)}) copy-start(s32[12]{0:T(128)} %copy-done.7) | copy-start | bytes 148
  381.1 232.8 %copy-start.15 = (pred[12]{0:T(512)(128)(4,1)S(1)}, pred[12]{0:T(512)(128)(4,1)}, u32[]{:S(2)}) copy-start(pred[12]{0:T(512)(128)(4,1)} %copy-done.14) | copy-start | bytes 40
  381.1 220.3 %all-reduce.8.cloned.1.call-start = ((), (), s32[]{:S(2)}) async-start(), calls=%async_computation.1 | async-start | bytes 393216 | tf_op jit(solution)/shard_map/psum | solution.py:82
  381.9 330.8 %all-gather.7.cloned.1.call-start = ((), (), s32[]{:S(2)}) async-start(), calls=%async_computation.3 | async-start | bytes 4718592 | tf_op jit(solution)/shard_map/all_gather | solution.py:98
  602.4 9.5 %collective-permute-start.10 = (bf16[1,6,2,48,256]{4,3,2,1,0:T(8,128)(2,1)S(1)}, bf16[1,6,2,48,256]{4,3,2,1,0:T(8,128)(2,1)S(1)}, u32[]{:S(2)}, u32[]{:S(2)}) collective-permute-start(bf16[1,6,2,48,256]{4,3,2,1,0:T(8,128)(2,1)S(1)} %maximum_bitcast_fusion), channel_id=1, source_target_pairs={{0,128},{128,256},{256,384},{384,0},{1,129},{129,257},{257,385},{3... | collective-permute-start | bytes 884744 | tf_op jit(solution)/shard_map/ppermute | solution.py:24
  604.3 9.4 %collective-permute-start.11 = (bf16[1,6,2,48,256]{4,3,2,1,0:T(8,128)(2,1)S(1)}, bf16[1,6,2,48,256]{4,3,2,1,0:T(8,128)(2,1)S(1)}, u32[]{:S(2)}, u32[]{:S(2)}) collective-permute-start(bf16[1,6,2,48,256]{4,3,2,1,0:T(8,128)(2,1)S(1)} %maximum_bitcast_fusion), channel_id=1, source_target_pairs={{128,0},{256,128},{384,256},{0,384},{129,1},{257,129},{385,257},{1... | collective-permute-start | bytes 884744 | tf_op jit(solution)/shard_map/ppermute | solution.py:26
  613.8 1.6 copy-start.13
  615.3 177.9 %all-gather.9.cloned.1.call-start = ((), (), s32[]{:S(2)}) async-start(), calls=%async_computation.4 | async-start | bytes 4456448 | tf_op jit(solution)/shard_map/all_gather | solution.py:99
  616.5 5.8 collective-permute-start.6
  619.8 7.2 collective-permute-start.7
  627.1 7.8 collective-permute-start.8
  631.2 8.6 %collective-permute-start.9 = (bf16[3,20,2,256]{3,2,1,0:T(2,128)(2,1)S(1)}, bf16[3,20,2,256]{3,2,1,0:T(2,128)(2,1)S(1)}, u32[]{:S(2)}, u32[]{:S(2)}) collective-permute-start(bf16[3,20,2,256]{3,2,1,0:T(2,128)(2,1)S(1)} %get-tuple-element.316), channel_id=1, source_target_pairs={{1,0},{2,1},{3,2},{4,3},{5,4},{6,5},{7,6},{9,8},{10,9},{11,10},{12... | collective-permute-start | bytes 184328 | tf_op jit(solution)/shard_map/ppermute | solution.py:26
  640.5 157.4 %copy-start.11 = (pred[12]{0:T(512)(128)(4,1)S(1)}, pred[12]{0:T(512)(128)(4,1)}, u32[]{:S(2)}) copy-start(pred[12]{0:T(512)(128)(4,1)} %copy-done.10) | copy-start | bytes 40
  802.8 3.3 copy-start.2
  802.8 3.3 copy-start.5
  802.8 3.3 copy-start.16
  802.8 3.3 copy-start.18
Sparse Core Ops, SparseCore 0:
  10.9 138.4 all-reduce.5
  161.3 47.6 all-gather.10
  211.3 72.2 all-gather.12
  381.2 81.4 all-reduce.9
  464.9 136.4 all-reduce.7
  615.4 97.2 all-gather.6
  715.0 78.2 all-gather.8
where the time goes:
time: 850 us; the launch traced here: 840 us
  waiting for transfers between devices  605 us (71%)
  matrix products  59.4 us (7%)
  local copies, waits for them, and re-layouts  55.6 us (7%)
  other arithmetic  38.3 us (5%)
  starting transfers between devices  35.4 us (4%)
  blocking collectives  31.4 us (4%)
  between operations  14.4 us (2%)
    psum x2, waiting for transfers between devices, convnext_level_block(): lax.psum(row_pieces.astype(jnp.float32).astype(jnp.bfloat16), 'row')  245 us
    all_gather x2, waiting for transfers between devices, convnext_level_block(): col_whole = lax.all_gather(col_sel, 'row', axis=2, tiled=True)  155 us
    all_gather x2, waiting for transfers between devices, convnext_level_block(): row_whole = lax.all_gather(row_sel, 'col', axis=2, tiled=True)  93.9 us
    psum x1, waiting for transfers between devices, convnext_level_block(): lax.psum(col_pieces.astype(jnp.float32).astype(jnp.bfloat16), 'col')  80.8 us
    dot_general x6, matrix products, convnext(): update = jnp.dot(hidden, w_out, preferred_element_type=jnp.float32)  54.8 us
    psum x1, blocking collectives, convnext_level_block(): lax.psum(col_pieces.astype(jnp.float32).astype(jnp.bfloat16), 'col')  31.4 us
    unnamed x44, local copies, waits for them, and re-layouts  26.2 us
    ppermute x6, waiting for transfers between devices, with_halo(): lax.ppermute(head, axis, [((i + 1) % count, i) for i in range(ends)])  21 us
  transfers between devices with their start and end apart: 19, of which 19 were waited for; matrix products, arithmetic and copies ran while one was open for 1% of the time, Pallas kernels for 0%

commit v1 on v0

v1 whole, which is shorter than its diff:
```python
import functools

import jax
import jax.numpy as jnp
import numpy as np
from jax import lax
from jax.experimental import pallas as pl
from jax.experimental.pallas import tpu as pltpu
from jax.sharding import PartitionSpec as P

CIN = 16
C1 = 128
C2 = 256
HID1 = 512
HID2 = 1024
EPSILON = 1e-06
DEPTH = 5
F32 = jnp.float32
BF16 = jnp.bfloat16

ERF = (7.97827572e-01, 3.64699375e-02, -1.25479103e-04, -3.04667360e-05, 1.11260815e-06)


def upper_windows():
    table = np.zeros((8, 16), np.int32)
    for c in range(8):
        for dest in range(16):
            flipped = 15 - dest
            if dest // 2 == c:
                table[c, dest] = dest % 2
            elif flipped // 2 == c:
                table[c, dest] = flipped % 2
            elif 2 * c + 2 in (dest, flipped):
                table[c, dest] = 1
    return table


UPPER = upper_windows()


def gelu(x):
    square = jnp.minimum(x * x, 36.0)
    poly = ERF[4]
    for coefficient in ERF[3::-1]:
        poly = poly * square + coefficient
    half = 0.5 * x
    return half + half * jnp.tanh(x * poly)


def spots(shape, dim):
    return lax.broadcasted_iota(jnp.int32, shape, dim)


def one_hot(mask):
    return jnp.where(mask, 1.0, 0.0).astype(BF16)


def dot(a, b):
    return jnp.dot(a, b, preferred_element_type=F32)


def route_kernel(nb, pos, recv, own, opp, out, chunks, strip):
    g, r, c = pos[0], pos[1], pos[2]
    outer = jnp.logical_or(r == 0, r == 15)
    side = jnp.logical_or(c == 0, c == 7)
    out[...] = jnp.zeros_like(out)
    chunks[...] = jnp.zeros_like(chunks)

    @pl.when(outer)
    def _():
        mine = jnp.where(r == 0, 0, 1)
        chunks[mine, 8:72, :] = own[...].astype(F32)
        chunks[1 - mine, 8:72, :] = opp[...].astype(F32)

    @pl.when(jnp.logical_not(outer))
    def _():
        flip = 15 - r
        far = jnp.where(
            r // 2 == c,
            r % 2,
            jnp.where(
                flip // 2 == c,
                flip % 2,
                jnp.where(jnp.logical_or(r == 2 * c + 2, flip == 2 * c + 2), 1, 0),
            ),
        )
        start = pl.multiple_of(8 + 16 * far, 8)
        chunks[0, pl.ds(start, 48), :] = recv[0].astype(F32)
        chunks[1, pl.ds(start, 48), :] = recv[15].astype(F32)

    @pl.when(side)
    def _():
        strip[0:8, :] = jnp.zeros((8, 256), F32)
        strip[520:528, :] = jnp.zeros((8, 256), F32)
        for k in range(16):
            strip[8 + 32 * k : 40 + 32 * k, :] = recv[k, 0:32, :].astype(F32)

        @pl.when(jnp.logical_not(outer))
        def _():
            for k, row in ((0, 32), (15, 488)):
                block = recv[k].astype(F32)
                strip[row : row + 8, :] = jnp.where(c == 0, block[0:8], block[40:48])

    def lanes(source_face, dest_face, dest_edge):
        a = spots((256, 256), 0)
        b = spots((256, 256), 1)
        rest = b - 80 * dest_face
        depth = rest // 16
        depth = jnp.where(dest_edge == 2, 4 - depth, depth)
        wanted = 80 * source_face + 16 * depth + rest % 16
        return one_hot(
            jnp.logical_and(jnp.logical_and(rest >= 0, rest < 80), a == wanted)
        )

    def one_strip(k, carry):
        face, edge = k // 4, k % 4
        base = ((3 * g + face) * 4 + edge) * 3
        other, dest_edge, turned = nb[base], nb[base + 1], nb[base + 2]
        dest_group, dest_face = other // 3, other % 3
        along_rows = edge < 2
        dest_rows = dest_edge < 2

        @pl.when(jnp.logical_and(along_rows, jnp.logical_not(dest_rows)))
        def _():
            data = chunks[edge].astype(BF16)
            moved = dot(data, lanes(face, dest_face, dest_edge)).astype(BF16)
            q = 64 * c + spots((48, 80), 1) - 8
            p = jnp.where(turned == 1, 511 - q, q)
            pick = one_hot(p - 32 * r + 8 == spots((48, 80), 0))
            block = dest_group * 8 + jnp.where(dest_edge == 2, 0, 7)
            out[block, 80:128, :] += dot(pick, moved).astype(BF16)

        @pl.when(
            jnp.logical_and(
                jnp.logical_and(along_rows, outer),
                jnp.logical_and(dest_rows, dest_edge == jnp.where(r == 0, 0, 1)),
            )
        )
        def _():
            data = chunks[edge].astype(BF16)
            moved = dot(data, lanes(face, dest_face, dest_edge)).astype(BF16)
            q = 64 * c + spots((80, 80), 1) - 8
            p = jnp.where(turned == 1, 511 - q, q)
            middle = jnp.where(turned == 1, 7 - c, c)
            for shift in (-1, 0, 1):
                target = middle + shift

                @pl.when(jnp.logical_and(target >= 0, target < 8))
                def _():
                    pick = one_hot(p - 64 * target + 8 == spots((80, 80), 0))
                    out[dest_group * 8 + target, 0:80, :] += dot(pick, moved).astype(BF16)

        held = jnp.logical_or(
            jnp.logical_and(edge == 2, c == 0), jnp.logical_and(edge == 3, c == 7)
        )

        @pl.when(jnp.logical_and(held, jnp.logical_not(dest_rows)))
        def _():
            start = pl.multiple_of(32 * jnp.where(turned == 1, 15 - r, r), 8)
            data = strip[pl.ds(start, 48), :].astype(BF16)
            moved = dot(data, lanes(face, dest_face, dest_edge)).astype(BF16)
            x = spots((48, 48), 1)
            pick = one_hot(jnp.where(turned == 1, 47 - x, x) == spots((48, 48), 0))
            block = dest_group * 8 + jnp.where(dest_edge == 2, 0, 7)
            out[block, 80:128, :] += dot(pick, moved).astype(BF16)

        @pl.when(
            jnp.logical_and(
                jnp.logical_and(held, outer),
                jnp.logical_and(dest_rows, dest_edge == jnp.where(r == 0, 0, 1)),
            )
        )
        def _():
            place = lanes(face, dest_face, dest_edge)
            x = spots((80, 80), 1)
            pick = one_hot(jnp.where(turned == 1, 79 - x, x) == spots((80, 80), 0))

            def one_chunk(target, carry):
                start = pl.multiple_of(
                    jnp.where(turned == 1, 448 - 64 * target, 64 * target), 8
                )
                data = strip[pl.ds(start, 80), :].astype(BF16)
                moved = dot(data, place).astype(BF16)
                out[dest_group * 8 + target, 0:80, :] += dot(pick, moved).astype(BF16)
                return carry

            lax.fori_loop(0, 8, one_chunk, 0)

        return carry

    lax.fori_loop(0, 12, one_strip, 0)

    @pl.when(jnp.logical_and(outer, side))
    def _():
        def one_run(k, carry):
            group, rest = k // 12, k % 12
            right, run = rest // 6, rest % 6
            level, dest_face = run // 3, run % 3
            dest_edge = jnp.where(
                level == 0, jnp.where(r == 0, 0, 1), jnp.where(right == 1, 3, 2)
            )
            first = ((3 * group + dest_face) * 4 + dest_edge) * 3
            far = jnp.where(level == 0, right, jnp.where(r == 0, 0, 1))
            edge = nb[first + 1]
            far = jnp.where(nb[first + 2] == 1, 1 - far, far)
            across = jnp.where(edge < 2, 2 + far, far)
            second = (nb[first] * 4 + across) * 3
            edge_far = edge % 2
            source, source_edge = nb[second], nb[second + 1]
            end = jnp.where(nb[second + 2] == 1, 1 - edge_far, edge_far)
            column = jnp.where(
                source_edge == 2, 0, jnp.where(source_edge == 3, 7, jnp.where(end == 0, 0, 7))
            )

            @pl.when(jnp.logical_and(source // 3 == g, column == c))
            def _():
                a = spots((256, 256), 0)
                b = spots((256, 256), 1)
                place = one_hot(
                    jnp.logical_and(b >= 240, a == 80 * (source % 3) + b - 240)
                )
                near = pl.multiple_of(jnp.where(end == 1, 64, 8), 8)
                in_chunk = chunks[jnp.minimum(source_edge, 1), pl.ds(near, 8), :]
                wide = pl.multiple_of(jnp.where(end == 1, 512, 8), 8)
                in_strip = strip[pl.ds(wide, 8), :]
                data = jnp.where(source_edge < 2, in_chunk, in_strip).astype(BF16)
                moved = dot(data, place).astype(BF16)
                x = spots((16, 8), 1)
                order = jnp.where(end == 1, 7 - x, x)
                order = jnp.where(order < DEPTH, order + 8 * (run % 2), -1)
                pick = one_hot(order == spots((16, 8), 0))
                row = pl.multiple_of(16 * (run // 2), 16)
                out[group * 8 + 7 * right, pl.ds(row, 16), :] += dot(pick, moved).astype(BF16)

            return carry

        lax.fori_loop(0, 48, one_run, 0)


def normalise(mixed, gain):
    center = jnp.mean(mixed, axis=-1, keepdims=True)
    apart = mixed - center
    spread = jnp.mean(apart * apart, axis=-1, keepdims=True)
    return (apart * lax.rsqrt(spread + EPSILON) * gain).astype(BF16)


def rounded(x):
    return x.astype(BF16).astype(F32)


def block_kernel(
    nb,
    pos,
    fields,
    above,
    below,
    before,
    after,
    bands,
    enc_cells,
    enc_bands,
    kernel_first,
    gain_first,
    expand_first,
    bias_first,
    contract_first,
    scale_first,
    down,
    kernel_second,
    gain_second,
    expand_second,
    bias_second,
    contract_second,
    scale_second,
    out,
    cells,
    grid,
    banded,
    taps,
    mix,
    rows,
    pooled,
    coarse,
):
    g, r, c = pos[0], pos[1], pos[2]
    top, bottom, left, right = r == 0, r == 15, c == 0, c == 7
    outer = jnp.logical_or(top, bottom)
    side = jnp.logical_or(left, right)
    corner = jnp.logical_and(outer, side)

    @pl.when(jnp.logical_or(outer, side))
    def _():
        def add(k, total):
            return total + bands[k].astype(F32)

        total = lax.fori_loop(0, 32, add, jnp.zeros((128, 256), F32)).astype(BF16)
        for k in range(16):
            banded[k] = rounded(dot(total, enc_bands[:, 128 * k : 128 * k + 128]))

    def band_tap(face, edge, a, b):
        base = ((3 * g + face) * 4 + edge) * 3
        other_edge, turned = nb[base + 1], nb[base + 2]
        down_row, down_col = a - 1, b - 1
        deep = jnp.where(
            edge == 0,
            -down_row,
            jnp.where(edge == 1, down_row, jnp.where(edge == 2, -down_col, down_col)),
        )
        along = jnp.where(edge < 2, down_col, down_row)
        along = jnp.where(turned == 1, -along, along)
        inward = jnp.where(other_edge % 2 == 0, deep, -deep)
        tap_row = jnp.where(other_edge < 2, inward, along)
        tap_col = jnp.where(other_edge < 2, along, inward)
        return kernel_first[pl.ds((tap_row + 1) * 3 + tap_col + 1, 1), :]

    def one_face(i, carry):
        cells[0] = before[i].astype(F32)
        cells[9] = after[i].astype(F32)
        for k in range(8):
            cells[1 + k, 0:8, :] = above[i, :, 128 * k : 128 * k + 128].astype(F32)
            cells[1 + k, 8:40, :] = fields[i, :, 128 * k : 128 * k + 128].astype(F32)
            cells[1 + k, 40:48, :] = below[i, :, 128 * k : 128 * k + 128].astype(F32)

        def encode(k, carry):
            product = rounded(dot(cells[k].astype(BF16), enc_cells[...]))
            for j in range(8):
                grid[8 * k + j] = product[:, 128 * j : 128 * j + 128]
            return carry

        lax.fori_loop(0, 10, encode, 0)

        @pl.when(left)
        def _():
            for k in range(DEPTH):
                grid[3 + k] = banded[5 * i + k, 80:128, :]

        @pl.when(right)
        def _():
            for k in range(DEPTH):
                grid[72 + k] = banded[5 * i + k, 80:128, :]

        @pl.when(outer)
        def _():
            def one_cell(j, carry):
                for k in range(DEPTH):
                    line = banded[5 * i + k, pl.ds(j, 1), :]
                    grid[j, pl.ds(jnp.where(top, 7 - k, 40 + k), 1), :] = line
                return carry

            lax.fori_loop(0, 80, one_cell, 0)

        for a in range(3):
            for b in range(3):
                tap = jnp.broadcast_to(kernel_first[3 * a + b : 3 * a + b + 1, :], (40, 128))
                for kind in range(3):
                    taps[kind, 3 * a + b] = tap

        @pl.when(outer)
        def _():
            edge = jnp.where(top, 0, 1)
            for a in range(3):
                for b in range(3):
                    line = jnp.broadcast_to(band_tap(i, edge, a, b), (4, 128))
                    for kind in range(3):

                        @pl.when(top)
                        def _():
                            taps[kind, 3 * a + b, 0:4, :] = line

                        @pl.when(bottom)
                        def _():
                            taps[kind, 3 * a + b, 36:40, :] = line

        @pl.when(side)
        def _():
            edge = jnp.where(left, 2, 3)
            for a in range(3):
                for b in range(3):
                    line = band_tap(i, edge, a, b)
                    taps[jnp.where(left, 0, 2), 3 * a + b] = jnp.broadcast_to(line, (40, 128))

        def one_chunk(k, carry):
            j0 = 4 + 8 * k
            for half in range(2):
                start = j0 + 4 * half
                place = 2 * k + half
                kind = jnp.where(place == 0, 0, jnp.where(place == 17, 2, 1))
                total = jnp.zeros((4, 40, 128), F32)
                for a in range(3):
                    for b in range(3):
                        window = grid[pl.ds(start + b - 1, 4), 3 + a : 43 + a, :]
                        total = total + window * taps[kind, 3 * a + b][None]
                mix[4 * half : 4 * half + 4] = total

            @pl.when(jnp.logical_and(corner, k == jnp.where(left, 0, 8)))
            def _():
                edge_row = jnp.where(top, 0, 1)
                edge_col = jnp.where(left, 2, 3)
                out_a = jnp.where(top, 0, 2)
                out_b = jnp.where(left, 0, 2)
                row_in, row_out = jnp.where(top, 8, 39), jnp.where(top, 7, 40)
                col_in, col_out = jnp.where(left, 8, 71), jnp.where(left, 7, 72)
                step_row, step_col = jnp.where(top, -1, 1), jnp.where(left, -1, 1)
                row_lines = [-grid[col_out, pl.ds(row_in, 1), :]] + [
                    banded[15, pl.ds(8 * i + d, 1), :] for d in range(DEPTH)
                ]
                col_lines = [-grid[col_in, pl.ds(row_out, 1), :]] + [
                    banded[15, pl.ds(24 + 8 * i + d, 1), :] for d in range(DEPTH)
                ]
                row_taps = [band_tap(i, edge_row, 1 + s * step_row, out_b) for s in (-1, 0, 1)]
                col_taps = [band_tap(i, edge_col, out_a, 1 + s * step_col) for s in (-1, 0, 1)]
                for depth in range(4):
                    extra = sum(row_taps[s] * row_lines[depth + s] for s in range(3))
                    at = (col_in - j0, pl.ds(row_out + depth * step_row - 4, 1))
                    mix[at[0], at[1], :] += extra
                    extra = sum(col_taps[s] * col_lines[depth + s] for s in range(3))
                    at = (col_out + depth * step_col - j0, pl.ds(row_in - 4, 1))
                    mix[at[0], at[1], :] += extra

            normed = normalise(mix[...].reshape(320, C1), gain_first[...])
            hidden = gelu(dot(normed, expand_first[...]) + bias_first[...]).astype(BF16)
            update = dot(hidden, contract_first[...])
            here = grid[pl.ds(j0, 8), 4:44, :].reshape(320, C1)
            rows[...] = rounded(here + scale_first[...] * update).reshape(8, 40, C1)
            paired = rows[:, pl.ds(0, 20, stride=2), :] + rows[:, pl.ds(1, 20, stride=2), :]
            paired = paired.reshape(4, 2, 20, C1)
            pooled[pl.ds(4 * k, 4), 0:20, :] = 0.25 * (paired[:, 0] + paired[:, 1])
            return carry

        lax.fori_loop(0, 9, one_chunk, 0)
        pooled[:, 20:24, :] = jnp.zeros((36, 4, C1), F32)
        product = dot(pooled[...].reshape(36 * 24, C1).astype(BF16), down[...])
        coarse[...] = rounded(product).reshape(36, 24, C2)

        for at_row, row in ((top, 0), (bottom, 18)):
            for at_col, column in ((left, 0), (right, 34)):

                @pl.when(jnp.logical_and(at_row, at_col))
                def _():
                    coarse[column : column + 2, row : row + 2, :] = jnp.zeros((2, 2, C2), F32)

        for part in range(2):
            total = jnp.zeros((16, 16, C2), F32)
            for a in range(3):
                for b in range(3):
                    window = coarse[16 * part + 2 * b : 16 * part + 2 * b + 16, 2 * a : 2 * a + 16, :]
                    total = total + window * kernel_second[3 * a + b : 3 * a + b + 1, :][None]
            normed = normalise(total.reshape(256, C2), gain_second[...])
            hidden = gelu(dot(normed, expand_second[...]) + bias_second[...]).astype(BF16)
            update = dot(hidden, contract_second[...])
            here = coarse[16 * part + 2 : 16 * part + 18, 2:18, :].reshape(256, C2)
            result = (here + scale_second[...] * update).astype(BF16).reshape(16, 16, C2)
            for j in range(16):
                column = (16 * part + j) * C2
                out[i, :, column : column + C2] = result[j]
        return carry

    lax.fori_loop(0, 3, one_face, 0)


def per_device(
    fields,
    neighbours,
    w_enc,
    depthwise_kernel_first,
    norm_gain_first,
    expand_weight_first,
    expand_bias_first,
    contract_weight_first,
    layer_scale_first,
    w_down,
    depthwise_kernel_second,
    norm_gain_second,
    expand_weight_second,
    expand_bias_second,
    contract_weight_second,
    layer_scale_second,
):
    r, c = lax.axis_index("row"), lax.axis_index("col")
    pos = jnp.stack([lax.axis_index("face"), r, c]).astype(jnp.int32)
    links = neighbours.reshape(144)

    lines = jnp.where(r == 15, jnp.flip(fields[:, 27:], axis=1), fields[:, :5])
    lines = lines.reshape(3, 5, 64, CIN).transpose(2, 0, 1, 3).reshape(64, 240)
    lines = jnp.pad(lines, ((0, 0), (0, 16)))
    sides = jnp.where(
        c == 7,
        jnp.flip(fields[:, :, 59 * CIN :].reshape(3, 32, 5, CIN), axis=2),
        fields[:, :, : 5 * CIN].reshape(3, 32, 5, CIN),
    )
    sides = sides.transpose(1, 0, 2, 3).reshape(32, 240)
    sides = jnp.pad(sides, ((0, 16), (0, 16)))
    on_side = jnp.logical_or(c == 0, c == 7)
    outer = jnp.logical_or(r == 0, r == 15)
    nearest = jnp.where(r == 0, sides[24:32], sides[0:8])
    upper = jnp.concatenate(
        [jnp.where(c == 0, nearest, lines[16:24]), lines[24:]], axis=0
    )
    lower = jnp.concatenate(
        [lines[:40], jnp.where(c == 7, nearest, lines[40:48])], axis=0
    )
    chosen = lax.dynamic_index_in_dim(jnp.asarray(UPPER), c, 0, keepdims=False)
    windows = jnp.where((chosen == 1)[:, None, None], upper[None], lower[None])
    inner = np.arange(16)
    inner = jnp.asarray((inner > 0) & (inner < 15))
    use_lines = jnp.logical_and(outer, inner)[:, None, None]
    send = jnp.where(use_lines, windows, sides[None])
    recv = lax.all_to_all(send, "row", 0, 0)
    opposite = lax.ppermute(lines, "row", [(0, 15), (15, 0)])

    above = lax.ppermute(fields[:, 24:], "row", [(k, k + 1) for k in range(15)])
    below = lax.ppermute(fields[:, :8], "row", [(k + 1, k) for k in range(15)])
    first = jnp.concatenate([above[:, :, :128], fields[:, :, :128], below[:, :, :128]], axis=1)
    last = jnp.concatenate([above[:, :, 896:], fields[:, :, 896:], below[:, :, 896:]], axis=1)
    before = lax.ppermute(last, "col", [(k, k + 1) for k in range(7)])
    after = lax.ppermute(first, "col", [(k + 1, k) for k in range(7)])

    smem = pl.BlockSpec(memory_space=pltpu.SMEM)
    vmem = pl.BlockSpec(memory_space=pltpu.VMEM)
    routed = pl.pallas_call(
        route_kernel,
        out_shape=jax.ShapeDtypeStruct((32, 128, 256), BF16),
        in_specs=[smem, smem, vmem, vmem, vmem],
        out_specs=vmem,
        scratch_shapes=[pltpu.VMEM((2, 80, 256), F32), pltpu.VMEM((528, 256), F32)],
        compiler_params=pltpu.CompilerParams(vmem_limit_bytes=32 * 2**20),
        name="route",
    )(links, pos, recv, lines, opposite)
    bands = lax.all_to_all(routed, ("face", "col"), 0, 0)

    enc_cells = jnp.kron(jnp.eye(8, dtype=BF16), w_enc)
    enc_bands = jnp.kron(jnp.eye(16, dtype=BF16), w_enc)
    operands = (
        links,
        pos,
        fields,
        above,
        below,
        before,
        after,
        bands,
        enc_cells,
        enc_bands,
        depthwise_kernel_first.reshape(9, C1),
        norm_gain_first.reshape(1, C1),
        expand_weight_first,
        expand_bias_first.reshape(1, HID1),
        contract_weight_first,
        layer_scale_first.reshape(1, C1),
        w_down,
        depthwise_kernel_second.reshape(9, C2),
        norm_gain_second.reshape(1, C2),
        expand_weight_second,
        expand_bias_second.reshape(1, HID2),
        contract_weight_second,
        layer_scale_second.reshape(1, C2),
    )
    return pl.pallas_call(
        block_kernel,
        out_shape=jax.ShapeDtypeStruct((3, 16, 32 * C2), BF16),
        in_specs=[smem, smem] + [vmem] * (len(operands) - 2),
        out_specs=vmem,
        scratch_shapes=[
            pltpu.VMEM((10, 48, 128), F32),
            pltpu.VMEM((80, 48, 128), F32),
            pltpu.VMEM((16, 128, 128), F32),
            pltpu.VMEM((3, 9, 40, 128), F32),
            pltpu.VMEM((8, 40, 128), F32),
            pltpu.VMEM((8, 40, 128), F32),
            pltpu.VMEM((36, 24, 128), F32),
            pltpu.VMEM((36, 24, 256), F32),
        ],
        compiler_params=pltpu.CompilerParams(vmem_limit_bytes=48 * 2**20),
        name="blocks",
    )(*operands)


def solution(mesh):
    return jax.shard_map(
        per_device,
        mesh=mesh,
        in_specs=(P("face", "row", "col"),) + (P(),) * 15,
        out_specs=P("face", "row", "col"),
        check_vma=False,
    )
```

time: 850 us -> 148 us (0.17)
  the two profiles are of different devices: /device:TPU:6 before, /device:TPU:1 now
where the time goes in v1:
time: 148 us; the launch traced here: 146 us
  Pallas kernels  51.5 us (35%)
  starting transfers between devices  45.6 us (31%)
  waiting for transfers between devices  28 us (19%)
  local copies, waits for them, and re-layouts  16.4 us (11%)
  other arithmetic  4.64 us (3%)
    pallas_call x1, Pallas kernels, per_device(): pl.pallas_call(block_kernel, out_shape=jax.ShapeDtypeStruct((3, 16, 32 *...  45.6 us
    all_to_all x1, starting transfers between devices, per_device(): bands = lax.all_to_all(routed, ('face', 'col'), 0, 0)  16.9 us
    all_to_all x1, starting transfers between devices, per_device(): recv = lax.all_to_all(send, 'row', 0, 0)  15.7 us
    unnamed x41, local copies, waits for them, and re-layouts  12.3 us
    ppermute x1, waiting for transfers between devices, per_device(): opposite = lax.ppermute(lines, 'row', [(0, 15), (15, 0)])  11.9 us
    ppermute x1, waiting for transfers between devices, per_device(): after = lax.ppermute(first, 'col', [(k + 1, k) for k in range(7)])  9.83 us
    pallas_call x1, Pallas kernels, per_device(): pl.pallas_call(route_kernel, out_shape=jax.ShapeDtypeStruct((32, 128, 256...  5.92 us
    ppermute x1, starting transfers between devices, per_device(): before = lax.ppermute(last, 'col', [(k, k + 1) for k in range(7)])  4.59 us
  transfers between devices with their start and end apart: 7, of which 5 were waited for; matrix products, arithmetic and copies ran while one was open for 3% of the time, Pallas kernels for 0%

profile of v1, /device:TPU:1, one launch (start us, length us, event | category | flops | bytes accessed | tf_op | source)
XLA Modules:
  0.0 146.4 jit_solution(8628992788733653542)
XLA Ops:
  0.0 0.0 copy-start.17
  0.0 0.8 fusion.2
  0.8 0.8 slice.66
  1.7 0.1 copy.29
  1.8 0.1 copy.30
  1.9 0.1 copy.25
  2.0 0.3 rev.9
  2.3 0.8 slice_select_fusion
  3.1 0.2 reshape.84
  3.3 0.1 copy.27
  3.5 0.1 copy.28
  3.6 0.7 compare_bitcast_fusion
  4.3 0.7 broadcast_and_fusion
  5.0 0.9 select_select_fusion
  5.9 15.7 %all-to-all-start = ((bf16[16,48,256]{2,1,0:T(8,128)(2,1)}), bf16[16,48,256]{2,1,0:T(8,128)(2,1)S(1)}, u32[]{:S(2)}, u32[]{:S(2)}) async-start(bf16[16,48,256]{2,1,0:T(8,128)(2,1)} %select_select_fusion), calls=%async_computation | async-start | bytes 786432 | tf_op jit(solution)/shard_map/all_to_all | solution.py:508
  21.6 4.5 %collective-permute-start.4 = (bf16[64,256]{1,0:T(8,128)(2,1)S(1)}, bf16[64,256]{1,0:T(8,128)(2,1)S(1)}, u32[]{:S(2)}, u32[]{:S(2)}) collective-permute-start(bf16[64,256]{1,0:T(8,128)(2,1)S(1)} %pad.9.own), channel_id=1, source_target_pairs={{0,120},{120,0},{1,121},{121,1},{2,122},{122,2},{3,123},{123,3},{4... | collective-permute-start | bytes 98312 | tf_op jit(solution)/shard_map/ppermute | solution.py:509
  26.1 0.1 pad_add_fusion.pos
  26.2 0.0 copy-done.17
  26.2 0.1 copy.22
  26.3 0.1 reshape.80.nb
  26.4 11.9 %collective-permute-done.4.opp = bf16[64,256]{1,0:T(8,128)(2,1)S(1)} collective-permute-done((bf16[64,256]{1,0:T(8,128)(2,1)S(1)}, bf16[64,256]{1,0:T(8,128)(2,1)S(1)}, u32[]{:S(2)}, u32[]{:S(2)}) %collective-permute-start.4) | collective-permute-done | bytes 32800 | tf_op jit(solution)/shard_map/ppermute | solution.py:509
  38.3 1.3 all-to-all-done.recv
  39.6 5.9 %route.1 = bf16[32,128,256]{2,1,0:T(8,128)(2,1)S(1)} custom-call(s32[144]{0:T(256)S(1)} %reshape.80.nb, s32[3]{0:T(128)S(1)} %pad_add_fusion.pos, bf16[16,48,256]{2,1,0:T(8,128)(2,1)S(1)} %all-to-all-done.recv, bf16[64,256]{1,0:T(8,128)(2,1)S(1)} %pad.9.own, bf16[64,256]{1,0:T(8,128)(2,1)S(1)} %collective-permute-done.4.opp), custom_call_target="tpu_custom_call" | custom-call | tf_op jit(solution)/shard_map/route/pallas_call | solution.py:520
  45.5 0.0 copy-start
  45.5 1.3 copy-done
  46.9 0.0 copy-start.1
  46.9 0.0 copy-start.16
  46.9 16.9 %all-to-all-start.1 = ((bf16[32,128,256]{2,1,0:T(8,128)(2,1)}), bf16[32,128,256]{2,1,0:T(8,128)(2,1)S(1)}, u32[]{:S(2)}, u32[]{:S(2)}) async-start(bf16[32,128,256]{2,1,0:T(8,128)(2,1)} %copy-done), calls=%async_computation.1 | async-start | bytes 4194304 | tf_op jit(solution)/shard_map/all_to_all | solution.py:529
  63.8 0.0 copy-done.1
  63.8 1.3 collective-permute-start
  65.1 1.3 collective-permute-start.1
  66.4 0.0 copy-done.16
  66.4 0.0 copy-start.5
  66.5 0.1 broadcast_multiply_fusion
  66.6 0.0 collective-permute-done.above
  66.6 3.6 %collective-permute-done.1.below = bf16[3,8,1024]{2,1,0:T(8,128)(2,1)S(1)} collective-permute-done((bf16[3,8,1024]{2,1,0:T(8,128)(2,1)S(1)}, bf16[3,8,1024]{2,1,0:T(8,128)(2,1)S(1)}, u32[]{:S(2)}, u32[]{:S(2)}) %collective-permute-start.1) | collective-permute-done | bytes 49184 | tf_op jit(solution)/shard_map/ppermute | solution.py:512
  70.2 0.0 copy-start.7
  70.2 0.6 pad_maximum_fusion.1
  70.9 1.3 collective-permute-start.3
  72.2 0.6 pad_maximum_fusion
  72.8 4.6 %collective-permute-start.2 = (bf16[3,48,128]{2,1,0:T(8,128)(2,1)}, bf16[3,48,128]{2,1,0:T(8,128)(2,1)}, u32[]{:S(2)}, u32[]{:S(2)}) collective-permute-start(bf16[3,48,128]{2,1,0:T(8,128)(2,1)} %pad_maximum_fusion), channel_id=1, source_target_pairs={{0,1},{1,2},{2,3},{3,4},{4,5},{5,6},{6,7},{8,9},{9,10},{10,11},{11... | collective-permute-start | bytes 110600 | tf_op jit(solution)/shard_map/ppermute | solution.py:515
  77.4 0.1 broadcast_multiply_fusion.1
  77.5 0.0 copy-done.7
  77.5 0.3 copy.35
  77.8 0.8 copy.36
  78.5 0.7 reshape.90.kernel_second
  79.2 0.7 reshape.86.kernel_first
  79.9 9.8 %collective-permute-done.3.after = bf16[3,48,128]{2,1,0:T(8,128)(2,1)} collective-permute-done((bf16[3,48,128]{2,1,0:T(8,128)(2,1)}, bf16[3,48,128]{2,1,0:T(8,128)(2,1)}, u32[]{:S(2)}, u32[]{:S(2)}) %collective-permute-start.3) | collective-permute-done | bytes 36896 | tf_op jit(solution)/shard_map/ppermute | solution.py:516
  89.7 0.0 collective-permute-done.2.before
  89.8 1.4 all-to-all-done.1.bands
  91.2 0.0 copy-done.5
  91.2 0.9 copy-done.2
  92.1 1.0 copy-done.3
  93.2 1.0 copy-done.4
  94.2 0.9 copy-done.6
  95.1 0.8 copy-done.8
  95.9 0.8 copy-done.9
  96.8 0.7 copy-done.10
  97.5 0.7 copy-done.11
  98.1 0.7 copy-done.12
  98.8 0.7 copy-done.13
  99.5 0.7 copy-done.14
  100.2 0.7 copy-done.15
  100.8 45.6 %blocks.1 = bf16[3,16,8192]{2,1,0:T(8,128)(2,1)} custom-call(s32[144]{0:T(256)S(1)} %reshape.80.nb, s32[3]{0:T(128)S(1)} %pad_add_fusion.pos, bf16[3,32,1024]{2,1,0:T(8,128)(2,1)S(1)} %copy-done.1, bf16[3,8,1024]{2,1,0:T(8,128)(2,1)S(1)} %collective-permute-done.above, bf16[3,8,1024]{2,1,0:T(8,128)(2,1)S(1)} %copy-done.8, ...), custom_call_target="tpu_custom_call" | custom-call | tf_op jit(solution)/shard_map/blocks/pallas_call | solution.py:558
  (25 shorter events, 0.2 us)
Async XLA Ops:
  0.0 26.2 %copy-start.17 = (s32[12,4,3]{0,1,2:T(4,128)S(1)}, s32[12,4,3]{0,1,2:T(4,128)}, u32[]{:S(2)}) copy-start(s32[12,4,3]{0,1,2:T(4,128)} %param.19) | copy-start | bytes 1732
  5.9 33.8 %all-to-all-start = ((bf16[16,48,256]{2,1,0:T(8,128)(2,1)}), bf16[16,48,256]{2,1,0:T(8,128)(2,1)S(1)}, u32[]{:S(2)}, u32[]{:S(2)}) async-start(bf16[16,48,256]{2,1,0:T(8,128)(2,1)} %select_select_fusion), calls=%async_computation | async-start | bytes 786432 | tf_op jit(solution)/shard_map/all_to_all | solution.py:508
  21.6 16.7 %collective-permute-start.4 = (bf16[64,256]{1,0:T(8,128)(2,1)S(1)}, bf16[64,256]{1,0:T(8,128)(2,1)S(1)}, u32[]{:S(2)}, u32[]{:S(2)}) collective-permute-start(bf16[64,256]{1,0:T(8,128)(2,1)S(1)} %pad.9.own), channel_id=1, source_target_pairs={{0,120},{120,0},{1,121},{121,1},{2,122},{122,2},{3,123},{123,3},{4... | collective-permute-start | bytes 98312 | tf_op jit(solution)/shard_map/ppermute | solution.py:509
  45.5 1.4 copy-start
  46.9 16.9 %copy-start.1 = (bf16[3,32,1024]{2,1,0:T(8,128)(2,1)S(1)}, bf16[3,32,1024]{2,1,0:T(8,128)(2,1)}, u32[]{:S(2)}) copy-start(bf16[3,32,1024]{2,1,0:T(8,128)(2,1)} %fields.1) | copy-start | bytes 589828
  46.9 19.5 %copy-start.16 = (bf16[16,128]{1,0:T(8,128)(2,1)S(1)}, bf16[16,128]{1,0:T(8,128)(2,1)}, u32[]{:S(2)}) copy-start(bf16[16,128]{1,0:T(8,128)(2,1)} %param.20) | copy-start | bytes 12292
  46.9 44.3 %all-to-all-start.1 = ((bf16[32,128,256]{2,1,0:T(8,128)(2,1)}), bf16[32,128,256]{2,1,0:T(8,128)(2,1)S(1)}, u32[]{:S(2)}, u32[]{:S(2)}) async-start(bf16[32,128,256]{2,1,0:T(8,128)(2,1)} %copy-done), calls=%async_computation.1 | async-start | bytes 4194304 | tf_op jit(solution)/shard_map/all_to_all | solution.py:529
  63.8 2.8 %collective-permute-start = (bf16[3,8,1024]{2,1,0:T(8,128)(2,1)S(1)}, bf16[3,8,1024]{2,1,0:T(8,128)(2,1)S(1)}, u32[]{:S(2)}, u32[]{:S(2)}) collective-permute-start(bf16[3,8,1024]{2,1,0:T(8,128)(2,1)S(1)} %get-tuple-element.10), channel_id=1, source_target_pairs={{0,8},{8,16},{16,24},{24,32},{32,40},{40,48},{48,56},{56,64},{64,7... | collective-permute-start | bytes 147464 | tf_op jit(solution)/shard_map/ppermute | solution.py:511
  65.1 5.1 %collective-permute-start.1 = (bf16[3,8,1024]{2,1,0:T(8,128)(2,1)S(1)}, bf16[3,8,1024]{2,1,0:T(8,128)(2,1)S(1)}, u32[]{:S(2)}, u32[]{:S(2)}) collective-permute-start(bf16[3,8,1024]{2,1,0:T(8,128)(2,1)S(1)} %get-tuple-element.9), channel_id=1, source_target_pairs={{8,0},{16,8},{24,16},{32,24},{40,32},{48,40},{56,48},{64,56},{72,6... | collective-permute-start | bytes 147464 | tf_op jit(solution)/shard_map/ppermute | solution.py:512
  66.4 24.7 %copy-start.5 = (bf16[128,512]{1,0:T(8,128)(2,1)S(1)}, bf16[128,512]{1,0:T(8,128)(2,1)}, u32[]{:S(2)}) copy-start(bf16[128,512]{1,0:T(8,128)(2,1)} %expand_first.1) | copy-start | bytes 393220
  70.2 7.2 %copy-start.7 = (bf16[3,8,1024]{2,1,0:T(8,128)(2,1)}, bf16[3,8,1024]{2,1,0:T(8,128)(2,1)S(1)}, u32[]{:S(2)}) copy-start(bf16[3,8,1024]{2,1,0:T(8,128)(2,1)S(1)} %collective-permute-done.1.below) | copy-start | bytes 147460
  70.9 18.9 %collective-permute-start.3 = (bf16[3,48,128]{2,1,0:T(8,128)(2,1)}, bf16[3,48,128]{2,1,0:T(8,128)(2,1)}, u32[]{:S(2)}, u32[]{:S(2)}) collective-permute-start(bf16[3,48,128]{2,1,0:T(8,128)(2,1)} %pad_maximum_fusion.1), channel_id=1, source_target_pairs={{1,0},{2,1},{3,2},{4,3},{5,4},{6,5},{7,6},{9,8},{10,9},{11,10},{12... | collective-permute-start | bytes 110600 | tf_op jit(solution)/shard_map/ppermute | solution.py:516
  72.8 17.0 %collective-permute-start.2 = (bf16[3,48,128]{2,1,0:T(8,128)(2,1)}, bf16[3,48,128]{2,1,0:T(8,128)(2,1)}, u32[]{:S(2)}, u32[]{:S(2)}) collective-permute-start(bf16[3,48,128]{2,1,0:T(8,128)(2,1)} %pad_maximum_fusion), channel_id=1, source_target_pairs={{0,1},{1,2},{2,3},{3,4},{4,5},{5,6},{6,7},{8,9},{9,10},{10,11},{11... | collective-permute-start | bytes 110600 | tf_op jit(solution)/shard_map/ppermute | solution.py:515
  91.2 1.0 copy-start.2
  92.1 1.0 copy-start.3
  93.2 1.0 copy-start.4
  94.2 0.9 copy-start.6
  95.1 0.8 copy-start.8
  95.9 0.8 copy-start.9
  96.8 0.7 copy-start.10
  97.5 0.7 copy-start.11
  98.1 0.7 copy-start.12
  98.8 0.7 copy-start.13
  99.5 0.7 copy-start.14
  100.2 0.7 copy-start.15

commit v2 on v0

v2 whole, which is shorter than its diff:
```python
import jax
import jax.numpy as jnp
from jax import lax
from jax.experimental import pallas as pl
from jax.experimental.pallas import tpu as pltpu
from jax.sharding import PartitionSpec as P

CIN = 16
C1 = 128
C2 = 256
HID1 = 512
HID2 = 1024
EPSILON = 1e-06
DEPTH = 5
F32 = jnp.float32
BF16 = jnp.bfloat16

ERF = (7.97827572e-01, 3.64699375e-02, -1.25479103e-04, -3.04667360e-05, 1.11260815e-06)


def gelu(x):
    x = x.astype(BF16)
    square = jnp.minimum(x * x, BF16(36.0))
    poly = BF16(ERF[4])
    for coefficient in ERF[3::-1]:
        poly = poly * square + BF16(coefficient)
    half = BF16(0.5) * x
    return half + half * jnp.tanh(x * poly)


def spots(shape, dim):
    return lax.broadcasted_iota(jnp.int32, shape, dim)


def one_hot(mask):
    return jnp.where(mask, 1.0, 0.0).astype(BF16)


def third(x):
    return (11 * x) >> 5


def dot(a, b):
    return jnp.dot(a, b, preferred_element_type=F32)


def route_kernel(nb, pos, recv, own, opp, target, chunks, strip, out, sem):
    g, r, c = pos[0], pos[1], pos[2]
    outer = jnp.logical_or(r == 0, r == 15)
    side = jnp.logical_or(c == 0, c == 7)
    out[...] = jnp.zeros_like(out)
    chunks[...] = jnp.zeros_like(chunks)

    @pl.when(outer)
    def _():
        mine = jnp.where(r == 0, 0, 1)
        chunks[mine, 8:72, :] = own[...].astype(F32)
        chunks[1 - mine, 8:72, :] = opp[...].astype(F32)

    @pl.when(jnp.logical_not(outer))
    def _():
        flip = 15 - r
        far = jnp.where(
            r >> 1 == c,
            r & 1,
            jnp.where(
                flip >> 1 == c,
                flip & 1,
                jnp.where(jnp.logical_or(r == 2 * c + 2, flip == 2 * c + 2), 1, 0),
            ),
        )
        start = pl.multiple_of(8 + 16 * far, 8)
        chunks[0, pl.ds(start, 48), :] = recv[0].astype(F32)
        chunks[1, pl.ds(start, 48), :] = recv[15].astype(F32)

    @pl.when(side)
    def _():
        strip[0:8, :] = jnp.zeros((8, 256), F32)
        strip[520:528, :] = jnp.zeros((8, 256), F32)
        for k in range(16):
            strip[8 + 32 * k : 40 + 32 * k, :] = recv[k, 0:32, :].astype(F32)

        @pl.when(jnp.logical_not(outer))
        def _():
            for k, row in ((0, 32), (15, 488)):
                block = recv[k].astype(F32)
                strip[row : row + 8, :] = jnp.where(c == 0, block[0:8], block[40:48])

    def place(data, source_face, dest_face):
        moved = pltpu.roll(data, (80 * (dest_face - source_face) + 256) & 255, 1)
        lane = spots(data.shape, 1) - 80 * dest_face
        inside = jnp.logical_and(lane >= 0, lane < 80)
        return jnp.where(inside, moved, 0.0).astype(BF16)

    def one_strip(k, carry):
        face, edge = k >> 2, k & 3
        base = ((3 * g + face) * 4 + edge) * 3
        other, dest_edge, turned = nb[base], nb[base + 1], nb[base + 2]
        dest_group = third(other)
        dest_face = other - 3 * dest_group
        dest_rows = dest_edge < 2
        to_rows = jnp.logical_and(
            outer, jnp.logical_and(dest_rows, dest_edge == jnp.where(r == 0, 0, 1))
        )
        to_cols = jnp.logical_not(dest_rows)
        block = dest_group * 8 + jnp.where(dest_edge == 2, 0, 7)

        @pl.when(edge < 2)
        def _():
            @pl.when(to_cols)
            def _():
                moved = place(chunks[edge], face, dest_face)
                q = 64 * c + spots((48, 80), 1) - 8
                p = jnp.where(turned == 1, 511 - q, q)
                pick = one_hot(p - 32 * r + 8 == spots((48, 80), 0))
                out[block, 80:128, :] += dot(pick, moved).astype(BF16)

            @pl.when(to_rows)
            def _():
                moved = place(chunks[edge], face, dest_face)
                q = 64 * c + spots((80, 80), 1) - 8
                p = jnp.where(turned == 1, 511 - q, q)
                middle = jnp.where(turned == 1, 7 - c, c)
                for shift in (-1, 0, 1):
                    target = middle + shift

                    @pl.when(jnp.logical_and(target >= 0, target < 8))
                    def _():
                        pick = one_hot(p - 64 * target + 8 == spots((80, 80), 0))
                        out[dest_group * 8 + target, 0:80, :] += dot(pick, moved).astype(BF16)

        @pl.when(jnp.logical_and(edge >= 2, c == jnp.where(edge == 2, 0, 7)))
        def _():
            @pl.when(to_cols)
            def _():
                start = pl.multiple_of(32 * jnp.where(turned == 1, 15 - r, r), 8)
                moved = place(strip[pl.ds(start, 48), :], face, dest_face)
                x = spots((48, 48), 1)
                pick = one_hot(jnp.where(turned == 1, 47 - x, x) == spots((48, 48), 0))
                out[block, 80:128, :] += dot(pick, moved).astype(BF16)

            @pl.when(to_rows)
            def _():
                x = spots((80, 80), 1)
                pick = one_hot(jnp.where(turned == 1, 79 - x, x) == spots((80, 80), 0))
                for target in range(8):
                    start = pl.multiple_of(
                        jnp.where(turned == 1, 448 - 64 * target, 64 * target), 8
                    )
                    moved = place(strip[pl.ds(start, 80), :], face, dest_face)
                    out[dest_group * 8 + target, 0:80, :] += dot(pick, moved).astype(BF16)

        return carry

    lax.fori_loop(0, 12, one_strip, 0)

    @pl.when(jnp.logical_and(outer, side))
    def _():
        def one_run(k, carry):
            face, kind = k >> 2, k & 3
            edge = jnp.where(kind < 2, kind, jnp.where(c == 0, 2, 3))
            end = jnp.where(kind < 2, jnp.where(c == 0, 0, 1), kind & 1)
            first = ((3 * g + face) * 4 + edge) * 3
            between, across = nb[first], nb[first + 1]
            far = jnp.where(nb[first + 2] == 1, 1 - end, end)
            second = (between * 4 + jnp.where(across < 2, 2 + far, far)) * 3
            dest, dest_edge = nb[second], nb[second + 1]
            near = across & 1
            near = jnp.where(nb[second + 2] == 1, 1 - near, near)
            dest_group = third(dest)
            slot = dest - 3 * dest_group + jnp.where(dest_edge < 2, 0, 3)
            dest_row = jnp.where(dest_edge < 2, dest_edge, near)
            dest_col = jnp.where(dest_edge < 2, near, dest_edge - 2)

            @pl.when(dest_row == jnp.where(r == 0, 0, 1))
            def _():
                at_chunk = pl.multiple_of(jnp.where(end == 1, 64, 8), 8)
                at_strip = pl.multiple_of(jnp.where(end == 1, 512, 8), 8)
                data = jnp.where(
                    edge < 2,
                    chunks[jnp.minimum(edge, 1), pl.ds(at_chunk, 8), :],
                    strip[pl.ds(at_strip, 8), :],
                )
                data = pltpu.roll(data, 240 - 80 * face, 1)[:, 128:256]
                data = jnp.where(spots((8, 128), 1) >= 112, data, 0.0)
                data = jnp.concatenate([data, jnp.zeros((8, 128), F32)], axis=0).astype(BF16)
                row = pl.multiple_of(16 * slot, 16)
                out[dest_group * 8 + 7 * dest_col, pl.ds(row, 16), 128:256] += data

            return carry

        lax.fori_loop(0, 12, one_run, 0)

    copy = pltpu.make_async_copy(out, target, sem)
    copy.start()
    copy.wait()


def normalise(mixed, gain):
    center = jnp.mean(mixed, axis=-1, keepdims=True)
    apart = mixed - center
    spread = jnp.mean(apart * apart, axis=-1, keepdims=True)
    return (apart * lax.rsqrt(spread + EPSILON) * gain).astype(BF16)


def rounded(x):
    return x.astype(BF16).astype(F32)


def fetch(sources, targets, sems):
    copies = [
        pltpu.make_async_copy(a, b, sems.at[k]) for k, (a, b) in enumerate(zip(sources, targets))
    ]
    for copy in copies:
        copy.start()
    return copies


def spread(index, above, fields, below, before, after, cells):
    cells[0] = before[index].astype(F32)
    cells[9] = after[index].astype(F32)
    for k in range(8):
        cells[1 + k, 0:8, :] = above[index, :, 128 * k : 128 * k + 128].astype(F32)
        cells[1 + k, 8:40, :] = fields[index, :, 128 * k : 128 * k + 128].astype(F32)
        cells[1 + k, 40:48, :] = below[index, :, 128 * k : 128 * k + 128].astype(F32)


def bulk_kernel(
    pos, fields, above, below, before, after, enc_cells,
    kernel_first, gain_first, expand_first, bias_first, contract_first, scale_first, down,
    kernel_second, gain_second, expand_second, bias_second, contract_second, scale_second,
    out, edge_rows, edge_cols,
    cells, grid, rows, pooled, coarse, *rest,
):
    r, c = pos[1], pos[2]
    sources = (
        kernel_first, gain_first, expand_first, bias_first, contract_first, scale_first, down,
        kernel_second, gain_second, expand_second, bias_second, contract_second, scale_second,
    )
    held, sems = rest[:-1], rest[-1]
    copies = fetch(sources, held, sems)
    (
        kernel_first, gain_first, expand_first, bias_first, contract_first, scale_first, down,
        kernel_second, gain_second, expand_second, bias_second, contract_second, scale_second,
    ) = held
    for copy in copies:
        copy.wait()

    def one_face(i, carry):
        spread(i, above, fields, below, before, after, cells)

        stacked = cells[...].reshape(480, 128).astype(BF16)
        for n in range(4):
            product = rounded(dot(stacked, enc_cells[:, 256 * n : 256 * n + 256]))
            for k in range(10):
                for j in range(2):
                    grid[8 * k + 2 * n + j] = product[48 * k : 48 * k + 48, 128 * j : 128 * j + 128]

        def one_chunk(k, carry):
            j0 = 4 + 8 * k
            total = jnp.zeros((8, 40, 128), F32)
            for a in range(3):
                for b in range(3):
                    window = grid[pl.ds(j0 + b - 1, 8), 3 + a : 43 + a, :]
                    total = total + window * kernel_first[3 * a + b : 3 * a + b + 1, :][None]
            normed = normalise(total.reshape(320, C1), gain_first[...])
            hidden = gelu(dot(normed, expand_first[...]) + bias_first[...]).astype(BF16)
            update = dot(hidden, contract_first[...])
            here = grid[pl.ds(j0, 8), 4:44, :].reshape(320, C1)
            rows[...] = rounded(here + scale_first[...] * update).reshape(8, 40, C1)
            paired = rows[:, pl.ds(0, 20, stride=2), :] + rows[:, pl.ds(1, 20, stride=2), :]
            paired = paired.reshape(4, 2, 20, C1)
            pooled[pl.ds(4 * k, 4), 0:20, :] = 0.25 * (paired[:, 0] + paired[:, 1])
            return carry

        lax.fori_loop(0, 9, one_chunk, 0, unroll=3)
        pooled[:, 20:24, :] = jnp.zeros((36, 4, C1), F32)
        product = dot(pooled[...].reshape(36 * 24, C1).astype(BF16), down[...])
        coarse[...] = rounded(product).reshape(36, 24, C2)

        @pl.when(r == 0)
        def _():
            edge_rows[i] = coarse[:, 0:8, :]

        @pl.when(r == 15)
        def _():
            edge_rows[i, :, 0:7, :] = coarse[:, 13:20, :]

        @pl.when(c == 0)
        def _():
            edge_cols[i] = coarse[0:7]

        @pl.when(c == 7)
        def _():
            edge_cols[i] = coarse[29:36]

        for part in range(2):
            total = jnp.zeros((16, 16, C2), F32)
            for a in range(3):
                for b in range(3):
                    window = coarse[16 * part + 2 * b : 16 * part + 2 * b + 16, 2 * a : 2 * a + 16, :]
                    total = total + window * kernel_second[3 * a + b : 3 * a + b + 1, :][None]
            normed = normalise(total.reshape(256, C2), gain_second[...])
            hidden = gelu(dot(normed, expand_second[...]) + bias_second[...]).astype(BF16)
            update = dot(hidden, contract_second[...])
            here = coarse[16 * part + 2 : 16 * part + 18, 2:18, :].reshape(256, C2)
            result = (here + scale_second[...] * update).astype(BF16).reshape(16, 16, C2)
            for j in range(16):
                column = (16 * part + j) * C2
                out[i, :, column : column + C2] = result[j]
        return carry

    lax.fori_loop(0, 3, one_face, 0)


def edge_kernel(
    nb, pos, bands, fields, above, below, before, after, first_out, edge_rows, edge_cols, enc_cells,
    kernel_first, gain_first, expand_first, bias_first, contract_first, scale_first, down,
    kernel_second, gain_second, expand_second, bias_second, contract_second, scale_second,
    out, *scratch,
):
    r, c = pos[1], pos[2]
    either = jnp.logical_or(
        jnp.logical_or(r == 0, r == 15), jnp.logical_or(c == 0, c == 7)
    )
    held, sems = scratch[-23:-1], scratch[-1]
    sources = (
        fields, above, below, before, after, enc_cells,
        kernel_first, gain_first, expand_first, bias_first, contract_first, scale_first, down,
        kernel_second, edge_rows, edge_cols, gain_second, expand_second, bias_second,
        contract_second, scale_second, first_out,
    )

    @pl.when(jnp.logical_not(either))
    def _():
        copy = pltpu.make_async_copy(first_out, held[21], sems.at[21])
        copy.start()
        copy.wait()

    @pl.when(either)
    def _():
        copies = fetch(sources, held, sems)
        patched(nb, pos, bands, held, copies, *scratch[:-23])

    out[...] = held[21][...]


def patched(
    nb, pos, bands, held, copies,
    cells, grid, side_grid, banded, taps, side_taps, mix, strip, rows, pooled, side_pooled,
    level, side_level, mixed, center, packed, patch,
):
    (
        fields, above, below, before, after, enc_cells,
        kernel_first, gain_first, expand_first, bias_first, contract_first, scale_first, down,
        kernel_second, edge_rows, edge_cols, gain_second, expand_second, bias_second,
        contract_second, scale_second, result,
    ) = held
    g, r, c = pos[0], pos[1], pos[2]
    top, bottom, left, right = r == 0, r == 15, c == 0, c == 7
    outer = jnp.logical_or(top, bottom)
    side = jnp.logical_or(left, right)
    corner = jnp.logical_and(outer, side)
    edge_row, edge_col = jnp.where(top, 0, 1), jnp.where(left, 2, 3)

    def add(k, total):
        return total + bands[k].astype(F32)

    total = lax.fori_loop(0, 32, add, jnp.zeros((128, 256), F32), unroll=4).astype(BF16)
    both = jnp.concatenate([total[:, 0:128], total[:, 128:256]], axis=0)
    for copy in copies[:16]:
        copy.wait()
    for k in range(4):
        product = rounded(dot(both, enc_cells[:, 256 * k : 256 * k + 256]))
        for j in range(2):
            banded[2 * k + j] = product[0:128, 128 * j : 128 * j + 128]
            banded[8 + 2 * k + j] = product[128:256, 128 * j : 128 * j + 128]

    def band_tap(face, edge, a, b):
        base = ((3 * g + face) * 4 + edge) * 3
        other_edge, turned = nb[base + 1], nb[base + 2]
        down_row, down_col = a - 1, b - 1
        deep = jnp.where(
            edge == 0,
            -down_row,
            jnp.where(edge == 1, down_row, jnp.where(edge == 2, -down_col, down_col)),
        )
        along = jnp.where(edge < 2, down_col, down_row)
        along = jnp.where(turned == 1, -along, along)
        inward = jnp.where((other_edge & 1) == 0, deep, -deep)
        tap_row = jnp.where(other_edge < 2, inward, along)
        tap_col = jnp.where(other_edge < 2, along, inward)
        return kernel_first[pl.ds((tap_row + 1) * 3 + tap_col + 1, 1), :]

    def run_end(face, edge, end):
        first = ((3 * g + face) * 4 + edge) * 3
        far = jnp.where(nb[first + 2] == 1, 1 - end, end)
        across = jnp.where(nb[first + 1] < 2, 2 + far, far)
        near = nb[first + 1] & 1
        return jnp.where(nb[(nb[first] * 4 + across) * 3 + 2] == 1, 1 - near, near)

    def block_first(total, here):
        normed = normalise(total, gain_first[...])
        hidden = gelu(dot(normed, expand_first[...]) + bias_first[...]).astype(BF16)
        return rounded(here + scale_first[...] * dot(hidden, contract_first[...]))

    for i in range(3):
        spread(i, above, fields, below, before, after, cells.at[i])

    @pl.when(outer)
    def _():
        low = pl.multiple_of(jnp.where(top, 0, 32), 8)
        data = cells[:, :, pl.ds(low, 16), :].reshape(480, 128).astype(BF16)
        for n in range(4):
            product = rounded(dot(data, enc_cells[:, 256 * n : 256 * n + 256]))
            for i in range(3):
                for k in range(10):
                    for j in range(2):
                        row = 160 * i + 16 * k
                        line = product[row : row + 16, 128 * j : 128 * j + 128]
                        grid[80 * i + 8 * k + 2 * n + j] = line
        flat = grid.reshape(3840, 128)
        for at, first, step in ((top, 7, -1), (bottom, 8, 1)):

            @pl.when(at)
            def _():
                for i in range(3):
                    for k in range(DEPTH):
                        line = banded[5 * i + k, 0:80, :]
                        flat[pl.ds(1280 * i + first + step * k, 80, stride=16), :] = line

        for a in range(3):
            for b in range(3):
                own = jnp.broadcast_to(kernel_first[3 * a + b : 3 * a + b + 1, :], (4, 128))
                for i in range(3):
                    line = jnp.broadcast_to(band_tap(i, edge_row, a, b), (4, 128))
                    taps[9 * i + 3 * a + b, 0:4, :] = jnp.where(top, line, own)
                    taps[9 * i + 3 * a + b, 4:8, :] = jnp.where(top, own, line)

        def one_chunk(k, carry):
            i = (k * 11) >> 5
            j0 = 80 * i + 4 + 24 * (k - 3 * i)
            total = jnp.zeros((24, 8, 128), F32)
            for a in range(3):
                for b in range(3):
                    window = grid[pl.ds(j0 + b - 1, 24), 3 + a : 11 + a, :]
                    total = total + window * taps[9 * i + 3 * a + b][None]
            here = grid[pl.ds(j0, 24), 4:12, :].reshape(192, C1)
            slot = lax.rem(k, 3)
            strip[slot] = block_first(total.reshape(192, C1), here).reshape(24, 8, C1)
            paired = strip[slot, :, pl.ds(0, 4, stride=2), :] + strip[slot, :, pl.ds(1, 4, stride=2), :]
            paired = paired.reshape(12, 2, 4, C1)
            pooled[pl.ds(12 * k, 12), 0:4, :] = 0.25 * (paired[:, 0] + paired[:, 1])
            return carry

        pooled[...] = jnp.zeros_like(pooled)
        lax.fori_loop(0, 9, one_chunk, 0, unroll=3)
        product = rounded(dot(pooled[...].reshape(864, C1).astype(BF16), down[...]))
        product = product.reshape(108, 8, C2)
        level[...] = edge_rows[...].reshape(108, 8, C2)

        @pl.when(top)
        def _():
            level[:, 0:4, :] = product[:, 0:4]

        @pl.when(bottom)
        def _():
            level[:, 3:7, :] = product[:, 0:4]

    @pl.when(side)
    def _():
        group = jnp.where(left, 0, 8)
        data = cells[:, pl.ds(group, 2)].reshape(288, 128).astype(BF16)
        for n in range(4):
            product = rounded(dot(data, enc_cells[:, 256 * n : 256 * n + 256]))
            for i in range(3):
                for k in range(2):
                    for j in range(2):
                        row = 96 * i + 48 * k
                        line = product[row : row + 48, 128 * j : 128 * j + 128]
                        side_grid[16 * i + 8 * k + 2 * n + j] = line
        for i in range(3):
            for k in range(DEPTH):
                j = jnp.where(left, 7 - k, 8 + k)
                side_grid[16 * i + j] = banded[5 * i + k, 80:128, :]

        flat = side_grid.reshape(2304, 128)
        near = pl.multiple_of(jnp.where(left, 0, 64), 8)
        for at, first, step in ((top, 7, -1), (bottom, 40, 1)):

            @pl.when(at)
            def _():
                for i in range(3):
                    for k in range(DEPTH):
                        line = banded[5 * i + k, pl.ds(near, 16), :]
                        flat[pl.ds(768 * i + first + step * k, 16, stride=48), :] = line

        inner = jnp.where(left, 1, 0)
        for a in range(3):
            for b in range(3):
                own = jnp.broadcast_to(kernel_first[3 * a + b : 3 * a + b + 1, :], (40, 128))
                for i in range(3):
                    line = jnp.broadcast_to(band_tap(i, edge_col, a, b), (40, 128))
                    side_taps[i, inner, 3 * a + b] = own
                    side_taps[i, 1 - inner, 3 * a + b] = line

        for at, row in ((top, 0), (bottom, 36)):

            @pl.when(at)
            def _():
                for a in range(3):
                    for b in range(3):
                        for i in range(3):
                            line = jnp.broadcast_to(band_tap(i, edge_row, a, b), (4, 128))
                            side_taps[i, inner, 3 * a + b, row : row + 4, :] = line

        for i in range(3):
            for half in range(2):
                total = jnp.zeros((4, 40, 128), F32)
                for a in range(3):
                    for b in range(3):
                        j = 16 * i + 3 + 4 * half + b
                        window = side_grid[j : j + 4, 3 + a : 43 + a, :]
                        total = total + window * side_taps[i, half, 3 * a + b][None]
                mix[i, 4 * half : 4 * half + 4] = total

        @pl.when(corner)
        def _():
            out_a, out_b = jnp.where(top, 0, 2), jnp.where(left, 0, 2)
            row_in, row_out = jnp.where(top, 8, 39), jnp.where(top, 7, 40)
            col_in, col_out = jnp.where(left, 8, 7), jnp.where(left, 7, 8)
            step_row, step_col = jnp.where(top, -1, 1), jnp.where(left, -1, 1)
            for i in range(3):
                row_end = run_end(i, edge_row, jnp.where(left, 0, 1))
                col_end = run_end(i, edge_col, jnp.where(top, 0, 1))
                row_lines = [-side_grid[16 * i + col_out, pl.ds(row_in, 1), :]] + [
                    banded[15, pl.ds(16 * i + jnp.where(row_end == 1, 7 - d, d), 1), :]
                    for d in range(DEPTH)
                ]
                col_lines = [-side_grid[16 * i + col_in, pl.ds(row_out, 1), :]] + [
                    banded[15, pl.ds(48 + 16 * i + jnp.where(col_end == 1, 7 - d, d), 1), :]
                    for d in range(DEPTH)
                ]
                row_taps = [band_tap(i, edge_row, 1 + s * step_row, out_b) for s in (-1, 0, 1)]
                col_taps = [band_tap(i, edge_col, out_a, 1 + s * step_col) for s in (-1, 0, 1)]
                for depth in range(4):
                    extra = sum(row_taps[s] * row_lines[depth + s] for s in range(3))
                    at = (i, col_in - 4, pl.ds(row_out + depth * step_row - 4, 1))
                    mix[at[0], at[1], at[2], :] += extra
                    extra = sum(col_taps[s] * col_lines[depth + s] for s in range(3))
                    at = (i, col_out + depth * step_col - 4, pl.ds(row_in - 4, 1))
                    mix[at[0], at[1], at[2], :] += extra

        side_pooled[...] = jnp.zeros_like(side_pooled)
        for i in range(3):
            here = side_grid[16 * i + 4 : 16 * i + 12, 4:44, :].reshape(320, C1)
            rows[i] = block_first(mix[i].reshape(320, C1), here).reshape(8, 40, C1)
            paired = rows[i, :, pl.ds(0, 20, stride=2), :] + rows[i, :, pl.ds(1, 20, stride=2), :]
            paired = paired.reshape(4, 2, 20, C1)
            side_pooled[4 * i : 4 * i + 4, 0:20, :] = 0.25 * (paired[:, 0] + paired[:, 1])
        product = rounded(dot(side_pooled[...].reshape(288, C1).astype(BF16), down[...]))
        product = product.reshape(12, 24, C2)
        side_level[...] = edge_cols[...].reshape(21, 24, C2)
        first = jnp.where(left, 0, 29)

        @pl.when(top)
        def _():
            for i in range(3):
                for k in range(7):
                    side_level[7 * i + k, 0:4, :] = level[36 * i + first + k, 0:4, :]

        @pl.when(bottom)
        def _():
            for i in range(3):
                for k in range(7):
                    side_level[7 * i + k, 16:20, :] = level[36 * i + first + k, 3:7, :]

        shift = jnp.where(left, 0, 3)
        dead = jnp.where(left, 0, 5)
        for i in range(3):
            for k in range(4):
                side_level[7 * i + shift + k] = product[4 * i + k]

        for at, row, low in ((top, 0, 0), (bottom, 18, 13)):

            @pl.when(at)
            def _():
                for i in range(3):
                    for k in range(2):
                        side_level[7 * i + dead + k, row : row + 2, :] = jnp.zeros((2, C2), F32)
                    for k in range(7):
                        line = side_level[7 * i + k, low : low + 7, :]
                        level[36 * i + first + k, 0:7, :] = line

    mixed[...] = jnp.zeros_like(mixed)
    center[...] = jnp.zeros_like(center)

    @pl.when(outer)
    def _():
        for i in range(3):
            total = jnp.zeros((32, 3, C2), F32)
            for a in range(3):
                for b in range(3):
                    first = 36 * i + 2 * b
                    window = level[first : first + 32, 2 * a : 2 * a + 3, :]
                    total = total + window * kernel_second[3 * a + b : 3 * a + b + 1, :][None]
            here = level[36 * i + 2 : 36 * i + 34, 2:5, :]
            for j in range(32):
                row = 96 * i + 3 * j
                mixed[row : row + 3, :] = total[j]
                center[row : row + 3, :] = here[j]

    @pl.when(side)
    def _():
        for i in range(3):
            total = jnp.zeros((3, 16, C2), F32)
            for a in range(3):
                for b in range(3):
                    first = 7 * i + 2 * b
                    window = side_level[first : first + 3, 2 * a : 2 * a + 16, :]
                    total = total + window * kernel_second[3 * a + b : 3 * a + b + 1, :][None]
            row = 288 + 48 * i
            mixed[row : row + 48, :] = total.reshape(48, C2)
            center[row : row + 48, :] = side_level[7 * i + 2 : 7 * i + 5, 2:18, :].reshape(48, C2)

    for copy in copies[16:]:
        copy.wait()
    normed = normalise(mixed[...], gain_second[...])
    hidden = gelu(dot(normed, expand_second[...]) + bias_second[...]).astype(BF16)
    center[...] = center[...] + scale_second[...] * dot(hidden, contract_second[...])

    for at, row in ((top, 0), (bottom, 13)):

        @pl.when(at)
        def _():
            for i in range(3):
                patch[...] = result[i].astype(F32)
                for j in range(32):
                    line = center[96 * i + 3 * j : 96 * i + 3 * j + 3, :]
                    patch[row : row + 3, C2 * j : C2 * j + C2] = line
                result[i] = patch[...].astype(BF16)

    for at, col in ((left, 0), (right, 29)):

        @pl.when(at)
        def _():
            for i in range(3):
                for j in range(3):
                    row = 288 + 48 * i + 16 * j
                    lane = C2 * (col + j)
                    result[i, :, lane : lane + C2] = center[row : row + 16, :].astype(BF16)


SMEM = pl.BlockSpec(memory_space=pltpu.SMEM)
WHOLE = pl.BlockSpec(memory_space=pltpu.VMEM)
FAR = pl.BlockSpec(memory_space=pltpu.HBM)

LIMIT = 56 * 2**20


def held_copies(weights):
    held = [pltpu.VMEM(w.shape, w.dtype) for w in weights]
    return held + [pltpu.SemaphoreType.DMA((len(weights),))]


def route(links, pos, recv, lines, opposite):
    return pl.pallas_call(
        route_kernel,
        out_shape=jax.ShapeDtypeStruct((32, 128, 256), BF16),
        in_specs=[SMEM, SMEM, WHOLE, WHOLE, WHOLE],
        out_specs=FAR,
        scratch_shapes=[
            pltpu.VMEM((2, 80, 256), F32),
            pltpu.VMEM((528, 256), F32),
            pltpu.VMEM((32, 128, 256), BF16),
            pltpu.SemaphoreType.DMA,
        ],
        compiler_params=pltpu.CompilerParams(vmem_limit_bytes=LIMIT),
        name="route",
    )(links, pos, recv, lines, opposite)


def bulk(pos, halos, enc_cells, weights):
    return pl.pallas_call(
        bulk_kernel,
        out_shape=(
            jax.ShapeDtypeStruct((3, 16, 32 * C2), BF16),
            jax.ShapeDtypeStruct((3, 36, 8, C2), F32),
            jax.ShapeDtypeStruct((3, 7, 24, C2), F32),
        ),
        in_specs=[SMEM] + [WHOLE] * 6 + [FAR] * len(weights),
        out_specs=(WHOLE, WHOLE, WHOLE),
        scratch_shapes=[
            pltpu.VMEM((10, 48, 128), F32),
            pltpu.VMEM((80, 48, 128), F32),
            pltpu.VMEM((8, 40, 128), F32),
            pltpu.VMEM((36, 24, 128), F32),
            pltpu.VMEM((36, 24, 256), F32),
        ]
        + held_copies(weights),
        compiler_params=pltpu.CompilerParams(vmem_limit_bytes=LIMIT),
        cost_estimate=pl.CostEstimate(
            flops=5 * 10**9, bytes_accessed=4 * 10**6, transcendentals=6 * 10**6
        ),
        name="bulk",
    )(pos, *halos, enc_cells, *weights)


def edges(links, pos, halos, bands, first_out, edge_rows, edge_cols, enc_cells, weights):
    sources = (*halos, enc_cells, *weights[:8], edge_rows, edge_cols, *weights[8:], first_out)
    operands = (*halos, first_out, edge_rows, edge_cols, enc_cells, *weights)
    return pl.pallas_call(
        edge_kernel,
        out_shape=jax.ShapeDtypeStruct((3, 16, 32 * C2), BF16),
        in_specs=[SMEM, SMEM, WHOLE] + [FAR] * len(operands),
        out_specs=WHOLE,
        scratch_shapes=[
            pltpu.VMEM((3, 10, 48, 128), F32),
            pltpu.VMEM((240, 16, 128), F32),
            pltpu.VMEM((48, 48, 128), F32),
            pltpu.VMEM((16, 128, 128), F32),
            pltpu.VMEM((27, 8, 128), F32),
            pltpu.VMEM((3, 2, 9, 40, 128), F32),
            pltpu.VMEM((3, 8, 40, 128), F32),
            pltpu.VMEM((3, 24, 8, 128), F32),
            pltpu.VMEM((3, 8, 40, 128), F32),
            pltpu.VMEM((108, 8, 128), F32),
            pltpu.VMEM((12, 24, 128), F32),
            pltpu.VMEM((108, 8, 256), F32),
            pltpu.VMEM((21, 24, 256), F32),
            pltpu.VMEM((432, 256), F32),
            pltpu.VMEM((432, 256), F32),
            pltpu.VMEM((8, 128), F32),
            pltpu.VMEM((16, 32 * C2), F32),
        ]
        + held_copies(sources),
        compiler_params=pltpu.CompilerParams(vmem_limit_bytes=LIMIT),
        name="edges",
    )(links, pos, bands, *operands)


def as_lines(rows):
    lines = rows.reshape(3, DEPTH, 64, CIN).transpose(2, 0, 1, 3).reshape(64, 240)
    return jnp.pad(lines, ((0, 0), (0, 16)))


def per_device(
    fields,
    neighbours,
    w_enc,
    depthwise_kernel_first,
    norm_gain_first,
    expand_weight_first,
    expand_bias_first,
    contract_weight_first,
    layer_scale_first,
    w_down,
    depthwise_kernel_second,
    norm_gain_second,
    expand_weight_second,
    expand_bias_second,
    contract_weight_second,
    layer_scale_second,
):
    r, c = lax.axis_index("row"), lax.axis_index("col")
    pos = jnp.stack([lax.axis_index("face"), r, c]).astype(jnp.int32)
    links = neighbours.reshape(144)

    lines = jnp.where(r == 15, jnp.flip(fields[:, 27:], axis=1), fields[:, :5])
    lines = as_lines(lines)
    sides = jnp.where(
        c == 7,
        jnp.flip(fields[:, :, 59 * CIN :].reshape(3, 32, 5, CIN), axis=2),
        fields[:, :, : 5 * CIN].reshape(3, 32, 5, CIN),
    )
    sides = sides.transpose(1, 0, 2, 3).reshape(32, 240)
    sides = jnp.pad(sides, ((0, 16), (0, 16)))
    outer = jnp.logical_or(r == 0, r == 15)
    nearest = jnp.where(r == 0, sides[24:32], sides[0:8])
    upper = jnp.concatenate([jnp.where(c == 0, nearest, lines[16:24]), lines[24:]], axis=0)
    lower = jnp.concatenate([lines[:40], jnp.where(c == 7, nearest, lines[40:48])], axis=0)
    dest = lax.broadcasted_iota(jnp.int32, (16, 48, 256), 0)
    far = jnp.where(
        dest >> 1 == c,
        dest & 1,
        jnp.where(
            (15 - dest) >> 1 == c,
            (15 - dest) & 1,
            jnp.where((dest == 2 * c + 2) | (15 - dest == 2 * c + 2), 1, 0),
        ),
    )
    use_lines = jnp.logical_and(outer, (dest > 0) & (dest < 15))
    send = jnp.where(use_lines, jnp.where(far == 1, upper[None], lower[None]), sides[None])
    above = lax.ppermute(fields[:, 24:], "row", [(k, (k + 1) % 16) for k in range(16)])
    below = lax.ppermute(fields[:, :8], "row", [((k + 1) % 16, k) for k in range(16)])
    send, above, below = lax.optimization_barrier((send, above, below))
    recv = lax.all_to_all(send, "row", 0, 0)

    opposite = as_lines(jnp.where(r == 0, jnp.flip(above[:, 3:], axis=1), below[:, :5]))
    first = jnp.concatenate([above[:, :, :128], fields[:, :, :128], below[:, :, :128]], axis=1)
    last = jnp.concatenate([above[:, :, 896:], fields[:, :, 896:], below[:, :, 896:]], axis=1)
    before = lax.ppermute(last, "col", [(k, k + 1) for k in range(7)])
    after = lax.ppermute(first, "col", [(k + 1, k) for k in range(7)])

    recv, before, after = lax.optimization_barrier((recv, before, after))

    routed = route(links, pos, recv, lines, opposite)
    bands = lax.all_to_all(routed, ("face", "col"), 0, 0)

    enc_cells = jnp.kron(jnp.eye(8, dtype=BF16), w_enc)
    weights = (
        depthwise_kernel_first.reshape(9, C1),
        norm_gain_first.reshape(1, C1),
        expand_weight_first,
        expand_bias_first.reshape(1, HID1),
        contract_weight_first,
        layer_scale_first.reshape(1, C1),
        w_down,
        depthwise_kernel_second.reshape(9, C2),
        norm_gain_second.reshape(1, C2),
        expand_weight_second,
        expand_bias_second.reshape(1, HID2),
        contract_weight_second,
        layer_scale_second.reshape(1, C2),
    )
    halos = (fields, above, below, before, after)
    first_out, edge_rows, edge_cols = bulk(pos, halos, enc_cells, weights)
    return edges(links, pos, halos, bands, first_out, edge_rows, edge_cols, enc_cells, weights)


def solution(mesh):
    return jax.shard_map(
        per_device,
        mesh=mesh,
        in_specs=(P("face", "row", "col"),) + (P(),) * 15,
        out_specs=P("face", "row", "col"),
        check_vma=False,
    )
```

time: 850 us -> 106 us (0.12)
  the two profiles are of different devices: /device:TPU:6 before, /device:TPU:1 now
where the time goes in v2:
time: 106 us
  Pallas kernels  43 us (41%)
  starting transfers between devices  38.5 us (36%)
  local copies, waits for them, and re-layouts  11.2 us (11%)
  waiting for transfers between devices  9.95 us (9%)
  other arithmetic  2.6 us (2%)
    pallas_call x1, Pallas kernels, bulk(): pl.pallas_call(bulk_kernel, out_shape=(jax.ShapeDtypeStruct((3, 16, 32 *...  23.4 us
    pallas_call x1, Pallas kernels, edges(): pl.pallas_call(edge_kernel, out_shape=jax.ShapeDtypeStruct((3, 16, 32 * C...  14.3 us
    all_to_all x1, starting transfers between devices, per_device(): bands = lax.all_to_all(routed, ('face', 'col'), 0, 0)  13 us
    ppermute x1, starting transfers between devices, per_device(): lax.ppermute(fields[:, :8], 'row', [((k + 1) % 16, k) for k in range(16)])  11.9 us
    all_to_all x1, starting transfers between devices, per_device(): recv = lax.all_to_all(send, 'row', 0, 0)  7.17 us
    all_to_all x1, waiting for transfers between devices, per_device(): recv = lax.all_to_all(send, 'row', 0, 0)  5.8 us
    pallas_call x1, Pallas kernels, route(): pl.pallas_call(route_kernel, out_shape=jax.ShapeDtypeStruct((32, 128, 256...  5.33 us
    unnamed x24, local copies, waits for them, and re-layouts  3.19 us
  transfers between devices with their start and end apart: 6, of which 3 were waited for; matrix products, arithmetic and copies ran while one was open for 10% of the time, Pallas kernels for 22%

profile of v2, /device:TPU:1, one launch (start us, length us, event | category | flops | bytes accessed | tf_op | source)
XLA Modules:
  0.0 105.6 jit_solution(11790792813543963966)
XLA Ops:
  0.0 0.0 copy-start.8
  0.0 0.8 fusion.5
  0.8 11.9 %collective-permute-start.1 = (bf16[3,8,1024]{2,1,0:T(8,128)(2,1)S(1)}, bf16[3,8,1024]{2,1,0:T(8,128)(2,1)S(1)}, u32[]{:S(2)}, u32[]{:S(2)}) collective-permute-start(bf16[3,8,1024]{2,1,0:T(8,128)(2,1)S(1)} %get-tuple-element.25), channel_id=1, source_target_pairs={{8,0},{16,8},{24,16},{32,24},{40,32},{48,40},{56,48},{64,56},{72,6... | collective-permute-start | bytes 147464 | tf_op jit(solution)/shard_map/ppermute | solution.py:795
  12.8 1.9 %collective-permute-start = (bf16[3,8,1024]{2,1,0:T(8,128)(2,1)S(1)}, bf16[3,8,1024]{2,1,0:T(8,128)(2,1)S(1)}, u32[]{:S(2)}, u32[]{:S(2)}) collective-permute-start(bf16[3,8,1024]{2,1,0:T(8,128)(2,1)S(1)} %get-tuple-element.26), channel_id=1, source_target_pairs={{0,8},{8,16},{16,24},{24,32},{32,40},{40,48},{48,56},{56,64},{64,7... | collective-permute-start | bytes 147464 | tf_op jit(solution)/shard_map/ppermute | solution.py:794
  14.7 0.8 slice.64
  15.6 0.8 fusion.6
  16.5 0.3 rev.12
  16.7 0.8 slice_select_fusion.1
  17.6 0.1 copy.31
  17.7 0.1 copy.32
  17.8 0.1 copy.24
  17.9 0.2 reshape.69
  18.1 0.1 copy.26
  18.3 0.1 copy.27
  18.4 0.9 fusion.1
  19.4 0.0 collective-permute-done.1.below
  19.4 0.0 copy-start.3
  19.4 0.0 collective-permute-done.above
  19.4 0.0 copy-start.2
  19.4 7.2 %all-to-all-start = ((bf16[16,48,256]{2,1,0:T(8,128)(2,1)}), bf16[16,48,256]{2,1,0:T(8,128)(2,1)S(1)}, u32[]{:S(2)}, u32[]{:S(2)}) async-start(bf16[16,48,256]{2,1,0:T(8,128)(2,1)} %fusion.1), calls=%async_computation | async-start | bytes 786432 | tf_op jit(solution)/shard_map/all_to_all | solution.py:797
  26.6 0.6 pad.12.own
  27.2 0.0 copy-done.8
  27.2 0.1 copy.21
  27.3 0.7 reshape.65.nb
  28.0 0.7 pad_add_fusion.pos
  28.7 0.8 fusion.4
  29.5 3.1 %collective-permute-start.2 = (bf16[3,48,128]{2,1,0:T(8,128)(2,1)S(1)}, bf16[3,48,128]{2,1,0:T(8,128)(2,1)S(1)}, u32[]{:S(2)}, u32[]{:S(2)}) collective-permute-start(bf16[3,48,128]{2,1,0:T(8,128)(2,1)S(1)} %pad_maximum_fusion), channel_id=1, source_target_pairs={{0,1},{1,2},{2,3},{3,4},{4,5},{5,6},{6,7},{8,9},{9,10},{10,11},{11... | collective-permute-start | bytes 110600 | tf_op jit(solution)/shard_map/ppermute | solution.py:802
  32.6 1.3 %collective-permute-start.3 = (bf16[3,48,128]{2,1,0:T(8,128)(2,1)S(1)}, bf16[3,48,128]{2,1,0:T(8,128)(2,1)S(1)}, u32[]{:S(2)}, u32[]{:S(2)}) collective-permute-start(bf16[3,48,128]{2,1,0:T(8,128)(2,1)S(1)} %pad_maximum_fusion.1), channel_id=1, source_target_pairs={{1,0},{2,1},{3,2},{4,3},{5,4},{6,5},{7,6},{9,8},{10,9},{11,10},{12... | collective-permute-start | bytes 110600 | tf_op jit(solution)/shard_map/ppermute | solution.py:803
  33.9 0.3 rev.13
  34.3 0.2 reshape.71
  34.5 0.1 copy.29
  34.6 0.1 copy.30
  34.7 0.6 pad.13.opp
  35.3 0.0 collective-permute-done.2.before
  35.3 0.0 copy-start.4
  35.3 2.2 %collective-permute-done.3.after = bf16[3,48,128]{2,1,0:T(8,128)(2,1)S(1)} collective-permute-done((bf16[3,48,128]{2,1,0:T(8,128)(2,1)S(1)}, bf16[3,48,128]{2,1,0:T(8,128)(2,1)S(1)}, u32[]{:S(2)}, u32[]{:S(2)}) %collective-permute-start.3) | collective-permute-done | bytes 36896 | tf_op jit(solution)/shard_map/ppermute | solution.py:803
  37.6 0.0 copy-start.5
  37.6 5.8 %all-to-all-done.recv = bf16[16,48,256]{2,1,0:T(8,128)(2,1)S(1)} async-done(((bf16[16,48,256]{2,1,0:T(8,128)(2,1)}), bf16[16,48,256]{2,1,0:T(8,128)(2,1)S(1)}, u32[]{:S(2)}, u32[]{:S(2)}) %all-to-all-start) | async-done | bytes 393248 | tf_op jit(solution)/shard_map/all_to_all | solution.py:797
  43.4 0.0 copy-start.1
  43.4 0.7 copy-done.1
  44.1 5.3 %route.1 = bf16[32,128,256]{2,1,0:T(8,128)(2,1)} custom-call(s32[144]{0:T(256)} %reshape.65.nb, s32[3]{0:T(128)} %pad_add_fusion.pos, bf16[16,48,256]{2,1,0:T(8,128)(2,1)} %copy-done.1, bf16[64,256]{1,0:T(8,128)(2,1)} %pad.12.own, bf16[64,256]{1,0:T(8,128)(2,1)} %pad.13.opp), custom_call_target="tpu_custom_call" | custom-call | tf_op jit(solution)/shard_map/route/pallas_call | solution.py:667
  49.5 0.0 copy-done.3
  49.5 0.0 copy-done.2
  49.5 0.0 copy-start.7
  49.5 0.0 copy-start.6
  49.5 0.0 copy-start.9
  49.5 13.0 %all-to-all-start.1 = ((bf16[32,128,256]{2,1,0:T(8,128)(2,1)}), bf16[32,128,256]{2,1,0:T(8,128)(2,1)S(1)}, u32[]{:S(2)}, u32[]{:S(2)}) async-start(bf16[32,128,256]{2,1,0:T(8,128)(2,1)} %route.1), calls=%async_computation.1 | async-start | bytes 4194304 | tf_op jit(solution)/shard_map/all_to_all | solution.py:808
  62.6 0.0 copy-done.7
  62.6 0.6 reshape.73.kernel_first
  63.2 0.0 copy-done.6
  63.2 0.6 reshape.77.kernel_second
  63.8 0.0 copy-done.9
  63.8 0.1 broadcast_multiply_fusion
  63.9 0.7 copy.35
  64.6 0.0 copy-done.4
  64.7 0.0 copy-done.5
  64.7 23.4 %bulk.1 = (bf16[3,16,8192]{2,1,0:T(8,128)(2,1)}, f32[3,36,8,256]{3,2,1,0:T(8,128)}, f32[3,7,24,256]{3,2,1,0:T(8,128)}) custom-call(s32[3]{0:T(128)} %pad_add_fusion.pos, bf16[3,32,1024]{2,1,0:T(8,128)(2,1)} %fields.3, bf16[3,8,1024]{2,1,0:T(8,128)(2,1)} %copy-done.2, bf16[3,8,1024]{2,1,0:T(8,128)(2,1)} %copy-done.3, bf16[3,48,128]{2,1,0:T(8,128)(2,1)} %copy-done.4, ...), custom_call_target="tpu_custom_call" | custom-call | flops 5000000000 | bytes 4000000 | tf_op jit(solution)/shard_map/bulk/pallas_call | solution.py:684
  88.1 1.9 %all-to-all-done.1.bands = bf16[32,128,256]{2,1,0:T(8,128)(2,1)S(1)} async-done(((bf16[32,128,256]{2,1,0:T(8,128)(2,1)}), bf16[32,128,256]{2,1,0:T(8,128)(2,1)S(1)}, u32[]{:S(2)}, u32[]{:S(2)}) %all-to-all-start.1) | async-done | bytes 2097184 | tf_op jit(solution)/shard_map/all_to_all | solution.py:808
  90.0 0.0 copy-start
  90.0 1.3 %copy-done = bf16[32,128,256]{2,1,0:T(8,128)(2,1)} copy-done((bf16[32,128,256]{2,1,0:T(8,128)(2,1)}, bf16[32,128,256]{2,1,0:T(8,128)(2,1)S(1)}, u32[]{:S(2)}) %copy-start) | copy-done | bytes 2097176
  91.3 14.3 %edges.1 = bf16[3,16,8192]{2,1,0:T(8,128)(2,1)} custom-call(s32[144]{0:T(256)} %reshape.65.nb, s32[3]{0:T(128)} %pad_add_fusion.pos, bf16[32,128,256]{2,1,0:T(8,128)(2,1)} %copy-done, bf16[3,32,1024]{2,1,0:T(8,128)(2,1)} %fields.3, bf16[3,8,1024]{2,1,0:T(8,128)(2,1)} %copy-done.2, bf16[3,8,1024]{2,1,0:T(8,128)(2,1)} %copy-done.3, ...), custom_call_target="tpu_custom_call" | custom-call | tf_op jit(solution)/shard_map/edges/pallas_call | solution.py:712
  (18 shorter events, 0.2 us)
Async XLA Ops:
  0.0 27.2 %copy-start.8 = (s32[12,4,3]{0,1,2:T(4,128)S(1)}, s32[12,4,3]{0,1,2:T(4,128)}, u32[]{:S(2)}) copy-start(s32[12,4,3]{0,1,2:T(4,128)} %param.17) | copy-start | bytes 1732
  0.8 18.5 %collective-permute-start.1 = (bf16[3,8,1024]{2,1,0:T(8,128)(2,1)S(1)}, bf16[3,8,1024]{2,1,0:T(8,128)(2,1)S(1)}, u32[]{:S(2)}, u32[]{:S(2)}) collective-permute-start(bf16[3,8,1024]{2,1,0:T(8,128)(2,1)S(1)} %get-tuple-element.25), channel_id=1, source_target_pairs={{8,0},{16,8},{24,16},{32,24},{40,32},{48,40},{56,48},{64,56},{72,6... | collective-permute-start | bytes 147464 | tf_op jit(solution)/shard_map/ppermute | solution.py:795
  12.8 6.6 %collective-permute-start = (bf16[3,8,1024]{2,1,0:T(8,128)(2,1)S(1)}, bf16[3,8,1024]{2,1,0:T(8,128)(2,1)S(1)}, u32[]{:S(2)}, u32[]{:S(2)}) collective-permute-start(bf16[3,8,1024]{2,1,0:T(8,128)(2,1)S(1)} %get-tuple-element.26), channel_id=1, source_target_pairs={{0,8},{8,16},{16,24},{24,32},{32,40},{40,48},{48,56},{56,64},{64,7... | collective-permute-start | bytes 147464 | tf_op jit(solution)/shard_map/ppermute | solution.py:794
  19.4 30.1 %copy-start.3 = (bf16[3,8,1024]{2,1,0:T(8,128)(2,1)}, bf16[3,8,1024]{2,1,0:T(8,128)(2,1)S(1)}, u32[]{:S(2)}) copy-start(bf16[3,8,1024]{2,1,0:T(8,128)(2,1)S(1)} %collective-permute-done.1.below) | copy-start | bytes 147460
  19.4 30.1 %copy-start.2 = (bf16[3,8,1024]{2,1,0:T(8,128)(2,1)}, bf16[3,8,1024]{2,1,0:T(8,128)(2,1)S(1)}, u32[]{:S(2)}) copy-start(bf16[3,8,1024]{2,1,0:T(8,128)(2,1)S(1)} %collective-permute-done.above) | copy-start | bytes 147460
  19.4 24.0 %all-to-all-start = ((bf16[16,48,256]{2,1,0:T(8,128)(2,1)}), bf16[16,48,256]{2,1,0:T(8,128)(2,1)S(1)}, u32[]{:S(2)}, u32[]{:S(2)}) async-start(bf16[16,48,256]{2,1,0:T(8,128)(2,1)} %fusion.1), calls=%async_computation | async-start | bytes 786432 | tf_op jit(solution)/shard_map/all_to_all | solution.py:797
  29.5 5.8 %collective-permute-start.2 = (bf16[3,48,128]{2,1,0:T(8,128)(2,1)S(1)}, bf16[3,48,128]{2,1,0:T(8,128)(2,1)S(1)}, u32[]{:S(2)}, u32[]{:S(2)}) collective-permute-start(bf16[3,48,128]{2,1,0:T(8,128)(2,1)S(1)} %pad_maximum_fusion), channel_id=1, source_target_pairs={{0,1},{1,2},{2,3},{3,4},{4,5},{5,6},{6,7},{8,9},{9,10},{10,11},{11... | collective-permute-start | bytes 110600 | tf_op jit(solution)/shard_map/ppermute | solution.py:802
  32.6 4.9 %collective-permute-start.3 = (bf16[3,48,128]{2,1,0:T(8,128)(2,1)S(1)}, bf16[3,48,128]{2,1,0:T(8,128)(2,1)S(1)}, u32[]{:S(2)}, u32[]{:S(2)}) collective-permute-start(bf16[3,48,128]{2,1,0:T(8,128)(2,1)S(1)} %pad_maximum_fusion.1), channel_id=1, source_target_pairs={{1,0},{2,1},{3,2},{4,3},{5,4},{6,5},{7,6},{9,8},{10,9},{11,10},{12... | collective-permute-start | bytes 110600 | tf_op jit(solution)/shard_map/ppermute | solution.py:803
  35.3 29.3 %copy-start.4 = (bf16[3,48,128]{2,1,0:T(8,128)(2,1)}, bf16[3,48,128]{2,1,0:T(8,128)(2,1)S(1)}, u32[]{:S(2)}) copy-start(bf16[3,48,128]{2,1,0:T(8,128)(2,1)S(1)} %collective-permute-done.2.before) | copy-start | bytes 110596
  37.6 27.1 %copy-start.5 = (bf16[3,48,128]{2,1,0:T(8,128)(2,1)}, bf16[3,48,128]{2,1,0:T(8,128)(2,1)S(1)}, u32[]{:S(2)}) copy-start(bf16[3,48,128]{2,1,0:T(8,128)(2,1)S(1)} %collective-permute-done.3.after) | copy-start | bytes 110596
  43.4 0.7 copy-start.1
  49.5 13.1 %copy-start.7 = (f32[3,3,128]{2,1,0:T(4,128)S(1)}, f32[3,3,128]{2,1,0:T(4,128)}, u32[]{:S(2)}) copy-start(f32[3,3,128]{2,1,0:T(4,128)} %param.19) | copy-start | bytes 13828
  49.5 13.7 %copy-start.6 = (f32[3,3,256]{2,1,0:T(4,128)S(1)}, f32[3,3,256]{2,1,0:T(4,128)}, u32[]{:S(2)}) copy-start(f32[3,3,256]{2,1,0:T(4,128)} %param.26) | copy-start | bytes 27652
  49.5 14.3 %copy-start.9 = (bf16[16,128]{1,0:T(8,128)(2,1)S(1)}, bf16[16,128]{1,0:T(8,128)(2,1)}, u32[]{:S(2)}) copy-start(bf16[16,128]{1,0:T(8,128)(2,1)} %param.18) | copy-start | bytes 12292
  49.5 40.5 %all-to-all-start.1 = ((bf16[32,128,256]{2,1,0:T(8,128)(2,1)}), bf16[32,128,256]{2,1,0:T(8,128)(2,1)S(1)}, u32[]{:S(2)}, u32[]{:S(2)}) async-start(bf16[32,128,256]{2,1,0:T(8,128)(2,1)} %route.1), calls=%async_computation.1 | async-start | bytes 4194304 | tf_op jit(solution)/shard_map/all_to_all | solution.py:808
  90.0 1.3 %copy-start = (bf16[32,128,256]{2,1,0:T(8,128)(2,1)}, bf16[32,128,256]{2,1,0:T(8,128)(2,1)S(1)}, u32[]{:S(2)}) copy-start(bf16[32,128,256]{2,1,0:T(8,128)(2,1)S(1)} %all-to-all-done.1.bands) | copy-start | bytes 6291460

commit v3 on v2

--- a/solution.py
+++ b/solution.py
@@ -15,14 +15,14 @@
 F32 = jnp.float32
 BF16 = jnp.bfloat16
 
-ERF = (7.97827572e-01, 3.64699375e-02, -1.25479103e-04, -3.04667360e-05, 1.11260815e-06)
+ERF = (7.97507541e-01, 3.70060348e-02, -3.51598854e-04)
 
 
 def gelu(x):
     x = x.astype(BF16)
     square = jnp.minimum(x * x, BF16(36.0))
-    poly = BF16(ERF[4])
-    for coefficient in ERF[3::-1]:
+    poly = BF16(ERF[-1])
+    for coefficient in ERF[-2::-1]:
         poly = poly * square + BF16(coefficient)
     half = BF16(0.5) * x
     return half + half * jnp.tanh(x * poly)
@@ -42,6 +42,55 @@
 
 def dot(a, b):
     return jnp.dot(a, b, preferred_element_type=F32)
+
+
+def strip_kernel(pos, fields, send, lines):
+    r, c = pos[1], pos[2]
+    lane = spots((1024, 256), 1) & 15
+    spread_out = one_hot((spots((1024, 256), 0) & 15) == lane)
+    own_cell = (spots((64, 1024), 1) >> 4) == spots((64, 1024), 0)
+    parts = []
+    for i in range(3):
+        near, far = fields[i, 0:16, :].astype(F32), fields[i, 16:32, :].astype(F32)
+        for d in range(DEPTH):
+            line = jnp.where(r == 15, far[15 - d : 16 - d], near[d : d + 1])
+            parts.append(jnp.where(own_cell, line, 0.0).astype(BF16))
+    product = dot(jnp.concatenate(parts, axis=0), spread_out)
+    place = spots((64, 256), 1) >> 4
+    along = jnp.zeros((64, 256), F32)
+    for k in range(15):
+        along = jnp.where(place == k, product[64 * k : 64 * k + 64], along)
+    down = jnp.zeros((32, 256), F32)
+    a, b = spots((128, 256), 0), spots((128, 256), 1)
+    for i in range(3):
+        data = jnp.where(c == 7, fields[i, :, 896:1024].astype(F32), fields[i, :, 0:128].astype(F32))
+        depth = (b >> 4) - 5 * i
+        depth = jnp.where(jnp.logical_and(depth >= 0, depth < DEPTH), depth, 99)
+        cell = jnp.where(c == 7, 7 - depth, depth)
+        pick = jnp.logical_and((a >> 4) == cell, (a & 15) == (b & 15))
+        down = down + dot(data.astype(BF16), one_hot(pick))
+    lines[...] = along.astype(BF16)
+    nearest = jnp.where(r == 0, down[24:32], down[0:8])
+    upper = jnp.concatenate([jnp.where(c == 0, nearest, along[16:24]), along[24:]], axis=0)
+    lower = jnp.concatenate([along[:40], jnp.where(c == 7, nearest, along[40:48])], axis=0)
+    upper, lower = upper.astype(BF16), lower.astype(BF16)
+    wide = jnp.concatenate([down, jnp.zeros((16, 256), F32)], axis=0).astype(BF16)
+    outer = jnp.logical_or(r == 0, r == 15)
+    for k in range(16):
+        flip = 15 - k
+        far = jnp.where(
+            c == k >> 1,
+            k & 1,
+            jnp.where(
+                c == flip >> 1,
+                flip & 1,
+                jnp.where(jnp.logical_or(2 * c + 2 == k, 2 * c + 2 == flip), 1, 0),
+            ),
+        )
+        if 0 < k < 15:
+            send[k] = jnp.where(outer, jnp.where(far == 1, upper, lower), wide)
+        else:
+            send[k] = wide
 
 
 def route_kernel(nb, pos, recv, own, opp, target, chunks, strip, out, sem):
@@ -104,6 +153,8 @@
         )
         to_cols = jnp.logical_not(dest_rows)
         block = dest_group * 8 + jnp.where(dest_edge == 2, 0, 7)
+        lower = jnp.where(r == 15, 5, 0)
+        line = spots((48, 80), 0) - lower
 
         @pl.when(edge < 2)
         def _():
@@ -112,8 +163,8 @@
                 moved = place(chunks[edge], face, dest_face)
                 q = 64 * c + spots((48, 80), 1) - 8
                 p = jnp.where(turned == 1, 511 - q, q)
-                pick = one_hot(p - 32 * r + 8 == spots((48, 80), 0))
-                out[block, 80:128, :] += dot(pick, moved).astype(BF16)
+                pick = one_hot(jnp.logical_and(p - 32 * r + 8 == line, line >= 3))
+                out[block, 64:112, :] += dot(pick, moved).astype(BF16)
 
             @pl.when(to_rows)
             def _():
@@ -126,7 +177,10 @@
 
                     @pl.when(jnp.logical_and(target >= 0, target < 8))
                     def _():
-                        pick = one_hot(p - 64 * target + 8 == spots((80, 80), 0))
+                        lead = jnp.where(target == 0, 0, 8)
+                        seen = p - 64 * target + lead
+                        kept = seen < jnp.where(target == 0, 72, 80)
+                        pick = one_hot(jnp.logical_and(kept, seen == spots((80, 80), 0)))
                         out[dest_group * 8 + target, 0:80, :] += dot(pick, moved).astype(BF16)
 
         @pl.when(jnp.logical_and(edge >= 2, c == jnp.where(edge == 2, 0, 7)))
@@ -136,8 +190,9 @@
                 start = pl.multiple_of(32 * jnp.where(turned == 1, 15 - r, r), 8)
                 moved = place(strip[pl.ds(start, 48), :], face, dest_face)
                 x = spots((48, 48), 1)
-                pick = one_hot(jnp.where(turned == 1, 47 - x, x) == spots((48, 48), 0))
-                out[block, 80:128, :] += dot(pick, moved).astype(BF16)
+                line = spots((48, 48), 0) - lower
+                pick = one_hot(jnp.logical_and(jnp.where(turned == 1, 47 - x, x) == line, line >= 3))
+                out[block, 64:112, :] += dot(pick, moved).astype(BF16)
 
             @pl.when(to_rows)
             def _():
@@ -148,7 +203,10 @@
                         jnp.where(turned == 1, 448 - 64 * target, 64 * target), 8
                     )
                     moved = place(strip[pl.ds(start, 80), :], face, dest_face)
-                    out[dest_group * 8 + target, 0:80, :] += dot(pick, moved).astype(BF16)
+                    chosen = dot(pick, moved)
+                    if target == 0:
+                        chosen = jnp.concatenate([chosen[8:], jnp.zeros((8, 256), F32)], axis=0)
+                    out[dest_group * 8 + target, 0:80, :] += chosen.astype(BF16)
 
         return carry
 
@@ -217,12 +275,13 @@
 
 
 def spread(index, above, fields, below, before, after, cells):
-    cells[0] = before[index].astype(F32)
-    cells[9] = after[index].astype(F32)
+    cells[0, 8:40, :] = before[index].astype(F32)
+    cells[9, 8:40, :] = after[index].astype(F32)
     for k in range(8):
-        cells[1 + k, 0:8, :] = above[index, :, 128 * k : 128 * k + 128].astype(F32)
         cells[1 + k, 8:40, :] = fields[index, :, 128 * k : 128 * k + 128].astype(F32)
-        cells[1 + k, 40:48, :] = below[index, :, 128 * k : 128 * k + 128].astype(F32)
+    for k in range(10):
+        cells[k, 0:8, :] = above[index, :, 128 * k : 128 * k + 128].astype(F32)
+        cells[k, 40:48, :] = below[index, :, 128 * k : 128 * k + 128].astype(F32)
 
 
 def bulk_kernel(
@@ -230,34 +289,42 @@
     kernel_first, gain_first, expand_first, bias_first, contract_first, scale_first, down,
     kernel_second, gain_second, expand_second, bias_second, contract_second, scale_second,
     out, edge_rows, edge_cols,
-    cells, grid, rows, pooled, coarse, *rest,
+    cells, grid, rows, pooled, coarse, result, *rest,
 ):
     r, c = pos[1], pos[2]
     sources = (
+        fields, above, below, before, after, enc_cells,
         kernel_first, gain_first, expand_first, bias_first, contract_first, scale_first, down,
         kernel_second, gain_second, expand_second, bias_second, contract_second, scale_second,
     )
-    held, sems = rest[:-1], rest[-1]
+    held, sems, leave = rest[:-2], rest[-2], rest[-1]
     copies = fetch(sources, held, sems)
     (
+        fields, above, below, before, after, enc_cells,
         kernel_first, gain_first, expand_first, bias_first, contract_first, scale_first, down,
         kernel_second, gain_second, expand_second, bias_second, contract_second, scale_second,
     ) = held
-    for copy in copies:
+    for copy in copies[:6]:
         copy.wait()
 
-    def one_face(i, carry):
+    def encode(i, carry):
         spread(i, above, fields, below, before, after, cells)
-
         stacked = cells[...].reshape(480, 128).astype(BF16)
         for n in range(4):
             product = rounded(dot(stacked, enc_cells[:, 256 * n : 256 * n + 256]))
             for k in range(10):
                 for j in range(2):
-                    grid[8 * k + 2 * n + j] = product[48 * k : 48 * k + 48, 128 * j : 128 * j + 128]
-
+                    line = product[48 * k : 48 * k + 48, 128 * j : 128 * j + 128]
+                    grid[80 * i + 8 * k + 2 * n + j] = line
+        return carry
+
+    lax.fori_loop(0, 3, encode, 0)
+    for copy in copies[6:13]:
+        copy.wait()
+
+    def one_face(i, carry):
         def one_chunk(k, carry):
-            j0 = 4 + 8 * k
+            j0 = 80 * i + 4 + 8 * k
             total = jnp.zeros((8, 40, 128), F32)
             for a in range(3):
                 for b in range(3):
@@ -273,44 +340,56 @@
             pooled[pl.ds(4 * k, 4), 0:20, :] = 0.25 * (paired[:, 0] + paired[:, 1])
             return carry
 
-        lax.fori_loop(0, 9, one_chunk, 0, unroll=3)
+        lax.fori_loop(0, 9, one_chunk, 0, unroll=9)
         pooled[:, 20:24, :] = jnp.zeros((36, 4, C1), F32)
         product = dot(pooled[...].reshape(36 * 24, C1).astype(BF16), down[...])
-        coarse[...] = rounded(product).reshape(36, 24, C2)
-
-        @pl.when(r == 0)
-        def _():
-            edge_rows[i] = coarse[:, 0:8, :]
-
-        @pl.when(r == 15)
-        def _():
-            edge_rows[i, :, 0:7, :] = coarse[:, 13:20, :]
-
-        @pl.when(c == 0)
-        def _():
-            edge_cols[i] = coarse[0:7]
-
-        @pl.when(c == 7)
-        def _():
-            edge_cols[i] = coarse[29:36]
-
-        for part in range(2):
-            total = jnp.zeros((16, 16, C2), F32)
-            for a in range(3):
-                for b in range(3):
-                    window = coarse[16 * part + 2 * b : 16 * part + 2 * b + 16, 2 * a : 2 * a + 16, :]
-                    total = total + window * kernel_second[3 * a + b : 3 * a + b + 1, :][None]
-            normed = normalise(total.reshape(256, C2), gain_second[...])
-            hidden = gelu(dot(normed, expand_second[...]) + bias_second[...]).astype(BF16)
-            update = dot(hidden, contract_second[...])
-            here = coarse[16 * part + 2 : 16 * part + 18, 2:18, :].reshape(256, C2)
-            result = (here + scale_second[...] * update).astype(BF16).reshape(16, 16, C2)
-            for j in range(16):
-                column = (16 * part + j) * C2
-                out[i, :, column : column + C2] = result[j]
+        coarse[i] = rounded(product).reshape(36, 24, C2)
         return carry
 
     lax.fori_loop(0, 3, one_face, 0)
+    for copy in copies[13:]:
+        copy.wait()
+
+    def at_edges(act):
+        for index, (at, source, target) in enumerate(
+            (
+                (r == 0, coarse.at[:, :, 0:8], edge_rows),
+                (r == 15, coarse.at[:, :, 12:20], edge_rows),
+                (c == 0, coarse.at[:, 0:7], edge_cols),
+                (c == 7, coarse.at[:, 29:36], edge_cols),
+            )
+        ):
+
+            @pl.when(at)
+            def _():
+                act(pltpu.make_async_copy(source, target, leave.at[3 + index]))
+
+    at_edges(lambda copy: copy.start())
+
+    def one_part(k, carry):
+        i, part = k >> 1, k & 1
+        first = 16 * part
+        total = jnp.zeros((16, 16, C2), F32)
+        for a in range(3):
+            for b in range(3):
+                window = coarse[i, pl.ds(first + 2 * b, 16), 2 * a : 2 * a + 16, :]
+                total = total + window * kernel_second[3 * a + b : 3 * a + b + 1, :][None]
+        normed = normalise(total.reshape(256, C2), gain_second[...])
+        hidden = gelu(dot(normed, expand_second[...]) + bias_second[...]).astype(BF16)
+        update = dot(hidden, contract_second[...])
+        here = coarse[i, pl.ds(first + 2, 16), 2:18, :].reshape(256, C2)
+        made = (here + scale_second[...] * update).astype(BF16).reshape(16, 16, C2)
+        for j in range(16):
+            lane = pl.multiple_of((first + j) * C2, C2)
+            result[i, :, pl.ds(lane, C2)] = made[j]
+        return carry
+
+    for i in range(3):
+        lax.fori_loop(2 * i, 2 * i + 2, one_part, 0, unroll=2)
+        pltpu.make_async_copy(result.at[i], out.at[i], leave.at[i]).start()
+    for i in range(3):
+        pltpu.make_async_copy(result.at[i], out.at[i], leave.at[i]).wait()
+    at_edges(lambda copy: copy.wait())
 
 
 def edge_kernel(
@@ -323,35 +402,27 @@
     either = jnp.logical_or(
         jnp.logical_or(r == 0, r == 15), jnp.logical_or(c == 0, c == 7)
     )
-    held, sems = scratch[-23:-1], scratch[-1]
+    held, sems = scratch[-24:-1], scratch[-1]
     sources = (
-        fields, above, below, before, after, enc_cells,
+        bands, enc_cells, fields, above, below, before, after,
         kernel_first, gain_first, expand_first, bias_first, contract_first, scale_first, down,
         kernel_second, edge_rows, edge_cols, gain_second, expand_second, bias_second,
         contract_second, scale_second, first_out,
     )
 
-    @pl.when(jnp.logical_not(either))
-    def _():
-        copy = pltpu.make_async_copy(first_out, held[21], sems.at[21])
-        copy.start()
-        copy.wait()
-
     @pl.when(either)
     def _():
         copies = fetch(sources, held, sems)
-        patched(nb, pos, bands, held, copies, *scratch[:-23])
-
-    out[...] = held[21][...]
+        patched(nb, pos, held, copies, out, sems, *scratch[:-24])
 
 
 def patched(
-    nb, pos, bands, held, copies,
+    nb, pos, held, copies, out, sems,
     cells, grid, side_grid, banded, taps, side_taps, mix, strip, rows, pooled, side_pooled,
     level, side_level, mixed, center, packed, patch,
 ):
     (
-        fields, above, below, before, after, enc_cells,
+        bands, enc_cells, fields, above, below, before, after,
         kernel_first, gain_first, expand_first, bias_first, contract_first, scale_first, down,
         kernel_second, edge_rows, edge_cols, gain_second, expand_second, bias_second,
         contract_second, scale_second, result,
@@ -364,17 +435,31 @@
     edge_row, edge_col = jnp.where(top, 0, 1), jnp.where(left, 2, 3)
 
     def add(k, total):
-        return total + bands[k].astype(F32)
-
-    total = lax.fori_loop(0, 32, add, jnp.zeros((128, 256), F32), unroll=4).astype(BF16)
+        return total + bands[k]
+
+    copies[0].wait()
+    total = lax.fori_loop(0, 32, add, jnp.zeros((112, 256), BF16), unroll=8)
     both = jnp.concatenate([total[:, 0:128], total[:, 128:256]], axis=0)
-    for copy in copies[:16]:
-        copy.wait()
+    copies[1].wait()
     for k in range(4):
         product = rounded(dot(both, enc_cells[:, 256 * k : 256 * k + 256]))
         for j in range(2):
-            banded[2 * k + j] = product[0:128, 128 * j : 128 * j + 128]
-            banded[8 + 2 * k + j] = product[128:256, 128 * j : 128 * j + 128]
+            banded[2 * k + j, 0:112, :] = product[0:112, 128 * j : 128 * j + 128]
+            banded[8 + 2 * k + j, 0:112, :] = product[112:224, 128 * j : 128 * j + 128]
+    banded[:, 112:120, :] = jnp.zeros((16, 8, 128), F32)
+    none = jnp.zeros((8, 128), F32)
+
+    def row_band(k):
+        body = banded[k, 0:80, :]
+        shifted = jnp.concatenate([none, body[0:72]], axis=0)
+        return jnp.where(left, shifted, jnp.concatenate([body[0:72], jnp.where(right, none, body[72:80])], axis=0))
+
+    def row_band_end(k):
+        at_left = jnp.concatenate([none, banded[k, 0:8, :]], axis=0)
+        return jnp.where(left, at_left, jnp.concatenate([banded[k, 64:72, :], none], axis=0))
+
+    def col_band(k):
+        return jnp.where(bottom, banded[k, 69:117, :], banded[k, 64:112, :])
 
     def band_tap(face, edge, a, b):
         base = ((3 * g + face) * 4 + edge) * 3
@@ -404,6 +489,8 @@
         hidden = gelu(dot(normed, expand_first[...]) + bias_first[...]).astype(BF16)
         return rounded(here + scale_first[...] * dot(hidden, contract_first[...]))
 
+    for copy in copies[2:14]:
+        copy.wait()
     for i in range(3):
         spread(i, above, fields, below, before, after, cells.at[i])
 
@@ -426,7 +513,7 @@
             def _():
                 for i in range(3):
                     for k in range(DEPTH):
-                        line = banded[5 * i + k, 0:80, :]
+                        line = row_band(5 * i + k)
                         flat[pl.ds(1280 * i + first + step * k, 80, stride=16), :] = line
 
         for a in range(3):
@@ -454,10 +541,16 @@
             return carry
 
         pooled[...] = jnp.zeros_like(pooled)
-        lax.fori_loop(0, 9, one_chunk, 0, unroll=3)
+        lax.fori_loop(0, 9, one_chunk, 0, unroll=9)
+    for copy in copies[14:17]:
+        copy.wait()
+
+    @pl.when(outer)
+    def _():
         product = rounded(dot(pooled[...].reshape(864, C1).astype(BF16), down[...]))
         product = product.reshape(108, 8, C2)
-        level[...] = edge_rows[...].reshape(108, 8, C2)
+        whole = edge_rows[...].reshape(108, 8, C2)
+        level[...] = jnp.where(top, whole, jnp.concatenate([whole[:, 1:], whole[:, :1]], axis=1))
 
         @pl.when(top)
         def _():
@@ -482,17 +575,16 @@
         for i in range(3):
             for k in range(DEPTH):
                 j = jnp.where(left, 7 - k, 8 + k)
-                side_grid[16 * i + j] = banded[5 * i + k, 80:128, :]
+                side_grid[16 * i + j] = col_band(5 * i + k)
 
         flat = side_grid.reshape(2304, 128)
-        near = pl.multiple_of(jnp.where(left, 0, 64), 8)
         for at, first, step in ((top, 7, -1), (bottom, 40, 1)):
 
             @pl.when(at)
             def _():
                 for i in range(3):
                     for k in range(DEPTH):
-                        line = banded[5 * i + k, pl.ds(near, 16), :]
+                        line = row_band_end(5 * i + k)
                         flat[pl.ds(768 * i + first + step * k, 16, stride=48), :] = line
 
         inner = jnp.where(left, 1, 0)
@@ -623,33 +715,36 @@
             mixed[row : row + 48, :] = total.reshape(48, C2)
             center[row : row + 48, :] = side_level[7 * i + 2 : 7 * i + 5, 2:18, :].reshape(48, C2)
 
-    for copy in copies[16:]:
+    for copy in copies[17:]:
         copy.wait()
     normed = normalise(mixed[...], gain_second[...])
     hidden = gelu(dot(normed, expand_second[...]) + bias_second[...]).astype(BF16)
     center[...] = center[...] + scale_second[...] * dot(hidden, contract_second[...])
 
-    for at, row in ((top, 0), (bottom, 13)):
-
-        @pl.when(at)
-        def _():
-            for i in range(3):
+    for i in range(3):
+        for at, row in ((top, 0), (bottom, 13)):
+
+            @pl.when(at)
+            def _():
                 patch[...] = result[i].astype(F32)
                 for j in range(32):
                     line = center[96 * i + 3 * j : 96 * i + 3 * j + 3, :]
                     patch[row : row + 3, C2 * j : C2 * j + C2] = line
                 result[i] = patch[...].astype(BF16)
 
-    for at, col in ((left, 0), (right, 29)):
-
-        @pl.when(at)
-        def _():
-            for i in range(3):
+        for at, col in ((left, 0), (right, 29)):
+
+            @pl.when(at)
+            def _():
                 for j in range(3):
                     row = 288 + 48 * i + 16 * j
                     lane = C2 * (col + j)
                     result[i, :, lane : lane + C2] = center[row : row + 16, :].astype(BF16)
 
+        pltpu.make_async_copy(result.at[i], out.at[i], sems.at[i]).start()
+    for i in range(3):
+        pltpu.make_async_copy(result.at[i], out.at[i], sems.at[i]).wait()
+
 
 SMEM = pl.BlockSpec(memory_space=pltpu.SMEM)
 WHOLE = pl.BlockSpec(memory_space=pltpu.VMEM)
@@ -663,24 +758,42 @@
     return held + [pltpu.SemaphoreType.DMA((len(weights),))]
 
 
+def strips(pos, fields):
+    return pl.pallas_call(
+        strip_kernel,
+        out_shape=(
+            jax.ShapeDtypeStruct((16, 48, 256), BF16),
+            jax.ShapeDtypeStruct((64, 256), BF16),
+        ),
+        in_specs=[SMEM, WHOLE],
+        out_specs=(WHOLE, WHOLE),
+        compiler_params=pltpu.CompilerParams(vmem_limit_bytes=24 * 2**20),
+        name="strips",
+    )(pos, fields)
+
+
 def route(links, pos, recv, lines, opposite):
     return pl.pallas_call(
         route_kernel,
-        out_shape=jax.ShapeDtypeStruct((32, 128, 256), BF16),
+        out_shape=jax.ShapeDtypeStruct((32, 112, 256), BF16),
         in_specs=[SMEM, SMEM, WHOLE, WHOLE, WHOLE],
         out_specs=FAR,
         scratch_shapes=[
             pltpu.VMEM((2, 80, 256), F32),
             pltpu.VMEM((528, 256), F32),
-            pltpu.VMEM((32, 128, 256), BF16),
+            pltpu.VMEM((32, 112, 256), BF16),
             pltpu.SemaphoreType.DMA,
         ],
-        compiler_params=pltpu.CompilerParams(vmem_limit_bytes=LIMIT),
+        compiler_params=pltpu.CompilerParams(vmem_limit_bytes=16 * 2**20),
+        cost_estimate=pl.CostEstimate(
+            flops=10**9, bytes_accessed=4 * 10**6, transcendentals=0
+        ),
         name="route",
     )(links, pos, recv, lines, opposite)
 
 
 def bulk(pos, halos, enc_cells, weights):
+    operands = (*halos, enc_cells, *weights)
     return pl.pallas_call(
         bulk_kernel,
         out_shape=(
@@ -688,37 +801,40 @@
             jax.ShapeDtypeStruct((3, 36, 8, C2), F32),
             jax.ShapeDtypeStruct((3, 7, 24, C2), F32),
         ),
-        in_specs=[SMEM] + [WHOLE] * 6 + [FAR] * len(weights),
-        out_specs=(WHOLE, WHOLE, WHOLE),
+        in_specs=[SMEM] + [FAR] * len(operands),
+        out_specs=(FAR, FAR, FAR),
         scratch_shapes=[
             pltpu.VMEM((10, 48, 128), F32),
-            pltpu.VMEM((80, 48, 128), F32),
+            pltpu.VMEM((240, 48, 128), F32),
             pltpu.VMEM((8, 40, 128), F32),
             pltpu.VMEM((36, 24, 128), F32),
-            pltpu.VMEM((36, 24, 256), F32),
+            pltpu.VMEM((3, 36, 24, 256), F32),
+            pltpu.VMEM((3, 16, 32 * C2), BF16),
         ]
-        + held_copies(weights),
+        + held_copies(operands)
+        + [pltpu.SemaphoreType.DMA((7,))],
         compiler_params=pltpu.CompilerParams(vmem_limit_bytes=LIMIT),
         cost_estimate=pl.CostEstimate(
             flops=5 * 10**9, bytes_accessed=4 * 10**6, transcendentals=6 * 10**6
         ),
         name="bulk",
-    )(pos, *halos, enc_cells, *weights)
+    )(pos, *operands)
 
 
 def edges(links, pos, halos, bands, first_out, edge_rows, edge_cols, enc_cells, weights):
-    sources = (*halos, enc_cells, *weights[:8], edge_rows, edge_cols, *weights[8:], first_out)
-    operands = (*halos, first_out, edge_rows, edge_cols, enc_cells, *weights)
+    sources = (bands, enc_cells, *halos, *weights[:8], edge_rows, edge_cols, *weights[8:], first_out)
+    operands = (bands, *halos, first_out, edge_rows, edge_cols, enc_cells, *weights)
     return pl.pallas_call(
         edge_kernel,
         out_shape=jax.ShapeDtypeStruct((3, 16, 32 * C2), BF16),
-        in_specs=[SMEM, SMEM, WHOLE] + [FAR] * len(operands),
-        out_specs=WHOLE,
+        in_specs=[SMEM, SMEM] + [FAR] * len(operands),
+        out_specs=FAR,
+        input_output_aliases={2 + len(halos) + 1: 0},
         scratch_shapes=[
             pltpu.VMEM((3, 10, 48, 128), F32),
             pltpu.VMEM((240, 16, 128), F32),
             pltpu.VMEM((48, 48, 128), F32),
-            pltpu.VMEM((16, 128, 128), F32),
+            pltpu.VMEM((16, 120, 128), F32),
             pltpu.VMEM((27, 8, 128), F32),
             pltpu.VMEM((3, 2, 9, 40, 128), F32),
             pltpu.VMEM((3, 8, 40, 128), F32),
@@ -736,12 +852,7 @@
         + held_copies(sources),
         compiler_params=pltpu.CompilerParams(vmem_limit_bytes=LIMIT),
         name="edges",
-    )(links, pos, bands, *operands)
-
-
-def as_lines(rows):
-    lines = rows.reshape(3, DEPTH, 64, CIN).transpose(2, 0, 1, 3).reshape(64, 240)
-    return jnp.pad(lines, ((0, 0), (0, 16)))
+    )(links, pos, *operands)
 
 
 def per_device(
@@ -766,45 +877,18 @@
     pos = jnp.stack([lax.axis_index("face"), r, c]).astype(jnp.int32)
     links = neighbours.reshape(144)
 
-    lines = jnp.where(r == 15, jnp.flip(fields[:, 27:], axis=1), fields[:, :5])
-    lines = as_lines(lines)
-    sides = jnp.where(
-        c == 7,
-        jnp.flip(fields[:, :, 59 * CIN :].reshape(3, 32, 5, CIN), axis=2),
-        fields[:, :, : 5 * CIN].reshape(3, 32, 5, CIN),
-    )
-    sides = sides.transpose(1, 0, 2, 3).reshape(32, 240)
-    sides = jnp.pad(sides, ((0, 16), (0, 16)))
-    outer = jnp.logical_or(r == 0, r == 15)
-    nearest = jnp.where(r == 0, sides[24:32], sides[0:8])
-    upper = jnp.concatenate([jnp.where(c == 0, nearest, lines[16:24]), lines[24:]], axis=0)
-    lower = jnp.concatenate([lines[:40], jnp.where(c == 7, nearest, lines[40:48])], axis=0)
-    dest = lax.broadcasted_iota(jnp.int32, (16, 48, 256), 0)
-    far = jnp.where(
-        dest >> 1 == c,
-        dest & 1,
-        jnp.where(
-            (15 - dest) >> 1 == c,
-            (15 - dest) & 1,
-            jnp.where((dest == 2 * c + 2) | (15 - dest == 2 * c + 2), 1, 0),
-        ),
-    )
-    use_lines = jnp.logical_and(outer, (dest > 0) & (dest < 15))
-    send = jnp.where(use_lines, jnp.where(far == 1, upper[None], lower[None]), sides[None])
-    above = lax.ppermute(fields[:, 24:], "row", [(k, (k + 1) % 16) for k in range(16)])
-    below = lax.ppermute(fields[:, :8], "row", [((k + 1) % 16, k) for k in range(16)])
-    send, above, below = lax.optimization_barrier((send, above, below))
+    send, lines = strips(pos, fields)
     recv = lax.all_to_all(send, "row", 0, 0)
-
-    opposite = as_lines(jnp.where(r == 0, jnp.flip(above[:, 3:], axis=1), below[:, :5]))
-    first = jnp.concatenate([above[:, :, :128], fields[:, :, :128], below[:, :, :128]], axis=1)
-    last = jnp.concatenate([above[:, :, 896:], fields[:, :, 896:], below[:, :, 896:]], axis=1)
-    before = lax.ppermute(last, "col", [(k, k + 1) for k in range(7)])
-    after = lax.ppermute(first, "col", [(k + 1, k) for k in range(7)])
-
-    recv, before, after = lax.optimization_barrier((recv, before, after))
+    opposite = lax.ppermute(lines, "row", [(0, 15), (15, 0)])
+
+    before = lax.ppermute(fields[:, :, 896:], "col", [(k, k + 1) for k in range(7)])
+    after = lax.ppermute(fields[:, :, :128], "col", [(k + 1, k) for k in range(7)])
+    wide = jnp.concatenate([before, fields, after], axis=2)
+    above = lax.ppermute(wide[:, 24:], "row", [(k, k + 1) for k in range(15)])
+    below = lax.ppermute(wide[:, :8], "row", [(k + 1, k) for k in range(15)])
 
     routed = route(links, pos, recv, lines, opposite)
+    routed, above, below = lax.optimization_barrier((routed, above, below))
     bands = lax.all_to_all(routed, ("face", "col"), 0, 0)
 
     enc_cells = jnp.kron(jnp.eye(8, dtype=BF16), w_enc)

time: 106 us -> 94.8 us (0.89)
  starting transfers between devices: 38.5 us -> 44.4 us
  waiting for transfers between devices: 9.95 us -> 4.4 us
  Pallas kernels: 43 us -> 38 us
  local copies, waits for them, and re-layouts: 11.2 us -> 6.87 us
  other arithmetic: 2.6 us -> 0.17 us
    all_to_all x1, starting transfers between devices: 7.17 us -> 15.7 us  [per_device(): recv = lax.all_to_all(send, 'row', 0, 0)]
    all_to_all x1, waiting for transfers between devices: 5.8 us -> 1.05 us  [per_device(): recv = lax.all_to_all(send, 'row', 0, 0)]
    pallas_call x1, Pallas kernels: 23.4 us -> 19.2 us  [bulk(): pl.pallas_call(bulk_kernel, out_shape=(jax.ShapeDtypeStruct((3, 16, 32 *...]
    ppermute x4 -> x5, starting transfers between devices: 18.3 us -> 14.2 us  [the longest x1 4.49 us: per_device(): opposite = lax.ppermute(lines, 'row', [(0, 15), (15, 0)])]
    slice x7 -> x1, local copies, waits for them, and re-layouts: 2.53 us -> 0.01 us  [per_device(): below = lax.ppermute(wide[:, :8], 'row', [(k + 1, k) for k in range(15)])]
    ppermute x4 -> x5, waiting for transfers between devices: 2.25 us -> 0.01 us  [the longest x1 0.01 us: per_device(): lax.ppermute(fields[:, :, :128], 'col', [(k + 1, k) for k in range(7)])]
    pallas_call x1, Pallas kernels: 14.3 us -> 12.3 us  [edges(): pl.pallas_call(edge_kernel, out_shape=jax.ShapeDtypeStruct((3, 16, 32 * C...]
    select_n x6 -> x0, other arithmetic: 1.8 us -> none  [the longest x1 0.94 us: per_device(): jnp.where(use_lines, jnp.where(far == 1, upper[None], lower[None]), sides...]
  transfers between devices with their start and end apart: 6 -> 7, of which waited for: 3 -> 2; matrix products, arithmetic and copies ran while one was open for 10% -> 5% of each run, Pallas kernels for 22% -> 25%
where the time goes in v3:
time: 94.8 us; the launch traced here: 94.2 us
  starting transfers between devices  44.4 us (47%)
  Pallas kernels  38 us (40%)
  local copies, waits for them, and re-layouts  6.87 us (7%)
  waiting for transfers between devices  4.4 us (5%)
    pallas_call x1, Pallas kernels, bulk(): pl.pallas_call(bulk_kernel, out_shape=(jax.ShapeDtypeStruct((3, 16, 32 *...  19.2 us
    all_to_all x1, starting transfers between devices, per_device(): recv = lax.all_to_all(send, 'row', 0, 0)  15.7 us
    all_to_all x1, starting transfers between devices, per_device(): bands = lax.all_to_all(routed, ('face', 'col'), 0, 0)  14.5 us
    pallas_call x1, Pallas kernels, edges(): pl.pallas_call(edge_kernel, out_shape=jax.ShapeDtypeStruct((3, 16, 32 * C...  12.3 us
    unnamed x26, local copies, waits for them, and re-layouts  4.74 us
    ppermute x1, starting transfers between devices, per_device(): opposite = lax.ppermute(lines, 'row', [(0, 15), (15, 0)])  4.49 us
    pallas_call x1, Pallas kernels, route(): pl.pallas_call(route_kernel, out_shape=jax.ShapeDtypeStruct((32, 112, 256...  4.33 us
    ppermute x1, starting transfers between devices, per_device(): above = lax.ppermute(wide[:, 24:], 'row', [(k, k + 1) for k in range(15)])  3.99 us
  transfers between devices with their start and end apart: 7, of which 2 were waited for; matrix products, arithmetic and copies ran while one was open for 5% of the time, Pallas kernels for 25%

profile of v3, /device:TPU:1, one launch (start us, length us, event | category | flops | bytes accessed | tf_op | source)
XLA Modules:
  0.0 94.2 jit_solution(16024006180568387715)
XLA Ops:
  0.0 0.1 pad_add_fusion.pos
  0.1 0.0 copy-start
  0.1 0.9 copy-done
  1.0 0.0 copy-start.1
  1.0 2.1 %strips.1 = (bf16[16,48,256]{2,1,0:T(8,128)(2,1)}, bf16[64,256]{1,0:T(8,128)(2,1)S(1)}) custom-call(s32[3]{0:T(128)S(1)} %pad_add_fusion.pos, bf16[3,32,1024]{2,1,0:T(8,128)(2,1)S(1)} %copy-done), custom_call_target="tpu_custom_call" | custom-call | tf_op jit(solution)/shard_map/strips/pallas_call | solution.py:762
  3.1 15.7 %all-to-all-start = ((bf16[16,48,256]{2,1,0:T(8,128)(2,1)}), bf16[16,48,256]{2,1,0:T(8,128)(2,1)S(1)}, u32[]{:S(2)}, u32[]{:S(2)}) async-start(bf16[16,48,256]{2,1,0:T(8,128)(2,1)} %get-tuple-element.13), calls=%async_computation | async-start | bytes 786432 | tf_op jit(solution)/shard_map/all_to_all | solution.py:881
  18.9 0.8 fusion.2
  19.6 3.1 %collective-permute-start.1 = (bf16[3,32,128]{2,1,0:T(8,128)(2,1)S(1)}, bf16[3,32,128]{2,1,0:T(8,128)(2,1)S(1)}, u32[]{:S(2)}, u32[]{:S(2)}) collective-permute-start(bf16[3,32,128]{2,1,0:T(8,128)(2,1)S(1)} %get-tuple-element.24), channel_id=1, source_target_pairs={{0,1},{1,2},{2,3},{3,4},{4,5},{5,6},{6,7},{8,9},{9,10},{10,11},{11... | collective-permute-start | bytes 73736 | tf_op jit(solution)/shard_map/ppermute | solution.py:884
  22.7 1.3 %collective-permute-start.2 = (bf16[3,32,128]{2,1,0:T(8,128)(2,1)S(1)}, bf16[3,32,128]{2,1,0:T(8,128)(2,1)S(1)}, u32[]{:S(2)}, u32[]{:S(2)}) collective-permute-start(bf16[3,32,128]{2,1,0:T(8,128)(2,1)S(1)} %get-tuple-element.23), channel_id=1, source_target_pairs={{1,0},{2,1},{3,2},{4,3},{5,4},{6,5},{7,6},{9,8},{10,9},{11,10},{12... | collective-permute-start | bytes 73736 | tf_op jit(solution)/shard_map/ppermute | solution.py:885
  24.0 4.5 %collective-permute-start = (bf16[64,256]{1,0:T(8,128)(2,1)S(1)}, bf16[64,256]{1,0:T(8,128)(2,1)S(1)}, u32[]{:S(2)}, u32[]{:S(2)}) collective-permute-start(bf16[64,256]{1,0:T(8,128)(2,1)S(1)} %get-tuple-element.14.own), channel_id=1, source_target_pairs={{0,120},{120,0},{1,121},{121,1},{2,122},{122,2},{3,123},{123,3},{4... | collective-permute-start | bytes 98312 | tf_op jit(solution)/shard_map/ppermute | solution.py:882
  28.5 0.8 copy.18
  29.3 0.1 reshape.41.nb
  29.5 0.0 copy-start.2
  29.5 0.0 collective-permute-done.1.before
  29.5 0.0 copy-start.4
  29.5 0.9 %constant_dynamic-update-slice_fusion.1 = bf16[3,32,1280]{2,1,0:T(8,128)(2,1)S(1)} fusion(bf16[3,32,1280]{2,1,0:T(8,128)(2,1)S(1)} %constant_dynamic-update-slice_fusion.2, bf16[3,32,1024]{2,1,0:T(8,128)(2,1)} %fields.5), kind=kLoop, calls=%fused_computation.3 | loop fusion | bytes 393216
  30.5 0.0 collective-permute-done.2.after
  30.5 0.0 copy-start.5
  30.5 1.3 %collective-permute-start.4 = (bf16[3,8,1280]{2,1,0:T(8,128)(2,1)S(1)}, bf16[3,8,1280]{2,1,0:T(8,128)(2,1)S(1)}, u32[]{:S(2)}, u32[]{:S(2)}) collective-permute-start(bf16[3,8,1280]{2,1,0:T(8,128)(2,1)S(1)} %get-tuple-element.21), channel_id=1, source_target_pairs={{8,0},{16,8},{24,16},{32,24},{40,32},{48,40},{56,48},{64,56},{72,6... | collective-permute-start | bytes 184328 | tf_op jit(solution)/shard_map/ppermute | solution.py:888
  31.8 4.0 %collective-permute-start.3 = (bf16[3,8,1280]{2,1,0:T(8,128)(2,1)S(1)}, bf16[3,8,1280]{2,1,0:T(8,128)(2,1)S(1)}, u32[]{:S(2)}, u32[]{:S(2)}) collective-permute-start(bf16[3,8,1280]{2,1,0:T(8,128)(2,1)S(1)} %get-tuple-element.22), channel_id=1, source_target_pairs={{0,8},{8,16},{16,24},{24,32},{32,40},{40,48},{48,56},{56,64},{64,7... | collective-permute-start | bytes 184328 | tf_op jit(solution)/shard_map/ppermute | solution.py:887
  35.8 0.0 collective-permute-done.opp
  35.8 1.0 %all-to-all-done.recv = bf16[16,48,256]{2,1,0:T(8,128)(2,1)S(1)} async-done(((bf16[16,48,256]{2,1,0:T(8,128)(2,1)}), bf16[16,48,256]{2,1,0:T(8,128)(2,1)S(1)}, u32[]{:S(2)}, u32[]{:S(2)}) %all-to-all-start) | async-done | bytes 393248 | tf_op jit(solution)/shard_map/all_to_all | solution.py:881
  36.9 4.3 %route.1 = bf16[32,112,256]{2,1,0:T(8,128)(2,1)} custom-call(s32[144]{0:T(256)S(1)} %reshape.41.nb, s32[3]{0:T(128)S(1)} %pad_add_fusion.pos, bf16[16,48,256]{2,1,0:T(8,128)(2,1)S(1)} %all-to-all-done.recv, bf16[64,256]{1,0:T(8,128)(2,1)S(1)} %get-tuple-element.14.own, bf16[64,256]{1,0:T(8,128)(2,1)S(1)} %collective-permute-done.opp), custom_call_target="tpu_custom_call" | custom-call | flops 1000000000 | bytes 4000000 | tf_op jit(solution)/shard_map/route/pallas_call | solution.py:776
  41.2 0.0 copy-done.1
  41.2 0.0 copy-done.2
  41.2 0.0 copy-done.4
  41.2 0.0 copy-done.5
  41.3 0.0 copy-start.9
  41.3 0.0 copy-start.8
  41.3 0.0 copy-start.10
  41.3 0.0 collective-permute-done.4.below
  41.3 0.0 copy-start.6
  41.3 0.0 collective-permute-done.3.above
  41.3 0.0 copy-start.7
  41.3 14.5 %all-to-all-start.1 = ((bf16[32,112,256]{2,1,0:T(8,128)(2,1)}), bf16[32,112,256]{2,1,0:T(8,128)(2,1)S(1)}, u32[]{:S(2)}, u32[]{:S(2)}) async-start(bf16[32,112,256]{2,1,0:T(8,128)(2,1)} %route.1), calls=%async_computation.1 | async-start | bytes 3670016 | tf_op jit(solution)/shard_map/all_to_all | solution.py:892
  55.8 0.0 copy-done.9
  55.8 0.6 reshape.42.kernel_first
  56.4 0.0 copy-done.6
  56.4 0.0 copy-done.7
  56.4 0.0 copy-done.8
  56.4 0.6 reshape.46.kernel_second
  57.0 0.0 copy-done.10
  57.0 0.1 broadcast_multiply_fusion
  57.1 0.8 copy.21
  57.9 19.2 %bulk.1 = (bf16[3,16,8192]{2,1,0:T(8,128)(2,1)}, f32[3,36,8,256]{3,2,1,0:T(8,128)}, f32[3,7,24,256]{3,2,1,0:T(8,128)}) custom-call(s32[3]{0:T(128)} %copy-done.1, bf16[3,32,1024]{2,1,0:T(8,128)(2,1)} %fields.5, bf16[3,8,1280]{2,1,0:T(8,128)(2,1)} %copy-done.7, bf16[3,8,1280]{2,1,0:T(8,128)(2,1)} %copy-done.6, bf16[3,32,128]{2,1,0:T(8,128)(2,1)} %copy-done.4, ...), custom_call_target="tpu_custom_call" | custom-call | flops 5000000000 | bytes 4000000 | tf_op jit(solution)/shard_map/bulk/pallas_call | solution.py:797
  77.1 3.3 %all-to-all-done.1.bands = bf16[32,112,256]{2,1,0:T(8,128)(2,1)S(1)} async-done(((bf16[32,112,256]{2,1,0:T(8,128)(2,1)}), bf16[32,112,256]{2,1,0:T(8,128)(2,1)S(1)}, u32[]{:S(2)}, u32[]{:S(2)}) %all-to-all-start.1) | async-done | bytes 1835040 | tf_op jit(solution)/shard_map/all_to_all | solution.py:892
  80.4 0.0 copy-start.3
  80.4 1.3 %copy-done.3 = bf16[32,112,256]{2,1,0:T(8,128)(2,1)} copy-done((bf16[32,112,256]{2,1,0:T(8,128)(2,1)}, bf16[32,112,256]{2,1,0:T(8,128)(2,1)S(1)}, u32[]{:S(2)}) %copy-start.3) | copy-done | bytes 1835032
  81.7 12.3 %edges.1 = bf16[3,16,8192]{2,1,0:T(8,128)(2,1)} custom-call(s32[144]{0:T(256)} %copy-done.2, s32[3]{0:T(128)} %copy-done.1, bf16[32,112,256]{2,1,0:T(8,128)(2,1)} %copy-done.3, bf16[3,32,1024]{2,1,0:T(8,128)(2,1)} %fields.5, bf16[3,8,1280]{2,1,0:T(8,128)(2,1)} %copy-done.7, bf16[3,8,1280]{2,1,0:T(8,128)(2,1)} %copy-done.6, ...), custom_call_target="tpu_custom_call", output_to_operand_aliasing={{}: (8, {})} | custom-call | tf_op jit(solution)/shard_map/edges/pallas_call | solution.py:827
  (4 shorter events, 0.0 us)
Async XLA Ops:
  0.1 0.9 copy-start
  1.0 40.2 %copy-start.1 = (s32[3]{0:T(128)}, s32[3]{0:T(128)S(1)}, u32[]{:S(2)}) copy-start(s32[3]{0:T(128)S(1)} %pad_add_fusion.pos) | copy-start | bytes 40
  3.1 33.8 %all-to-all-start = ((bf16[16,48,256]{2,1,0:T(8,128)(2,1)}), bf16[16,48,256]{2,1,0:T(8,128)(2,1)S(1)}, u32[]{:S(2)}, u32[]{:S(2)}) async-start(bf16[16,48,256]{2,1,0:T(8,128)(2,1)} %get-tuple-element.13), calls=%async_computation | async-start | bytes 786432 | tf_op jit(solution)/shard_map/all_to_all | solution.py:881
  19.6 9.9 %collective-permute-start.1 = (bf16[3,32,128]{2,1,0:T(8,128)(2,1)S(1)}, bf16[3,32,128]{2,1,0:T(8,128)(2,1)S(1)}, u32[]{:S(2)}, u32[]{:S(2)}) collective-permute-start(bf16[3,32,128]{2,1,0:T(8,128)(2,1)S(1)} %get-tuple-element.24), channel_id=1, source_target_pairs={{0,1},{1,2},{2,3},{3,4},{4,5},{5,6},{6,7},{8,9},{9,10},{10,11},{11... | collective-permute-start | bytes 73736 | tf_op jit(solution)/shard_map/ppermute | solution.py:884
  22.7 7.7 %collective-permute-start.2 = (bf16[3,32,128]{2,1,0:T(8,128)(2,1)S(1)}, bf16[3,32,128]{2,1,0:T(8,128)(2,1)S(1)}, u32[]{:S(2)}, u32[]{:S(2)}) collective-permute-start(bf16[3,32,128]{2,1,0:T(8,128)(2,1)S(1)} %get-tuple-element.23), channel_id=1, source_target_pairs={{1,0},{2,1},{3,2},{4,3},{5,4},{6,5},{7,6},{9,8},{10,9},{11,10},{12... | collective-permute-start | bytes 73736 | tf_op jit(solution)/shard_map/ppermute | solution.py:885
  24.0 11.8 %collective-permute-start = (bf16[64,256]{1,0:T(8,128)(2,1)S(1)}, bf16[64,256]{1,0:T(8,128)(2,1)S(1)}, u32[]{:S(2)}, u32[]{:S(2)}) collective-permute-start(bf16[64,256]{1,0:T(8,128)(2,1)S(1)} %get-tuple-element.14.own), channel_id=1, source_target_pairs={{0,120},{120,0},{1,121},{121,1},{2,122},{122,2},{3,123},{123,3},{4... | collective-permute-start | bytes 98312 | tf_op jit(solution)/shard_map/ppermute | solution.py:882
  29.5 11.8 %copy-start.2 = (s32[144]{0:T(256)}, s32[144]{0:T(256)S(1)}, u32[]{:S(2)}) copy-start(s32[144]{0:T(256)S(1)} %reshape.41.nb) | copy-start | bytes 1732
  29.5 11.7 %copy-start.4 = (bf16[3,32,128]{2,1,0:T(8,128)(2,1)}, bf16[3,32,128]{2,1,0:T(8,128)(2,1)S(1)}, u32[]{:S(2)}) copy-start(bf16[3,32,128]{2,1,0:T(8,128)(2,1)S(1)} %collective-permute-done.1.before) | copy-start | bytes 73732
  30.5 10.8 %copy-start.5 = (bf16[3,32,128]{2,1,0:T(8,128)(2,1)}, bf16[3,32,128]{2,1,0:T(8,128)(2,1)S(1)}, u32[]{:S(2)}) copy-start(bf16[3,32,128]{2,1,0:T(8,128)(2,1)S(1)} %collective-permute-done.2.after) | copy-start | bytes 73732
  30.5 10.8 %collective-permute-start.4 = (bf16[3,8,1280]{2,1,0:T(8,128)(2,1)S(1)}, bf16[3,8,1280]{2,1,0:T(8,128)(2,1)S(1)}, u32[]{:S(2)}, u32[]{:S(2)}) collective-permute-start(bf16[3,8,1280]{2,1,0:T(8,128)(2,1)S(1)} %get-tuple-element.21), channel_id=1, source_target_pairs={{8,0},{16,8},{24,16},{32,24},{40,32},{48,40},{56,48},{64,56},{72,6... | collective-permute-start | bytes 184328 | tf_op jit(solution)/shard_map/ppermute | solution.py:888
  31.8 9.5 %collective-permute-start.3 = (bf16[3,8,1280]{2,1,0:T(8,128)(2,1)S(1)}, bf16[3,8,1280]{2,1,0:T(8,128)(2,1)S(1)}, u32[]{:S(2)}, u32[]{:S(2)}) collective-permute-start(bf16[3,8,1280]{2,1,0:T(8,128)(2,1)S(1)} %get-tuple-element.22), channel_id=1, source_target_pairs={{0,8},{8,16},{16,24},{24,32},{32,40},{40,48},{48,56},{56,64},{64,7... | collective-permute-start | bytes 184328 | tf_op jit(solution)/shard_map/ppermute | solution.py:887
  41.3 14.5 %copy-start.9 = (f32[3,3,128]{2,1,0:T(4,128)S(1)}, f32[3,3,128]{2,1,0:T(4,128)}, u32[]{:S(2)}) copy-start(f32[3,3,128]{2,1,0:T(4,128)} %param.19) | copy-start | bytes 13828
  41.3 15.1 %copy-start.8 = (f32[3,3,256]{2,1,0:T(4,128)S(1)}, f32[3,3,256]{2,1,0:T(4,128)}, u32[]{:S(2)}) copy-start(f32[3,3,256]{2,1,0:T(4,128)} %param.26) | copy-start | bytes 27652
  41.3 15.8 %copy-start.10 = (bf16[16,128]{1,0:T(8,128)(2,1)S(1)}, bf16[16,128]{1,0:T(8,128)(2,1)}, u32[]{:S(2)}) copy-start(bf16[16,128]{1,0:T(8,128)(2,1)} %param.18) | copy-start | bytes 12292
  41.3 15.1 %copy-start.6 = (bf16[3,8,1280]{2,1,0:T(8,128)(2,1)}, bf16[3,8,1280]{2,1,0:T(8,128)(2,1)S(1)}, u32[]{:S(2)}) copy-start(bf16[3,8,1280]{2,1,0:T(8,128)(2,1)S(1)} %collective-permute-done.4.below) | copy-start | bytes 184324
  41.3 15.1 %copy-start.7 = (bf16[3,8,1280]{2,1,0:T(8,128)(2,1)}, bf16[3,8,1280]{2,1,0:T(8,128)(2,1)S(1)}, u32[]{:S(2)}) copy-start(bf16[3,8,1280]{2,1,0:T(8,128)(2,1)S(1)} %collective-permute-done.3.above) | copy-start | bytes 184324
  41.3 39.1 %all-to-all-start.1 = ((bf16[32,112,256]{2,1,0:T(8,128)(2,1)}), bf16[32,112,256]{2,1,0:T(8,128)(2,1)S(1)}, u32[]{:S(2)}, u32[]{:S(2)}) async-start(bf16[32,112,256]{2,1,0:T(8,128)(2,1)} %route.1), calls=%async_computation.1 | async-start | bytes 3670016 | tf_op jit(solution)/shard_map/all_to_all | solution.py:892
  80.4 1.3 %copy-start.3 = (bf16[32,112,256]{2,1,0:T(8,128)(2,1)}, bf16[32,112,256]{2,1,0:T(8,128)(2,1)S(1)}, u32[]{:S(2)}) copy-start(bf16[32,112,256]{2,1,0:T(8,128)(2,1)S(1)} %all-to-all-done.1.bands) | copy-start | bytes 5505028

commit v4 on v3

--- a/solution.py
+++ b/solution.py
@@ -324,23 +324,23 @@
 
     def one_face(i, carry):
         def one_chunk(k, carry):
-            j0 = 80 * i + 4 + 8 * k
-            total = jnp.zeros((8, 40, 128), F32)
+            j0 = 80 * i + 4 + 24 * k
+            total = jnp.zeros((24, 40, 128), F32)
             for a in range(3):
                 for b in range(3):
-                    window = grid[pl.ds(j0 + b - 1, 8), 3 + a : 43 + a, :]
+                    window = grid[pl.ds(j0 + b - 1, 24), 3 + a : 43 + a, :]
                     total = total + window * kernel_first[3 * a + b : 3 * a + b + 1, :][None]
-            normed = normalise(total.reshape(320, C1), gain_first[...])
+            normed = normalise(total.reshape(960, C1), gain_first[...])
             hidden = gelu(dot(normed, expand_first[...]) + bias_first[...]).astype(BF16)
             update = dot(hidden, contract_first[...])
-            here = grid[pl.ds(j0, 8), 4:44, :].reshape(320, C1)
-            rows[...] = rounded(here + scale_first[...] * update).reshape(8, 40, C1)
+            here = grid[pl.ds(j0, 24), 4:44, :].reshape(960, C1)
+            rows[...] = rounded(here + scale_first[...] * update).reshape(24, 40, C1)
             paired = rows[:, pl.ds(0, 20, stride=2), :] + rows[:, pl.ds(1, 20, stride=2), :]
-            paired = paired.reshape(4, 2, 20, C1)
-            pooled[pl.ds(4 * k, 4), 0:20, :] = 0.25 * (paired[:, 0] + paired[:, 1])
+            paired = paired.reshape(12, 2, 20, C1)
+            pooled[pl.ds(12 * k, 12), 0:20, :] = 0.25 * (paired[:, 0] + paired[:, 1])
             return carry
 
-        lax.fori_loop(0, 9, one_chunk, 0, unroll=9)
+        lax.fori_loop(0, 3, one_chunk, 0, unroll=3)
         pooled[:, 20:24, :] = jnp.zeros((36, 4, C1), F32)
         product = dot(pooled[...].reshape(36 * 24, C1).astype(BF16), down[...])
         coarse[i] = rounded(product).reshape(36, 24, C2)
@@ -402,9 +402,9 @@
     either = jnp.logical_or(
         jnp.logical_or(r == 0, r == 15), jnp.logical_or(c == 0, c == 7)
     )
-    held, sems = scratch[-24:-1], scratch[-1]
+    held, sems = scratch[-23:-1], scratch[-1]
     sources = (
-        bands, enc_cells, fields, above, below, before, after,
+        enc_cells, fields, above, below, before, after,
         kernel_first, gain_first, expand_first, bias_first, contract_first, scale_first, down,
         kernel_second, edge_rows, edge_cols, gain_second, expand_second, bias_second,
         contract_second, scale_second, first_out,
@@ -413,16 +413,16 @@
     @pl.when(either)
     def _():
         copies = fetch(sources, held, sems)
-        patched(nb, pos, held, copies, out, sems, *scratch[:-24])
+        patched(nb, pos, bands, held, copies, out, sems, *scratch[:-23])
 
 
 def patched(
-    nb, pos, held, copies, out, sems,
+    nb, pos, bands, held, copies, out, sems,
     cells, grid, side_grid, banded, taps, side_taps, mix, strip, rows, pooled, side_pooled,
     level, side_level, mixed, center, packed, patch,
 ):
     (
-        bands, enc_cells, fields, above, below, before, after,
+        enc_cells, fields, above, below, before, after,
         kernel_first, gain_first, expand_first, bias_first, contract_first, scale_first, down,
         kernel_second, edge_rows, edge_cols, gain_second, expand_second, bias_second,
         contract_second, scale_second, result,
@@ -437,10 +437,9 @@
     def add(k, total):
         return total + bands[k]
 
-    copies[0].wait()
     total = lax.fori_loop(0, 32, add, jnp.zeros((112, 256), BF16), unroll=8)
     both = jnp.concatenate([total[:, 0:128], total[:, 128:256]], axis=0)
-    copies[1].wait()
+    copies[0].wait()
     for k in range(4):
         product = rounded(dot(both, enc_cells[:, 256 * k : 256 * k + 256]))
         for j in range(2):
@@ -489,7 +488,7 @@
         hidden = gelu(dot(normed, expand_first[...]) + bias_first[...]).astype(BF16)
         return rounded(here + scale_first[...] * dot(hidden, contract_first[...]))
 
-    for copy in copies[2:14]:
+    for copy in copies[1:13]:
         copy.wait()
     for i in range(3):
         spread(i, above, fields, below, before, after, cells.at[i])
@@ -525,24 +524,24 @@
                     taps[9 * i + 3 * a + b, 4:8, :] = jnp.where(top, own, line)
 
         def one_chunk(k, carry):
-            i = (k * 11) >> 5
-            j0 = 80 * i + 4 + 24 * (k - 3 * i)
-            total = jnp.zeros((24, 8, 128), F32)
+            i = k
+            j0 = 80 * i + 4
+            total = jnp.zeros((72, 8, 128), F32)
             for a in range(3):
                 for b in range(3):
-                    window = grid[pl.ds(j0 + b - 1, 24), 3 + a : 11 + a, :]
+                    window = grid[pl.ds(j0 + b - 1, 72), 3 + a : 11 + a, :]
                     total = total + window * taps[9 * i + 3 * a + b][None]
-            here = grid[pl.ds(j0, 24), 4:12, :].reshape(192, C1)
+            here = grid[pl.ds(j0, 72), 4:12, :].reshape(576, C1)
             slot = lax.rem(k, 3)
-            strip[slot] = block_first(total.reshape(192, C1), here).reshape(24, 8, C1)
+            strip[slot] = block_first(total.reshape(576, C1), here).reshape(72, 8, C1)
             paired = strip[slot, :, pl.ds(0, 4, stride=2), :] + strip[slot, :, pl.ds(1, 4, stride=2), :]
-            paired = paired.reshape(12, 2, 4, C1)
-            pooled[pl.ds(12 * k, 12), 0:4, :] = 0.25 * (paired[:, 0] + paired[:, 1])
+            paired = paired.reshape(36, 2, 4, C1)
+            pooled[pl.ds(36 * k, 36), 0:4, :] = 0.25 * (paired[:, 0] + paired[:, 1])
             return carry
 
         pooled[...] = jnp.zeros_like(pooled)
-        lax.fori_loop(0, 9, one_chunk, 0, unroll=9)
-    for copy in copies[14:17]:
+        lax.fori_loop(0, 3, one_chunk, 0, unroll=3)
+    for copy in copies[13:16]:
         copy.wait()
 
     @pl.when(outer)
@@ -715,7 +714,7 @@
             mixed[row : row + 48, :] = total.reshape(48, C2)
             center[row : row + 48, :] = side_level[7 * i + 2 : 7 * i + 5, 2:18, :].reshape(48, C2)
 
-    for copy in copies[17:]:
+    for copy in copies[16:]:
         copy.wait()
     normed = normalise(mixed[...], gain_second[...])
     hidden = gelu(dot(normed, expand_second[...]) + bias_second[...]).astype(BF16)
@@ -806,7 +805,7 @@
         scratch_shapes=[
             pltpu.VMEM((10, 48, 128), F32),
             pltpu.VMEM((240, 48, 128), F32),
-            pltpu.VMEM((8, 40, 128), F32),
+            pltpu.VMEM((24, 40, 128), F32),
             pltpu.VMEM((36, 24, 128), F32),
             pltpu.VMEM((3, 36, 24, 256), F32),
             pltpu.VMEM((3, 16, 32 * C2), BF16),
@@ -822,12 +821,12 @@
 
 
 def edges(links, pos, halos, bands, first_out, edge_rows, edge_cols, enc_cells, weights):
-    sources = (bands, enc_cells, *halos, *weights[:8], edge_rows, edge_cols, *weights[8:], first_out)
+    sources = (enc_cells, *halos, *weights[:8], edge_rows, edge_cols, *weights[8:], first_out)
     operands = (bands, *halos, first_out, edge_rows, edge_cols, enc_cells, *weights)
     return pl.pallas_call(
         edge_kernel,
         out_shape=jax.ShapeDtypeStruct((3, 16, 32 * C2), BF16),
-        in_specs=[SMEM, SMEM] + [FAR] * len(operands),
+        in_specs=[SMEM, SMEM, WHOLE] + [FAR] * (len(operands) - 1),
         out_specs=FAR,
         input_output_aliases={2 + len(halos) + 1: 0},
         scratch_shapes=[
@@ -838,7 +837,7 @@
             pltpu.VMEM((27, 8, 128), F32),
             pltpu.VMEM((3, 2, 9, 40, 128), F32),
             pltpu.VMEM((3, 8, 40, 128), F32),
-            pltpu.VMEM((3, 24, 8, 128), F32),
+            pltpu.VMEM((3, 72, 8, 128), F32),
             pltpu.VMEM((3, 8, 40, 128), F32),
             pltpu.VMEM((108, 8, 128), F32),
             pltpu.VMEM((12, 24, 128), F32),

time: 94.8 us -> 94.1 us (level)
  Pallas kernels: 38 us -> 37 us
  transfers between devices with their start and end apart: 7 -> 7, of which waited for: 2 -> 2; matrix products, arithmetic and copies ran while one was open for 5% -> 5% of each run, Pallas kernels for 25% -> 24%
where the time goes in v4:
time: 94.1 us; the launch traced here: 93.9 us
  starting transfers between devices  44.7 us (48%)
  Pallas kernels  37 us (39%)
  local copies, waits for them, and re-layouts  6.87 us (7%)
  waiting for transfers between devices  4.7 us (5%)
    pallas_call x1, Pallas kernels, bulk(): pl.pallas_call(bulk_kernel, out_shape=(jax.ShapeDtypeStruct((3, 16, 32 *...  18.9 us
    all_to_all x1, starting transfers between devices, per_device(): recv = lax.all_to_all(send, 'row', 0, 0)  15.7 us
    all_to_all x1, starting transfers between devices, per_device(): bands = lax.all_to_all(routed, ('face', 'col'), 0, 0)  14.8 us
    pallas_call x1, Pallas kernels, edges(): pl.pallas_call(edge_kernel, out_shape=jax.ShapeDtypeStruct((3, 16, 32 * C...  11.9 us
    unnamed x26, local copies, waits for them, and re-layouts  4.74 us
    ppermute x1, starting transfers between devices, per_device(): opposite = lax.ppermute(lines, 'row', [(0, 15), (15, 0)])  4.49 us
    pallas_call x1, Pallas kernels, route(): pl.pallas_call(route_kernel, out_shape=jax.ShapeDtypeStruct((32, 112, 256...  4.04 us
    ppermute x1, starting transfers between devices, per_device(): above = lax.ppermute(wide[:, 24:], 'row', [(k, k + 1) for k in range(15)])  3.99 us
  transfers between devices with their start and end apart: 7, of which 2 were waited for; matrix products, arithmetic and copies ran while one was open for 5% of the time, Pallas kernels for 24%

profile of v4, /device:TPU:1, one launch (start us, length us, event | category | flops | bytes accessed | tf_op | source)
XLA Modules:
  0.0 93.9 jit_solution(10004980196988612637)
XLA Ops:
  0.0 0.1 pad_add_fusion.pos
  0.1 0.0 copy-start
  0.1 0.9 copy-done
  1.0 0.0 copy-start.1
  1.0 2.1 %strips.1 = (bf16[16,48,256]{2,1,0:T(8,128)(2,1)}, bf16[64,256]{1,0:T(8,128)(2,1)S(1)}) custom-call(s32[3]{0:T(128)S(1)} %pad_add_fusion.pos, bf16[3,32,1024]{2,1,0:T(8,128)(2,1)S(1)} %copy-done), custom_call_target="tpu_custom_call" | custom-call | tf_op jit(solution)/shard_map/strips/pallas_call | solution.py:761
  3.1 15.7 %all-to-all-start = ((bf16[16,48,256]{2,1,0:T(8,128)(2,1)}), bf16[16,48,256]{2,1,0:T(8,128)(2,1)S(1)}, u32[]{:S(2)}, u32[]{:S(2)}) async-start(bf16[16,48,256]{2,1,0:T(8,128)(2,1)} %get-tuple-element.13), calls=%async_computation | async-start | bytes 786432 | tf_op jit(solution)/shard_map/all_to_all | solution.py:880
  18.9 0.8 fusion.2
  19.6 3.1 %collective-permute-start.1 = (bf16[3,32,128]{2,1,0:T(8,128)(2,1)S(1)}, bf16[3,32,128]{2,1,0:T(8,128)(2,1)S(1)}, u32[]{:S(2)}, u32[]{:S(2)}) collective-permute-start(bf16[3,32,128]{2,1,0:T(8,128)(2,1)S(1)} %get-tuple-element.24), channel_id=1, source_target_pairs={{0,1},{1,2},{2,3},{3,4},{4,5},{5,6},{6,7},{8,9},{9,10},{10,11},{11... | collective-permute-start | bytes 73736 | tf_op jit(solution)/shard_map/ppermute | solution.py:883
  22.7 1.3 %collective-permute-start.2 = (bf16[3,32,128]{2,1,0:T(8,128)(2,1)S(1)}, bf16[3,32,128]{2,1,0:T(8,128)(2,1)S(1)}, u32[]{:S(2)}, u32[]{:S(2)}) collective-permute-start(bf16[3,32,128]{2,1,0:T(8,128)(2,1)S(1)} %get-tuple-element.23), channel_id=1, source_target_pairs={{1,0},{2,1},{3,2},{4,3},{5,4},{6,5},{7,6},{9,8},{10,9},{11,10},{12... | collective-permute-start | bytes 73736 | tf_op jit(solution)/shard_map/ppermute | solution.py:884
  24.0 4.5 %collective-permute-start = (bf16[64,256]{1,0:T(8,128)(2,1)S(1)}, bf16[64,256]{1,0:T(8,128)(2,1)S(1)}, u32[]{:S(2)}, u32[]{:S(2)}) collective-permute-start(bf16[64,256]{1,0:T(8,128)(2,1)S(1)} %get-tuple-element.14.own), channel_id=1, source_target_pairs={{0,120},{120,0},{1,121},{121,1},{2,122},{122,2},{3,123},{123,3},{4... | collective-permute-start | bytes 98312 | tf_op jit(solution)/shard_map/ppermute | solution.py:881
  28.5 0.8 copy.18
  29.3 0.1 reshape.41.nb
  29.5 0.0 copy-start.2
  29.5 0.0 collective-permute-done.1.before
  29.5 0.0 copy-start.4
  29.5 0.9 %constant_dynamic-update-slice_fusion.1 = bf16[3,32,1280]{2,1,0:T(8,128)(2,1)S(1)} fusion(bf16[3,32,1280]{2,1,0:T(8,128)(2,1)S(1)} %constant_dynamic-update-slice_fusion.2, bf16[3,32,1024]{2,1,0:T(8,128)(2,1)} %fields.5), kind=kLoop, calls=%fused_computation.3 | loop fusion | bytes 393216
  30.5 0.0 collective-permute-done.2.after
  30.5 0.0 copy-start.5
  30.5 1.3 %collective-permute-start.4 = (bf16[3,8,1280]{2,1,0:T(8,128)(2,1)S(1)}, bf16[3,8,1280]{2,1,0:T(8,128)(2,1)S(1)}, u32[]{:S(2)}, u32[]{:S(2)}) collective-permute-start(bf16[3,8,1280]{2,1,0:T(8,128)(2,1)S(1)} %get-tuple-element.21), channel_id=1, source_target_pairs={{8,0},{16,8},{24,16},{32,24},{40,32},{48,40},{56,48},{64,56},{72,6... | collective-permute-start | bytes 184328 | tf_op jit(solution)/shard_map/ppermute | solution.py:887
  31.8 4.0 %collective-permute-start.3 = (bf16[3,8,1280]{2,1,0:T(8,128)(2,1)S(1)}, bf16[3,8,1280]{2,1,0:T(8,128)(2,1)S(1)}, u32[]{:S(2)}, u32[]{:S(2)}) collective-permute-start(bf16[3,8,1280]{2,1,0:T(8,128)(2,1)S(1)} %get-tuple-element.22), channel_id=1, source_target_pairs={{0,8},{8,16},{16,24},{24,32},{32,40},{40,48},{48,56},{56,64},{64,7... | collective-permute-start | bytes 184328 | tf_op jit(solution)/shard_map/ppermute | solution.py:886
  35.8 0.0 collective-permute-done.opp
  35.8 1.0 %all-to-all-done.recv = bf16[16,48,256]{2,1,0:T(8,128)(2,1)S(1)} async-done(((bf16[16,48,256]{2,1,0:T(8,128)(2,1)}), bf16[16,48,256]{2,1,0:T(8,128)(2,1)S(1)}, u32[]{:S(2)}, u32[]{:S(2)}) %all-to-all-start) | async-done | bytes 393248 | tf_op jit(solution)/shard_map/all_to_all | solution.py:880
  36.9 4.0 %route.1 = bf16[32,112,256]{2,1,0:T(8,128)(2,1)} custom-call(s32[144]{0:T(256)S(1)} %reshape.41.nb, s32[3]{0:T(128)S(1)} %pad_add_fusion.pos, bf16[16,48,256]{2,1,0:T(8,128)(2,1)S(1)} %all-to-all-done.recv, bf16[64,256]{1,0:T(8,128)(2,1)S(1)} %get-tuple-element.14.own, bf16[64,256]{1,0:T(8,128)(2,1)S(1)} %collective-permute-done.opp), custom_call_target="tpu_custom_call" | custom-call | flops 1000000000 | bytes 4000000 | tf_op jit(solution)/shard_map/route/pallas_call | solution.py:775
  40.9 0.0 copy-done.1
  40.9 0.0 copy-done.2
  40.9 0.0 copy-done.4
  41.0 0.0 copy-done.5
  41.0 0.0 copy-start.9
  41.0 0.0 copy-start.8
  41.0 0.0 copy-start.10
  41.0 0.0 collective-permute-done.4.below
  41.0 0.0 copy-start.6
  41.0 0.0 collective-permute-done.3.above
  41.0 0.0 copy-start.7
  41.0 14.8 %all-to-all-start.1 = ((bf16[32,112,256]{2,1,0:T(8,128)(2,1)}), bf16[32,112,256]{2,1,0:T(8,128)(2,1)S(1)}, u32[]{:S(2)}, u32[]{:S(2)}) async-start(bf16[32,112,256]{2,1,0:T(8,128)(2,1)} %route.1), calls=%async_computation.1 | async-start | bytes 3670016 | tf_op jit(solution)/shard_map/all_to_all | solution.py:891
  55.8 0.0 copy-done.9
  55.9 0.6 reshape.42.kernel_first
  56.5 0.0 copy-done.6
  56.5 0.0 copy-done.7
  56.5 0.0 copy-done.8
  56.5 0.6 reshape.46.kernel_second
  57.1 0.0 copy-done.10
  57.1 0.1 broadcast_multiply_fusion
  57.2 0.8 copy.21
  57.9 18.9 %bulk.1 = (bf16[3,16,8192]{2,1,0:T(8,128)(2,1)}, f32[3,36,8,256]{3,2,1,0:T(8,128)}, f32[3,7,24,256]{3,2,1,0:T(8,128)}) custom-call(s32[3]{0:T(128)} %copy-done.1, bf16[3,32,1024]{2,1,0:T(8,128)(2,1)} %fields.5, bf16[3,8,1280]{2,1,0:T(8,128)(2,1)} %copy-done.7, bf16[3,8,1280]{2,1,0:T(8,128)(2,1)} %copy-done.6, bf16[3,32,128]{2,1,0:T(8,128)(2,1)} %copy-done.4, ...), custom_call_target="tpu_custom_call" | custom-call | flops 5000000000 | bytes 4000000 | tf_op jit(solution)/shard_map/bulk/pallas_call | solution.py:796
  76.8 3.6 %all-to-all-done.1.bands = bf16[32,112,256]{2,1,0:T(8,128)(2,1)S(1)} async-done(((bf16[32,112,256]{2,1,0:T(8,128)(2,1)}), bf16[32,112,256]{2,1,0:T(8,128)(2,1)S(1)}, u32[]{:S(2)}, u32[]{:S(2)}) %all-to-all-start.1) | async-done | bytes 1835040 | tf_op jit(solution)/shard_map/all_to_all | solution.py:891
  80.5 0.0 copy-start.3
  80.5 1.3 %copy-done.3 = bf16[32,112,256]{2,1,0:T(8,128)(2,1)} copy-done((bf16[32,112,256]{2,1,0:T(8,128)(2,1)}, bf16[32,112,256]{2,1,0:T(8,128)(2,1)S(1)}, u32[]{:S(2)}) %copy-start.3) | copy-done | bytes 1835032
  81.8 11.9 %edges.1 = bf16[3,16,8192]{2,1,0:T(8,128)(2,1)} custom-call(s32[144]{0:T(256)} %copy-done.2, s32[3]{0:T(128)} %copy-done.1, bf16[32,112,256]{2,1,0:T(8,128)(2,1)} %copy-done.3, bf16[3,32,1024]{2,1,0:T(8,128)(2,1)} %fields.5, bf16[3,8,1280]{2,1,0:T(8,128)(2,1)} %copy-done.7, bf16[3,8,1280]{2,1,0:T(8,128)(2,1)} %copy-done.6, ...), custom_call_target="tpu_custom_call", output_to_operand_aliasing={{}: (8, {})} | custom-call | tf_op jit(solution)/shard_map/edges/pallas_call | solution.py:826
  (4 shorter events, 0.0 us)
Async XLA Ops:
  0.1 0.9 copy-start
  1.0 39.9 %copy-start.1 = (s32[3]{0:T(128)}, s32[3]{0:T(128)S(1)}, u32[]{:S(2)}) copy-start(s32[3]{0:T(128)S(1)} %pad_add_fusion.pos) | copy-start | bytes 40
  3.1 33.8 %all-to-all-start = ((bf16[16,48,256]{2,1,0:T(8,128)(2,1)}), bf16[16,48,256]{2,1,0:T(8,128)(2,1)S(1)}, u32[]{:S(2)}, u32[]{:S(2)}) async-start(bf16[16,48,256]{2,1,0:T(8,128)(2,1)} %get-tuple-element.13), calls=%async_computation | async-start | bytes 786432 | tf_op jit(solution)/shard_map/all_to_all | solution.py:880
  19.6 9.9 %collective-permute-start.1 = (bf16[3,32,128]{2,1,0:T(8,128)(2,1)S(1)}, bf16[3,32,128]{2,1,0:T(8,128)(2,1)S(1)}, u32[]{:S(2)}, u32[]{:S(2)}) collective-permute-start(bf16[3,32,128]{2,1,0:T(8,128)(2,1)S(1)} %get-tuple-element.24), channel_id=1, source_target_pairs={{0,1},{1,2},{2,3},{3,4},{4,5},{5,6},{6,7},{8,9},{9,10},{10,11},{11... | collective-permute-start | bytes 73736 | tf_op jit(solution)/shard_map/ppermute | solution.py:883
  22.7 7.7 %collective-permute-start.2 = (bf16[3,32,128]{2,1,0:T(8,128)(2,1)S(1)}, bf16[3,32,128]{2,1,0:T(8,128)(2,1)S(1)}, u32[]{:S(2)}, u32[]{:S(2)}) collective-permute-start(bf16[3,32,128]{2,1,0:T(8,128)(2,1)S(1)} %get-tuple-element.23), channel_id=1, source_target_pairs={{1,0},{2,1},{3,2},{4,3},{5,4},{6,5},{7,6},{9,8},{10,9},{11,10},{12... | collective-permute-start | bytes 73736 | tf_op jit(solution)/shard_map/ppermute | solution.py:884
  24.0 11.8 %collective-permute-start = (bf16[64,256]{1,0:T(8,128)(2,1)S(1)}, bf16[64,256]{1,0:T(8,128)(2,1)S(1)}, u32[]{:S(2)}, u32[]{:S(2)}) collective-permute-start(bf16[64,256]{1,0:T(8,128)(2,1)S(1)} %get-tuple-element.14.own), channel_id=1, source_target_pairs={{0,120},{120,0},{1,121},{121,1},{2,122},{122,2},{3,123},{123,3},{4... | collective-permute-start | bytes 98312 | tf_op jit(solution)/shard_map/ppermute | solution.py:881
  29.5 11.5 %copy-start.2 = (s32[144]{0:T(256)}, s32[144]{0:T(256)S(1)}, u32[]{:S(2)}) copy-start(s32[144]{0:T(256)S(1)} %reshape.41.nb) | copy-start | bytes 1732
  29.5 11.5 %copy-start.4 = (bf16[3,32,128]{2,1,0:T(8,128)(2,1)}, bf16[3,32,128]{2,1,0:T(8,128)(2,1)S(1)}, u32[]{:S(2)}) copy-start(bf16[3,32,128]{2,1,0:T(8,128)(2,1)S(1)} %collective-permute-done.1.before) | copy-start | bytes 73732
  30.5 10.5 %copy-start.5 = (bf16[3,32,128]{2,1,0:T(8,128)(2,1)}, bf16[3,32,128]{2,1,0:T(8,128)(2,1)S(1)}, u32[]{:S(2)}) copy-start(bf16[3,32,128]{2,1,0:T(8,128)(2,1)S(1)} %collective-permute-done.2.after) | copy-start | bytes 73732
  30.5 10.5 %collective-permute-start.4 = (bf16[3,8,1280]{2,1,0:T(8,128)(2,1)S(1)}, bf16[3,8,1280]{2,1,0:T(8,128)(2,1)S(1)}, u32[]{:S(2)}, u32[]{:S(2)}) collective-permute-start(bf16[3,8,1280]{2,1,0:T(8,128)(2,1)S(1)} %get-tuple-element.21), channel_id=1, source_target_pairs={{8,0},{16,8},{24,16},{32,24},{40,32},{48,40},{56,48},{64,56},{72,6... | collective-permute-start | bytes 184328 | tf_op jit(solution)/shard_map/ppermute | solution.py:887
  31.8 9.2 %collective-permute-start.3 = (bf16[3,8,1280]{2,1,0:T(8,128)(2,1)S(1)}, bf16[3,8,1280]{2,1,0:T(8,128)(2,1)S(1)}, u32[]{:S(2)}, u32[]{:S(2)}) collective-permute-start(bf16[3,8,1280]{2,1,0:T(8,128)(2,1)S(1)} %get-tuple-element.22), channel_id=1, source_target_pairs={{0,8},{8,16},{16,24},{24,32},{32,40},{40,48},{48,56},{56,64},{64,7... | collective-permute-start | bytes 184328 | tf_op jit(solution)/shard_map/ppermute | solution.py:886
  41.0 14.9 %copy-start.9 = (f32[3,3,128]{2,1,0:T(4,128)S(1)}, f32[3,3,128]{2,1,0:T(4,128)}, u32[]{:S(2)}) copy-start(f32[3,3,128]{2,1,0:T(4,128)} %param.19) | copy-start | bytes 13828
  41.0 15.5 %copy-start.8 = (f32[3,3,256]{2,1,0:T(4,128)S(1)}, f32[3,3,256]{2,1,0:T(4,128)}, u32[]{:S(2)}) copy-start(f32[3,3,256]{2,1,0:T(4,128)} %param.26) | copy-start | bytes 27652
  41.0 16.1 %copy-start.10 = (bf16[16,128]{1,0:T(8,128)(2,1)S(1)}, bf16[16,128]{1,0:T(8,128)(2,1)}, u32[]{:S(2)}) copy-start(bf16[16,128]{1,0:T(8,128)(2,1)} %param.18) | copy-start | bytes 12292
  41.0 15.5 %copy-start.6 = (bf16[3,8,1280]{2,1,0:T(8,128)(2,1)}, bf16[3,8,1280]{2,1,0:T(8,128)(2,1)S(1)}, u32[]{:S(2)}) copy-start(bf16[3,8,1280]{2,1,0:T(8,128)(2,1)S(1)} %collective-permute-done.4.below) | copy-start | bytes 184324
  41.0 15.4 %copy-start.7 = (bf16[3,8,1280]{2,1,0:T(8,128)(2,1)}, bf16[3,8,1280]{2,1,0:T(8,128)(2,1)S(1)}, u32[]{:S(2)}) copy-start(bf16[3,8,1280]{2,1,0:T(8,128)(2,1)S(1)} %collective-permute-done.3.above) | copy-start | bytes 184324
  41.0 39.4 %all-to-all-start.1 = ((bf16[32,112,256]{2,1,0:T(8,128)(2,1)}), bf16[32,112,256]{2,1,0:T(8,128)(2,1)S(1)}, u32[]{:S(2)}, u32[]{:S(2)}) async-start(bf16[32,112,256]{2,1,0:T(8,128)(2,1)} %route.1), calls=%async_computation.1 | async-start | bytes 3670016 | tf_op jit(solution)/shard_map/all_to_all | solution.py:891
  80.5 1.3 %copy-start.3 = (bf16[32,112,256]{2,1,0:T(8,128)(2,1)}, bf16[32,112,256]{2,1,0:T(8,128)(2,1)S(1)}, u32[]{:S(2)}) copy-start(bf16[32,112,256]{2,1,0:T(8,128)(2,1)S(1)} %all-to-all-done.1.bands) | copy-start | bytes 5505028
